TPU v7x, 32 devices: a whole 2x2x4 slice. The times are simulated.
32 devices in a mesh: narrow: 4 (over x, core), wide: 8 (over z, y).
Axes of the slice: x: 2, y: 2, z: 4, core: 2. Of those that a mesh axis runs over, the one named last changes fastest.
Arguments:
- vectors: float32 [512, 6144], P('wide', 'narrow'), may hold values from -63 to 63
- blocks: float32 [48, 5, 128, 128], P('narrow'), may hold values from -0.125 to 0.125
- columns: int32 [48, 5], P('narrow'), may hold values from 0 to 47, as said below
- lower_bound: float32 [1], replicated, may hold values from -0.8 to -0.2
- upper_bound: float32 [1], replicated, may hold values from 2.2 to 2.8
Outputs:
- basis: float32 [512, 6144], P(None, ('narrow', 'wide'))
Inputs may be any that keep to these rules, and one draw needn't show every extreme that they name: `columns`: row r holds 5 different block-rows, each within 3 of r along the closed loop of 48 block-rows (indices taken modulo 48); r - 1 and r + 1 appear in every row, r - 3 in every even row and r + 3 in every odd row.
All inputs are finite; a program needn't handle non-finite values.
Results may differ from a plain program's by a relative error of at most 0.0001.
Values sent between devices are 32-bit elements; how exact they have to be, the bound alone decides.
No kernel may reach another device: no remote copies, remote signals or barrier semaphores. Data moves between devices by JAX's collectives and lax.ppermute only.
A program may use at most 64 MiB of HBM per device.

v0:
```python
import functools

import jax
import jax.numpy as jnp
from jax import lax
from jax.experimental import pallas as pl
from jax.experimental.pallas import tpu as pltpu
from jax.sharding import PartitionSpec as P

REACH = 3
STEPS = 8
TILE = 128
VM = pl.BlockSpec(memory_space=pltpu.VMEM)
SM = pl.BlockSpec(memory_space=pltpu.SMEM)
NT = (((1,), (1,)), ((), ()))
NN = (((1,), (0,)), ((), ()))
F32 = jnp.float32
BF16 = jnp.bfloat16


def params():
    return pltpu.CompilerParams(vmem_limit_bytes=40 * 1024 * 1024)


def split(x):
    hi = x.astype(BF16)
    return hi, (x - hi.astype(F32)).astype(BF16)


def dot(a, b, dims):
    return lax.dot_general(a, b, dims, preferred_element_type=F32)


def dot_split(a_hi, a_both, b_hi, b_lo, dims):
    rows = a_hi.shape[0]
    upper = dot(a_both, b_hi, dims)
    return upper[:rows] + (upper[rows:] + dot(a_hi, b_lo, dims))


def setup_kernel(total_blocks, columns_ref, lower_ref, upper_ref, blocks_ref, hi_ref, lo_ref):
    rows, slots, size, _ = blocks_ref.shape
    first = lax.axis_index("narrow") * rows
    half_width = (jnp.full((1, size), upper_ref[0], F32) - jnp.full((1, size), lower_ref[0], F32)) * 0.5
    scale = 2.0 / half_width
    hi_ref[...] = jnp.zeros_like(hi_ref)
    lo_ref[...] = jnp.zeros_like(lo_ref)
    for row in range(rows):
        pair, half = divmod(row, 2)
        here = slice(half * size, half * size + size)
        for slot in range(slots):
            place = lax.rem(columns_ref[row, slot] - first + REACH + total_blocks, total_blocks) - 2 * pair
            hi, lo = split(blocks_ref[row, slot] * scale)
            there = pl.ds(pl.multiple_of(place * size, size), size)
            hi_ref[pair, here, there] = hi
            lo_ref[pair, here, there] = lo


def setup(columns, lower_bound, upper_bound, blocks, total_blocks):
    rows, _, size, _ = blocks.shape
    shape = jax.ShapeDtypeStruct((rows // 2, 2 * size, (2 * REACH + 2) * size), BF16)
    return pl.pallas_call(
        functools.partial(setup_kernel, total_blocks),
        in_specs=[SM, SM, SM, VM],
        out_specs=[VM, VM],
        out_shape=[shape, shape],
        compiler_params=params(),
        name="setup",
    )(columns, lower_bound, upper_bound, blocks)


def diagonal(lower_ref, upper_ref, width):
    upper = jnp.full((1, width), upper_ref[0], F32)
    lower = jnp.full((1, width), lower_ref[0], F32)
    return 2.0 * (1.0 - (upper + lower) * 0.5) / ((upper - lower) * 0.5)


def odd_device():
    return lax.rem(lax.axis_index("narrow"), 2) == 1


def local_kernel(first_step, lower_ref, upper_ref, *refs):
    if first_step:
        mid_ref, hi_ref, lo_ref, out_ref = refs
        current = mid_ref[...]
    else:
        mid_ref, far_ref, near_ref, previous_ref, hi_ref, lo_ref, out_ref, full_ref = refs
        edge = far_ref.shape[1]
        odd = odd_device()
        left = jnp.where(odd, near_ref[...], far_ref[...])
        right = jnp.where(odd, far_ref[...], near_ref[...])
        current = jnp.concatenate([left, mid_ref[:, edge:-edge], right], axis=1)
        full_ref[...] = current
    pairs, width, window = hi_ref.shape
    size = width // 2
    diag = diagonal(lower_ref, upper_ref, width)
    hi, lo = split(current)
    both = jnp.concatenate([hi, lo], axis=0)
    for pair in range(pairs):
        start = 2 * pair - REACH
        begin, end = max(start, 0), min(start + window // size, 2 * pairs)
        there = slice(begin * size, end * size)
        inside = slice((begin - start) * size, (end - start) * size)
        here = slice(pair * width, pair * width + width)
        total = dot_split(hi[:, there], both[:, there], hi_ref[pair, :, inside], lo_ref[pair, :, inside], NT)
        total = total + diag * current[:, here]
        out_ref[:, here] = total * 0.5 if first_step else total - previous_ref[:, here]


def local_part(bounds, state, previous, operator):
    mid = state[0]
    shape = jax.ShapeDtypeStruct(mid.shape, F32)
    first_step = previous is None
    operands = (*bounds, *state, *(() if first_step else (previous,)), *operator)
    width = operator[0].shape[1]
    return pl.pallas_call(
        functools.partial(local_kernel, first_step),
        in_specs=[SM, SM] + [VM] * (len(operands) - 2),
        out_specs=VM if first_step else [VM, VM],
        out_shape=shape if first_step else [shape, shape],
        compiler_params=params(),
        cost_estimate=pl.CostEstimate(flops=24 * mid.size * width, bytes_accessed=8 * mid.size, transcendentals=0),
        name="local_part",
    )(*operands)


def halo_sums(first_step, mid_ref, far_ref, near_ref, hi_ref, lo_ref):
    pairs, width, window = hi_ref.shape
    size = width // 2
    edge = REACH * size
    odd = odd_device()
    left = jnp.where(odd, near_ref[...], far_ref[...])
    right = jnp.where(odd, far_ref[...], near_ref[...])
    factor = 0.5 if first_step else 1.0

    def reach_into(pair, halo, inside):
        hi, lo = split(halo)
        both = jnp.concatenate([hi, lo], axis=0)
        return factor * dot_split(hi, both, hi_ref[pair, :, inside], lo_ref[pair, :, inside], NT)

    outer = reach_into(0, left, slice(0, edge))
    inner = reach_into(1, left[:, -size:], slice(0, size))
    left_out = mid_ref[:, :edge] + jnp.concatenate([outer, inner[:, :size]], axis=1)
    outer = reach_into(pairs - 1, right, slice(window - edge, window))
    inner = reach_into(pairs - 2, right[:, :size], slice(window - size, window))
    right_out = mid_ref[:, -edge:] + jnp.concatenate([inner[:, size:], outer], axis=1)
    return left_out, right_out


def halo_kernel(first_step, mid_ref, far_ref, near_ref, hi_ref, lo_ref, far_out_ref, near_out_ref):
    left, right = halo_sums(first_step, mid_ref, far_ref, near_ref, hi_ref, lo_ref)
    odd = odd_device()
    far_out_ref[...] = jnp.where(odd, right, left)
    near_out_ref[...] = jnp.where(odd, left, right)


def halo_part(first_step, mid, far, near, operator):
    return pl.pallas_call(
        functools.partial(halo_kernel, first_step),
        in_specs=[VM] * 5,
        out_specs=[VM, VM],
        out_shape=[jax.ShapeDtypeStruct(far.shape, F32)] * 2,
        compiler_params=params(),
        cost_estimate=pl.CostEstimate(flops=24 * far.size * 512, bytes_accessed=8 * mid.size, transcendentals=0),
        name="halo_part",
    )(mid, far, near, *operator)


def last_kernel(mid_ref, far_ref, near_ref, hi_ref, lo_ref, out_ref):
    left, right = halo_sums(False, mid_ref, far_ref, near_ref, hi_ref, lo_ref)
    edge = left.shape[1]
    out_ref[...] = jnp.concatenate([left, mid_ref[:, edge:-edge], right], axis=1)


def last_part(mid, far, near, operator):
    return pl.pallas_call(
        last_kernel,
        in_specs=[VM] * 5,
        out_specs=VM,
        out_shape=jax.ShapeDtypeStruct(mid.shape, F32),
        compiler_params=params(),
        name="last_part",
    )(mid, far, near, *operator)


def exchange(far, near):
    size = lax.axis_size("narrow")
    far_pairs = [(i, (i + 1) % size if i % 2 else (i - 1) % size) for i in range(size)]
    near_pairs = [(i, i ^ 1) for i in range(size)]
    return lax.ppermute(far, "narrow", far_pairs), lax.ppermute(near, "narrow", near_pairs)


def filtered_rows(vectors, blocks, columns, lower_bound, upper_bound):
    total_blocks = blocks.shape[0] * lax.axis_size("narrow")
    edge = REACH * blocks.shape[2]
    bounds = (lower_bound, upper_bound)
    odd = odd_device()
    left, right = vectors[:, :edge], vectors[:, -edge:]
    far, near = jnp.where(odd, right, left), jnp.where(odd, left, right)
    operator = setup(columns, lower_bound, upper_bound, blocks, total_blocks)
    state, previous = (vectors,), None
    for step in range(STEPS):
        halo = exchange(far, near)
        if step == 0:
            mid, full = local_part(bounds, state, None, operator), vectors
        else:
            mid, full = local_part(bounds, state, previous, operator)
        previous = full
        if step == STEPS - 1:
            return last_part(mid, *halo, operator)
        far, near = halo_part(step == 0, mid, *halo, operator)
        state = (mid, far, near)


def pair_perm(mask):
    narrow, wide = lax.axis_size("narrow"), lax.axis_size("wide")
    return [(n * wide + w, (n ^ mask[0]) * wide + (w ^ mask[1])) for n in range(narrow) for w in range(wide)]


def swap(x, mask):
    return lax.ppermute(x, ("narrow", "wide"), pair_perm(mask))


def bit_groups():
    narrow = [(1 << b, 0) for b in range(lax.axis_size("narrow").bit_length() - 1)]
    wide = [(0, 1 << b) for b in range(lax.axis_size("wide").bit_length() - 1)]
    rest = wide[1:] + narrow[2:]
    return [narrow[:1], narrow[1:2] + wide[:1]] + [rest[i : i + 2] for i in range(0, len(rest), 2)]


def masks(bits):
    out = []
    for d in range(1 << len(bits)):
        chosen = [b for k, b in enumerate(bits) if d >> k & 1]
        out.append((sum(b[0] for b in chosen), sum(b[1] for b in chosen)))
    return out


def place_in(bits):
    n, w = lax.axis_index("narrow"), lax.axis_index("wide")
    place = 0
    for k, b in enumerate(bits):
        bit = (n // b[0]) % 2 if b[0] else (w // b[1]) % 2
        place = place + (bit << k)
    return place


def all_sum(x):
    groups = bit_groups()
    for bits in groups[:-1]:
        place, members = place_in(bits), masks(bits)
        parts = x.reshape(len(members), -1, x.shape[-1])
        own = lax.dynamic_index_in_dim(parts, place, 0, keepdims=False)
        for d in range(1, len(members)):
            sent = lax.dynamic_index_in_dim(parts, place ^ d, 0, keepdims=False)
            own = own + swap(sent, members[d])
        x = own
    members = masks(groups[-1])
    x = x + sum(swap(x, members[d]) for d in range(1, len(members)))
    for bits in groups[:-1][::-1]:
        place, members = place_in(bits), masks(bits)
        parts = jnp.stack([x] + [swap(x, members[d]) for d in range(1, len(members))])
        x = jnp.concatenate([lax.dynamic_index_in_dim(parts, place ^ a, 0, keepdims=False) for a in range(len(members))])
    return x


def tile_pairs(count):
    return [(i, j) for i in range(count) for j in range(i, count)]


def gram_kernel(rows_ref, out_ref):
    count = rows_ref.shape[0] // TILE
    hi, lo = split(rows_ref[...])
    at = 0
    for i in range(count):
        here, there = slice(i * TILE, (i + 1) * TILE), slice(i * TILE, None)
        both = jnp.concatenate([hi[here], lo[here]], axis=0)
        strip = dot_split(hi[here], both, hi[there], lo[there], NT)
        for j in range(i, count):
            out_ref[at * TILE : (at + 1) * TILE, :] = strip[:, (j - i) * TILE : (j - i + 1) * TILE]
            at += 1


def gram(rows):
    count = rows.shape[0] // TILE
    return pl.pallas_call(
        gram_kernel,
        in_specs=[VM],
        out_specs=VM,
        out_shape=jax.ShapeDtypeStruct((len(tile_pairs(count)) * TILE, TILE), F32),
        compiler_params=params(),
        name="gram",
    )(rows)


def rotate_kernel(total_rows, gram_ref, rows_ref, out_ref):
    count = rows_ref.shape[0] // TILE
    order = tile_pairs(count)
    squares = jnp.zeros((TILE, TILE), F32)
    for at, (i, j) in enumerate(order):
        tile = gram_ref[at * TILE : (at + 1) * TILE, :]
        squares = squares + tile * tile * (1.0 if i == j else 2.0)
    frob = jnp.sqrt(jnp.sum(squares, axis=(0, 1), keepdims=True) + 1e-06)
    half = 0.5 / frob
    gain = jnp.sqrt(total_rows / frob)
    rows = rows_ref[...]
    rows_hi, rows_lo = split(rows)
    for i in range(count):
        pieces = []
        for j in range(count):
            at = order.index((min(i, j), max(i, j)))
            tile = gram_ref[at * TILE : (at + 1) * TILE, :]
            pieces.append(tile if i <= j else tile.T)
        strip = jnp.concatenate(pieces, axis=1) * half
        hi, lo = split(strip)
        both = jnp.concatenate([hi, lo], axis=0)
        here = slice(i * TILE, (i + 1) * TILE)
        out_ref[here, :] = gain * (1.5 * rows[here] - dot_split(hi, both, rows_hi, rows_lo, NN))


def rotate(gram_sum, rows, total_rows):
    return pl.pallas_call(
        functools.partial(rotate_kernel, float(total_rows)),
        in_specs=[VM, VM],
        out_specs=VM,
        out_shape=jax.ShapeDtypeStruct(rows.shape, F32),
        compiler_params=params(),
        name="rotate",
    )(gram_sum, rows)


def regroup(rows):
    count, length = rows.shape
    size = lax.axis_size("wide")
    own = length // size
    parts = rows.reshape(count, size, own).transpose(1, 0, 2).reshape(size, count * own // TILE, TILE)
    parts = lax.all_to_all(parts, "wide", split_axis=0, concat_axis=0, tiled=True)
    return parts.reshape(size * count, own)


def on_device(vectors, blocks, columns, lower_bound, upper_bound):
    total_rows = vectors.shape[1] * lax.axis_size("narrow")
    rows = regroup(filtered_rows(vectors, blocks, columns, lower_bound, upper_bound))
    return rotate(all_sum(gram(rows)), rows, total_rows)


def solution(mesh):
    return jax.shard_map(
        on_device,
        mesh=mesh,
        in_specs=(P("wide", "narrow"), P("narrow", None, None, None), P("narrow", None), P(), P()),
        out_specs=P(None, ("narrow", "wide")),
        check_vma=False,
    )
```

profile of v0, /device:TPU:0, one launch (start us, length us, event | category | flops | bytes accessed | tf_op | source)
XLA Modules:
  0.0 99.1 jit_solution(10283707352552443629)
XLA Ops:
  0.0 1.0 %slice_select_fusion = (f32[64,384]{1,0:T(8,128)S(1)}, f32[64,384]{1,0:T(8,128)S(1)}) fusion(f32[64,1536]{1,0:T(8,128)} %refs_3_.1, pred[]{:T(512)S(6)} %eq.10), kind=kLoop, calls=%fused_computation.13 | loop fusion | flops 49152 | bytes 393217 | tf_op jit(solution)/shard_map/jit(_where)/select_n | solution.py:198
  1.0 2.4 %collective-permute-start = (f32[64,384]{1,0:T(8,128)S(1)}, f32[64,384]{1,0:T(8,128)S(1)}, u32[]{:S(2)}, u32[]{:S(2)}) collective-permute-start(f32[64,384]{1,0:T(8,128)S(1)} %get-tuple-element.66), channel_id=1, source_target_pairs={{0,24},{8,16},{16,8},{24,0},{1,25},{9,17},{17,9},{25,1},{2,26},{10... | collective-permute-start | bytes 294920 | tf_op jit(solution)/shard_map/ppermute | solution.py:189
  3.5 0.7 collective-permute-start.1
  5.4 0.8 copy.9.columns_ref
  6.2 2.1 %copy-done = f32[12,5,128,128]{3,2,1,0:T(8,128)S(1)} copy-done((f32[12,5,128,128]{3,2,1,0:T(8,128)S(1)}, f32[12,5,128,128]{3,2,1,0:T(8,128)}, u32[]{:S(2)}) %copy-start) | copy-done | bytes 3932184
  8.3 2.2 %setup.1 = (bf16[6,256,1024]{2,1,0:T(8,128)(2,1)S(1)}, bf16[6,256,1024]{2,1,0:T(8,128)(2,1)S(1)}) custom-call(s32[12,5]{1,0:T(8,128)S(1)} %copy.9.columns_ref, f32[1]{0:T(128)S(6)} %copy.12.lower_ref, f32[1]{0:T(128)S(6)} %copy.13.upper_ref, f32[12,5,128,128]{3,2,1,0:T(8,128)S(1)} %copy-done), custom_call_target="tpu_custom_call" | custom-call | tf_op jit(solution)/shard_map/setup/pallas_call | solution.py:61
  10.6 1.7 %local_part.8.mid_ref.refs_0_ = f32[64,1536]{1,0:T(8,128)S(1)} custom-call(f32[1]{0:T(128)S(6)} %copy.12.lower_ref, f32[1]{0:T(128)S(6)} %copy.13.upper_ref, f32[64,1536]{1,0:T(8,128)S(1)} %copy-done.1, bf16[6,256,1024]{2,1,0:T(8,128)(2,1)S(1)} %get-tuple-element.34.refs_1_.hi_ref.refs_4_, bf16[6,256,1024]{2,1,0:T(8,128)(2,1)S(1)} %get-tuple-element.35.refs_2_.lo_ref.refs_5_), custom_call_target="tpu_custom_call" | custom-call | flops 603979776 | bytes 786432 | tf_op jit(solution)/shard_map/local_part/pallas_call | solution.py:115
  12.9 1.7 %local_part.9 = (f32[64,1536]{1,0:T(8,128)S(1)}, f32[64,1536]{1,0:T(8,128)S(1)}) custom-call(f32[1]{0:T(128)S(6)} %copy.12.lower_ref, f32[1]{0:T(128)S(6)} %copy.13.upper_ref, f32[64,1536]{1,0:T(8,128)S(1)} %local_part.8.mid_ref.refs_0_, f32[64,384]{1,0:T(8,128)S(1)} %get-tuple-element.36.refs_1_, f32[64,384]{1,0:T(8,128)S(1)} %get-tuple-element.37.refs_2_, ...), custom_call_target="tpu_custom_call" | custom-call | flops 603979776 | bytes 786432 | tf_op jit(solution)/shard_map/local_part/pallas_call | solution.py:115
  14.6 3.1 %collective-permute-done.2.far_ref = f32[64,384]{1,0:T(8,128)S(1)} collective-permute-done((f32[64,384]{1,0:T(8,128)S(1)}, f32[64,384]{1,0:T(8,128)S(1)}, u32[]{:S(2)}, u32[]{:S(2)}) %collective-permute-start.2) | collective-permute-done | bytes 98336 | tf_op jit(solution)/shard_map/ppermute | solution.py:189
  18.4 1.7 %local_part.10 = (f32[64,1536]{1,0:T(8,128)S(1)}, f32[64,1536]{1,0:T(8,128)S(1)}) custom-call(f32[1]{0:T(128)S(6)} %copy.12.lower_ref, f32[1]{0:T(128)S(6)} %copy.13.upper_ref, f32[64,1536]{1,0:T(8,128)S(1)} %get-tuple-element.38.mid_ref.refs_0_, f32[64,384]{1,0:T(8,128)S(1)} %get-tuple-element.39.refs_1_, f32[64,384]{1,0:T(8,128)S(1)} %get-tuple-element.40.refs_2_, ...), custom_call_target="tpu_custom_call" | custom-call | flops 603979776 | bytes 786432 | tf_op jit(solution)/shard_map/local_part/pallas_call | solution.py:115
  20.1 2.9 %collective-permute-done.4.far_ref = f32[64,384]{1,0:T(8,128)S(1)} collective-permute-done((f32[64,384]{1,0:T(8,128)S(1)}, f32[64,384]{1,0:T(8,128)S(1)}, u32[]{:S(2)}, u32[]{:S(2)}) %collective-permute-start.4) | collective-permute-done | bytes 98336 | tf_op jit(solution)/shard_map/ppermute | solution.py:189
  23.7 1.7 %local_part.11 = (f32[64,1536]{1,0:T(8,128)S(1)}, f32[64,1536]{1,0:T(8,128)S(1)}) custom-call(f32[1]{0:T(128)S(6)} %copy.12.lower_ref, f32[1]{0:T(128)S(6)} %copy.13.upper_ref, f32[64,1536]{1,0:T(8,128)S(1)} %get-tuple-element.42.mid_ref.refs_0_, f32[64,384]{1,0:T(8,128)S(1)} %get-tuple-element.43.refs_1_, f32[64,384]{1,0:T(8,128)S(1)} %get-tuple-element.44.refs_2_, ...), custom_call_target="tpu_custom_call" | custom-call | flops 603979776 | bytes 786432 | tf_op jit(solution)/shard_map/local_part/pallas_call | solution.py:115
  25.4 2.9 %collective-permute-done.6.far_ref = f32[64,384]{1,0:T(8,128)S(1)} collective-permute-done((f32[64,384]{1,0:T(8,128)S(1)}, f32[64,384]{1,0:T(8,128)S(1)}, u32[]{:S(2)}, u32[]{:S(2)}) %collective-permute-start.6) | collective-permute-done | bytes 98336 | tf_op jit(solution)/shard_map/ppermute | solution.py:189
  28.3 0.4 halo_part.10
  29.0 1.7 %local_part.12 = (f32[64,1536]{1,0:T(8,128)S(1)}, f32[64,1536]{1,0:T(8,128)S(1)}) custom-call(f32[1]{0:T(128)S(6)} %copy.12.lower_ref, f32[1]{0:T(128)S(6)} %copy.13.upper_ref, f32[64,1536]{1,0:T(8,128)S(1)} %get-tuple-element.46.mid_ref.refs_0_, f32[64,384]{1,0:T(8,128)S(1)} %get-tuple-element.47.refs_1_, f32[64,384]{1,0:T(8,128)S(1)} %get-tuple-element.48.refs_2_, ...), custom_call_target="tpu_custom_call" | custom-call | flops 603979776 | bytes 786432 | tf_op jit(solution)/shard_map/local_part/pallas_call | solution.py:115
  30.7 2.9 %collective-permute-done.8.far_ref = f32[64,384]{1,0:T(8,128)S(1)} collective-permute-done((f32[64,384]{1,0:T(8,128)S(1)}, f32[64,384]{1,0:T(8,128)S(1)}, u32[]{:S(2)}, u32[]{:S(2)}) %collective-permute-start.8) | collective-permute-done | bytes 98336 | tf_op jit(solution)/shard_map/ppermute | solution.py:189
  33.6 0.4 halo_part.11
  34.3 1.7 %local_part.13 = (f32[64,1536]{1,0:T(8,128)S(1)}, f32[64,1536]{1,0:T(8,128)S(1)}) custom-call(f32[1]{0:T(128)S(6)} %copy.12.lower_ref, f32[1]{0:T(128)S(6)} %copy.13.upper_ref, f32[64,1536]{1,0:T(8,128)S(1)} %get-tuple-element.50.mid_ref.refs_0_, f32[64,384]{1,0:T(8,128)S(1)} %get-tuple-element.51.refs_1_, f32[64,384]{1,0:T(8,128)S(1)} %get-tuple-element.52.refs_2_, ...), custom_call_target="tpu_custom_call" | custom-call | flops 603979776 | bytes 786432 | tf_op jit(solution)/shard_map/local_part/pallas_call | solution.py:115
  36.1 2.9 %collective-permute-done.10.far_ref = f32[64,384]{1,0:T(8,128)S(1)} collective-permute-done((f32[64,384]{1,0:T(8,128)S(1)}, f32[64,384]{1,0:T(8,128)S(1)}, u32[]{:S(2)}, u32[]{:S(2)}) %collective-permute-start.10) | collective-permute-done | bytes 98336 | tf_op jit(solution)/shard_map/ppermute | solution.py:189
  38.9 0.4 halo_part.12
  39.7 1.7 %local_part.14 = (f32[64,1536]{1,0:T(8,128)S(1)}, f32[64,1536]{1,0:T(8,128)S(1)}) custom-call(f32[1]{0:T(128)S(6)} %copy.12.lower_ref, f32[1]{0:T(128)S(6)} %copy.13.upper_ref, f32[64,1536]{1,0:T(8,128)S(1)} %get-tuple-element.54.mid_ref.refs_0_, f32[64,384]{1,0:T(8,128)S(1)} %get-tuple-element.55.refs_1_, f32[64,384]{1,0:T(8,128)S(1)} %get-tuple-element.56.refs_2_, ...), custom_call_target="tpu_custom_call" | custom-call | flops 603979776 | bytes 786432 | tf_op jit(solution)/shard_map/local_part/pallas_call | solution.py:115
  41.4 2.9 %collective-permute-done.12.far_ref = f32[64,384]{1,0:T(8,128)S(1)} collective-permute-done((f32[64,384]{1,0:T(8,128)S(1)}, f32[64,384]{1,0:T(8,128)S(1)}, u32[]{:S(2)}, u32[]{:S(2)}) %collective-permute-start.12) | collective-permute-done | bytes 98336 | tf_op jit(solution)/shard_map/ppermute | solution.py:189
  44.2 0.4 halo_part.13
  45.0 2.5 %local_part.15 = (f32[64,1536]{1,0:T(8,128)S(1)}, f32[64,1536]{1,0:T(8,128)}) custom-call(f32[1]{0:T(128)S(6)} %copy.12.lower_ref, f32[1]{0:T(128)S(6)} %copy.13.upper_ref, f32[64,1536]{1,0:T(8,128)S(1)} %get-tuple-element.58.mid_ref.refs_0_, f32[64,384]{1,0:T(8,128)S(1)} %get-tuple-element.59.refs_1_, f32[64,384]{1,0:T(8,128)S(1)} %get-tuple-element.60.refs_2_, ...), custom_call_target="tpu_custom_call" | custom-call | flops 603979776 | bytes 786432 | tf_op jit(solution)/shard_map/local_part/pallas_call | solution.py:115
  47.4 2.1 %collective-permute-done.14.far_ref = f32[64,384]{1,0:T(8,128)S(1)} collective-permute-done((f32[64,384]{1,0:T(8,128)S(1)}, f32[64,384]{1,0:T(8,128)S(1)}, u32[]{:S(2)}, u32[]{:S(2)}) %collective-permute-start.14) | collective-permute-done | bytes 98336 | tf_op jit(solution)/shard_map/ppermute | solution.py:189
  50.3 1.0 %reshape.16 = f32[8,96,128]{2,1,0:T(8,128)} reshape(f32[8,64,192]{2,1,0:T(8,128)S(1)} %copy.10) | data formatting | bytes 786432 | tf_op jit(solution)/shard_map/reshape | solution.py:335
  51.3 5.9 %all-to-all-start = ((f32[8,96,128]{2,1,0:T(8,128)}), f32[8,96,128]{2,1,0:T(8,128)S(1)}, u32[]{:S(2)}, u32[]{:S(2)}) async-start(f32[8,96,128]{2,1,0:T(8,128)} %reshape.16), calls=%async_computation | async-start | bytes 786432 | tf_op jit(solution)/shard_map/all_to_all | solution.py:336
  57.2 12.0 %all-to-all-done = f32[8,96,128]{2,1,0:T(8,128)S(1)} async-done(((f32[8,96,128]{2,1,0:T(8,128)}), f32[8,96,128]{2,1,0:T(8,128)S(1)}, u32[]{:S(2)}, u32[]{:S(2)}) %all-to-all-start) | async-done | bytes 393248 | tf_op jit(solution)/shard_map/all_to_all | solution.py:336
  69.3 0.5 gram.1
  70.0 1.6 %collective-permute-done.16 = f32[640,128]{1,0:T(8,128)S(1)} collective-permute-done((f32[640,128]{1,0:T(8,128)S(1)}, f32[640,128]{1,0:T(8,128)S(1)}, u32[]{:S(2)}, u32[]{:S(2)}) %collective-permute-start.16) | collective-permute-done | bytes 327712 | tf_op jit(solution)/shard_map/ppermute | solution.py:220
  71.7 0.6 collective-permute-start.17
  72.3 1.5 %collective-permute-start.18 = (f32[160,128]{1,0:T(8,128)S(1)}, f32[160,128]{1,0:T(8,128)S(1)}, u32[]{:S(2)}, u32[]{:S(2)}) collective-permute-start(f32[160,128]{1,0:T(8,128)S(1)} %get-tuple-element.75), channel_id=1, source_target_pairs={{0,1},{1,0},{2,3},{3,2},{4,5},{5,4},{6,7},{7,6},{8,9},{9,8},{10,11... | collective-permute-start | bytes 245768 | tf_op jit(solution)/shard_map/ppermute | solution.py:220
  73.8 1.5 %collective-permute-start.19 = (f32[160,128]{1,0:T(8,128)S(1)}, f32[160,128]{1,0:T(8,128)S(1)}, u32[]{:S(2)}, u32[]{:S(2)}) collective-permute-start(f32[160,128]{1,0:T(8,128)S(1)} %get-tuple-element.74), channel_id=1, source_target_pairs={{0,17},{1,16},{2,19},{3,18},{4,21},{5,20},{6,23},{7,22},{8,25},{9,... | collective-permute-start | bytes 245768 | tf_op jit(solution)/shard_map/ppermute | solution.py:220
  75.2 1.3 %collective-permute-done.17 = f32[160,128]{1,0:T(8,128)S(1)} collective-permute-done((f32[160,128]{1,0:T(8,128)S(1)}, f32[160,128]{1,0:T(8,128)S(1)}, u32[]{:S(2)}, u32[]{:S(2)}) %collective-permute-start.17) | collective-permute-done | bytes 81952 | tf_op jit(solution)/shard_map/ppermute | solution.py:220
  76.6 0.9 collective-permute-done.18
  77.5 1.6 %collective-permute-done.19 = f32[160,128]{1,0:T(8,128)S(1)} collective-permute-done((f32[160,128]{1,0:T(8,128)S(1)}, f32[160,128]{1,0:T(8,128)S(1)}, u32[]{:S(2)}, u32[]{:S(2)}) %collective-permute-start.19) | collective-permute-done | bytes 81952 | tf_op jit(solution)/shard_map/ppermute | solution.py:220
  79.3 1.9 %collective-permute-start.21 = (f32[160,128]{1,0:T(8,128)S(1)}, f32[160,128]{1,0:T(8,128)S(1)}, u32[]{:S(2)}, u32[]{:S(2)}) collective-permute-start(f32[160,128]{1,0:T(8,128)S(1)} %fusion.5), channel_id=1, source_target_pairs={{0,4},{1,5},{2,6},{3,7},{4,0},{5,1},{6,2},{7,3},{8,12},{9,13},{10,... | collective-permute-start | bytes 245768 | tf_op jit(solution)/shard_map/ppermute | solution.py:220
  81.2 2.4 %collective-permute-start.22 = (f32[160,128]{1,0:T(8,128)S(1)}, f32[160,128]{1,0:T(8,128)S(1)}, u32[]{:S(2)}, u32[]{:S(2)}) collective-permute-start(f32[160,128]{1,0:T(8,128)S(1)} %fusion.5), channel_id=1, source_target_pairs={{0,6},{1,7},{2,4},{3,5},{4,2},{5,3},{6,0},{7,1},{8,14},{9,15},{10,... | collective-permute-start | bytes 245768 | tf_op jit(solution)/shard_map/ppermute | solution.py:220
  83.6 4.0 %collective-permute-done.21 = f32[160,128]{1,0:T(8,128)S(1)} collective-permute-done((f32[160,128]{1,0:T(8,128)S(1)}, f32[160,128]{1,0:T(8,128)S(1)}, u32[]{:S(2)}, u32[]{:S(2)}) %collective-permute-start.21) | collective-permute-done | bytes 81952 | tf_op jit(solution)/shard_map/ppermute | solution.py:220
  87.6 1.5 %collective-permute-start.23 = (f32[160,128]{1,0:T(8,128)S(1)}, f32[160,128]{1,0:T(8,128)S(1)}, u32[]{:S(2)}, u32[]{:S(2)}) collective-permute-start(f32[160,128]{1,0:T(8,128)S(1)} %add_add_fusion), channel_id=1, source_target_pairs={{0,16},{1,17},{2,18},{3,19},{4,20},{5,21},{6,22},{7,23},{8,24},{9,... | collective-permute-start | bytes 245768 | tf_op jit(solution)/shard_map/ppermute | solution.py:220
  89.1 0.9 collective-permute-start.24
  90.0 1.2 %collective-permute-start.25 = (f32[160,128]{1,0:T(8,128)S(1)}, f32[160,128]{1,0:T(8,128)S(1)}, u32[]{:S(2)}, u32[]{:S(2)}) collective-permute-start(f32[160,128]{1,0:T(8,128)S(1)} %add_add_fusion), channel_id=1, source_target_pairs={{0,17},{1,16},{2,19},{3,18},{4,21},{5,20},{6,23},{7,22},{8,25},{9,... | collective-permute-start | bytes 245768 | tf_op jit(solution)/shard_map/ppermute | solution.py:220
  91.2 1.0 collective-permute-done.23
  92.1 1.4 %collective-permute-done.24 = f32[160,128]{1,0:T(8,128)S(1)} collective-permute-done((f32[160,128]{1,0:T(8,128)S(1)}, f32[160,128]{1,0:T(8,128)S(1)}, u32[]{:S(2)}, u32[]{:S(2)}) %collective-permute-start.24) | collective-permute-done | bytes 81952 | tf_op jit(solution)/shard_map/ppermute | solution.py:220
  93.5 1.8 %collective-permute-done.25 = f32[160,128]{1,0:T(8,128)S(1)} collective-permute-done((f32[160,128]{1,0:T(8,128)S(1)}, f32[160,128]{1,0:T(8,128)S(1)}, u32[]{:S(2)}, u32[]{:S(2)}) %collective-permute-start.25) | collective-permute-done | bytes 81952 | tf_op jit(solution)/shard_map/ppermute | solution.py:220
  95.6 1.6 %collective-permute-done.26 = f32[640,128]{1,0:T(8,128)S(1)} collective-permute-done((f32[640,128]{1,0:T(8,128)S(1)}, f32[640,128]{1,0:T(8,128)S(1)}, u32[]{:S(2)}, u32[]{:S(2)}) %collective-permute-start.26) | collective-permute-done | bytes 327712 | tf_op jit(solution)/shard_map/ppermute | solution.py:220
  97.4 0.8 rotate.1
  98.1 0.9 copy.11
  (48 shorter events, 4.8 us)
Async XLA Ops:
  0.0 10.5 %copy-start.1 = (f32[64,1536]{1,0:T(8,128)S(1)}, f32[64,1536]{1,0:T(8,128)}, u32[]{:S(2)}) copy-start(f32[64,1536]{1,0:T(8,128)} %refs_3_.1) | copy-start | bytes 1179652
  1.0 11.2 %collective-permute-start = (f32[64,384]{1,0:T(8,128)S(1)}, f32[64,384]{1,0:T(8,128)S(1)}, u32[]{:S(2)}, u32[]{:S(2)}) collective-permute-start(f32[64,384]{1,0:T(8,128)S(1)} %get-tuple-element.66), channel_id=1, source_target_pairs={{0,24},{8,16},{16,8},{24,0},{1,25},{9,17},{17,9},{25,1},{2,26},{10... | collective-permute-start | bytes 294920 | tf_op jit(solution)/shard_map/ppermute | solution.py:189
  3.5 8.8 %collective-permute-start.1 = (f32[64,384]{1,0:T(8,128)S(1)}, f32[64,384]{1,0:T(8,128)S(1)}, u32[]{:S(2)}, u32[]{:S(2)}) collective-permute-start(f32[64,384]{1,0:T(8,128)S(1)} %get-tuple-element.65), channel_id=1, source_target_pairs={{0,8},{8,0},{16,24},{24,16},{1,9},{9,1},{17,25},{25,17},{2,10},{10... | collective-permute-start | bytes 294920 | tf_op jit(solution)/shard_map/ppermute | solution.py:189
  6.2 2.1 %copy-start = (f32[12,5,128,128]{3,2,1,0:T(8,128)S(1)}, f32[12,5,128,128]{3,2,1,0:T(8,128)}, u32[]{:S(2)}) copy-start(f32[12,5,128,128]{3,2,1,0:T(8,128)} %blocks_ref.1) | copy-start | bytes 11796484
  12.7 5.0 %collective-permute-start.2 = (f32[64,384]{1,0:T(8,128)S(1)}, f32[64,384]{1,0:T(8,128)S(1)}, u32[]{:S(2)}, u32[]{:S(2)}) collective-permute-start(f32[64,384]{1,0:T(8,128)S(1)} %get-tuple-element.36.refs_1_), channel_id=1, source_target_pairs={{0,24},{8,16},{16,8},{24,0},{1,25},{9,17},{17,9},{25,1},{2,26},{10... | collective-permute-start | bytes 294920 | tf_op jit(solution)/shard_map/ppermute | solution.py:189
  12.9 4.8 %collective-permute-start.3 = (f32[64,384]{1,0:T(8,128)S(1)}, f32[64,384]{1,0:T(8,128)S(1)}, u32[]{:S(2)}, u32[]{:S(2)}) collective-permute-start(f32[64,384]{1,0:T(8,128)S(1)} %get-tuple-element.37.refs_2_), channel_id=1, source_target_pairs={{0,8},{8,0},{16,24},{24,16},{1,9},{9,1},{17,25},{25,17},{2,10},{10... | collective-permute-start | bytes 294920 | tf_op jit(solution)/shard_map/ppermute | solution.py:189
  18.2 4.9 %collective-permute-start.4 = (f32[64,384]{1,0:T(8,128)S(1)}, f32[64,384]{1,0:T(8,128)S(1)}, u32[]{:S(2)}, u32[]{:S(2)}) collective-permute-start(f32[64,384]{1,0:T(8,128)S(1)} %get-tuple-element.39.refs_1_), channel_id=1, source_target_pairs={{0,24},{8,16},{16,8},{24,0},{1,25},{9,17},{17,9},{25,1},{2,26},{10... | collective-permute-start | bytes 294920 | tf_op jit(solution)/shard_map/ppermute | solution.py:189
  18.2 4.8 %collective-permute-start.5 = (f32[64,384]{1,0:T(8,128)S(1)}, f32[64,384]{1,0:T(8,128)S(1)}, u32[]{:S(2)}, u32[]{:S(2)}) collective-permute-start(f32[64,384]{1,0:T(8,128)S(1)} %get-tuple-element.40.refs_2_), channel_id=1, source_target_pairs={{0,8},{8,0},{16,24},{24,16},{1,9},{9,1},{17,25},{25,17},{2,10},{10... | collective-permute-start | bytes 294920 | tf_op jit(solution)/shard_map/ppermute | solution.py:189
  23.5 4.9 %collective-permute-start.6 = (f32[64,384]{1,0:T(8,128)S(1)}, f32[64,384]{1,0:T(8,128)S(1)}, u32[]{:S(2)}, u32[]{:S(2)}) collective-permute-start(f32[64,384]{1,0:T(8,128)S(1)} %get-tuple-element.43.refs_1_), channel_id=1, source_target_pairs={{0,24},{8,16},{16,8},{24,0},{1,25},{9,17},{17,9},{25,1},{2,26},{10... | collective-permute-start | bytes 294920 | tf_op jit(solution)/shard_map/ppermute | solution.py:189
  23.5 4.8 %collective-permute-start.7 = (f32[64,384]{1,0:T(8,128)S(1)}, f32[64,384]{1,0:T(8,128)S(1)}, u32[]{:S(2)}, u32[]{:S(2)}) collective-permute-start(f32[64,384]{1,0:T(8,128)S(1)} %get-tuple-element.44.refs_2_), channel_id=1, source_target_pairs={{0,8},{8,0},{16,24},{24,16},{1,9},{9,1},{17,25},{25,17},{2,10},{10... | collective-permute-start | bytes 294920 | tf_op jit(solution)/shard_map/ppermute | solution.py:189
  28.8 4.9 %collective-permute-start.8 = (f32[64,384]{1,0:T(8,128)S(1)}, f32[64,384]{1,0:T(8,128)S(1)}, u32[]{:S(2)}, u32[]{:S(2)}) collective-permute-start(f32[64,384]{1,0:T(8,128)S(1)} %get-tuple-element.47.refs_1_), channel_id=1, source_target_pairs={{0,24},{8,16},{16,8},{24,0},{1,25},{9,17},{17,9},{25,1},{2,26},{10... | collective-permute-start | bytes 294920 | tf_op jit(solution)/shard_map/ppermute | solution.py:189
  28.9 4.8 %collective-permute-start.9 = (f32[64,384]{1,0:T(8,128)S(1)}, f32[64,384]{1,0:T(8,128)S(1)}, u32[]{:S(2)}, u32[]{:S(2)}) collective-permute-start(f32[64,384]{1,0:T(8,128)S(1)} %get-tuple-element.48.refs_2_), channel_id=1, source_target_pairs={{0,8},{8,0},{16,24},{24,16},{1,9},{9,1},{17,25},{25,17},{2,10},{10... | collective-permute-start | bytes 294920 | tf_op jit(solution)/shard_map/ppermute | solution.py:189
  34.1 4.9 %collective-permute-start.10 = (f32[64,384]{1,0:T(8,128)S(1)}, f32[64,384]{1,0:T(8,128)S(1)}, u32[]{:S(2)}, u32[]{:S(2)}) collective-permute-start(f32[64,384]{1,0:T(8,128)S(1)} %get-tuple-element.51.refs_1_), channel_id=1, source_target_pairs={{0,24},{8,16},{16,8},{24,0},{1,25},{9,17},{17,9},{25,1},{2,26},{10... | collective-permute-start | bytes 294920 | tf_op jit(solution)/shard_map/ppermute | solution.py:189
  34.2 4.8 %collective-permute-start.11 = (f32[64,384]{1,0:T(8,128)S(1)}, f32[64,384]{1,0:T(8,128)S(1)}, u32[]{:S(2)}, u32[]{:S(2)}) collective-permute-start(f32[64,384]{1,0:T(8,128)S(1)} %get-tuple-element.52.refs_2_), channel_id=1, source_target_pairs={{0,8},{8,0},{16,24},{24,16},{1,9},{9,1},{17,25},{25,17},{2,10},{10... | collective-permute-start | bytes 294920 | tf_op jit(solution)/shard_map/ppermute | solution.py:189
  39.4 4.8 %collective-permute-start.12 = (f32[64,384]{1,0:T(8,128)S(1)}, f32[64,384]{1,0:T(8,128)S(1)}, u32[]{:S(2)}, u32[]{:S(2)}) collective-permute-start(f32[64,384]{1,0:T(8,128)S(1)} %get-tuple-element.55.refs_1_), channel_id=1, source_target_pairs={{0,24},{8,16},{16,8},{24,0},{1,25},{9,17},{17,9},{25,1},{2,26},{10... | collective-permute-start | bytes 294920 | tf_op jit(solution)/shard_map/ppermute | solution.py:189
  39.5 4.8 %collective-permute-start.13 = (f32[64,384]{1,0:T(8,128)S(1)}, f32[64,384]{1,0:T(8,128)S(1)}, u32[]{:S(2)}, u32[]{:S(2)}) collective-permute-start(f32[64,384]{1,0:T(8,128)S(1)} %get-tuple-element.56.refs_2_), channel_id=1, source_target_pairs={{0,8},{8,0},{16,24},{24,16},{1,9},{9,1},{17,25},{25,17},{2,10},{10... | collective-permute-start | bytes 294920 | tf_op jit(solution)/shard_map/ppermute | solution.py:189
  44.7 4.8 %collective-permute-start.14 = (f32[64,384]{1,0:T(8,128)S(1)}, f32[64,384]{1,0:T(8,128)S(1)}, u32[]{:S(2)}, u32[]{:S(2)}) collective-permute-start(f32[64,384]{1,0:T(8,128)S(1)} %get-tuple-element.59.refs_1_), channel_id=1, source_target_pairs={{0,24},{8,16},{16,8},{24,0},{1,25},{9,17},{17,9},{25,1},{2,26},{10... | collective-permute-start | bytes 294920 | tf_op jit(solution)/shard_map/ppermute | solution.py:189
  44.8 4.8 %collective-permute-start.15 = (f32[64,384]{1,0:T(8,128)S(1)}, f32[64,384]{1,0:T(8,128)S(1)}, u32[]{:S(2)}, u32[]{:S(2)}) collective-permute-start(f32[64,384]{1,0:T(8,128)S(1)} %get-tuple-element.60.refs_2_), channel_id=1, source_target_pairs={{0,8},{8,0},{16,24},{24,16},{1,9},{9,1},{17,25},{25,17},{2,10},{10... | collective-permute-start | bytes 294920 | tf_op jit(solution)/shard_map/ppermute | solution.py:189
  51.3 17.8 %all-to-all-start = ((f32[8,96,128]{2,1,0:T(8,128)}), f32[8,96,128]{2,1,0:T(8,128)S(1)}, u32[]{:S(2)}, u32[]{:S(2)}) async-start(f32[8,96,128]{2,1,0:T(8,128)} %reshape.16), calls=%async_computation | async-start | bytes 786432 | tf_op jit(solution)/shard_map/all_to_all | solution.py:336
  69.9 1.7 %collective-permute-start.16 = (f32[640,128]{1,0:T(8,128)S(1)}, f32[640,128]{1,0:T(8,128)S(1)}, u32[]{:S(2)}, u32[]{:S(2)}) collective-permute-start(f32[640,128]{1,0:T(8,128)S(1)} %dynamic-slice_bitcast_fusion), channel_id=1, source_target_pairs={{0,8},{1,9},{2,10},{3,11},{4,12},{5,13},{6,14},{7,15},{8,0},{9,1},... | collective-permute-start | bytes 983048 | tf_op jit(solution)/shard_map/ppermute | solution.py:220
  71.7 4.9 %collective-permute-start.17 = (f32[160,128]{1,0:T(8,128)S(1)}, f32[160,128]{1,0:T(8,128)S(1)}, u32[]{:S(2)}, u32[]{:S(2)}) collective-permute-start(f32[160,128]{1,0:T(8,128)S(1)} %get-tuple-element.73), channel_id=1, source_target_pairs={{0,16},{1,17},{2,18},{3,19},{4,20},{5,21},{6,22},{7,23},{8,24},{9,... | collective-permute-start | bytes 245768 | tf_op jit(solution)/shard_map/ppermute | solution.py:220
  72.3 5.2 %collective-permute-start.18 = (f32[160,128]{1,0:T(8,128)S(1)}, f32[160,128]{1,0:T(8,128)S(1)}, u32[]{:S(2)}, u32[]{:S(2)}) collective-permute-start(f32[160,128]{1,0:T(8,128)S(1)} %get-tuple-element.75), channel_id=1, source_target_pairs={{0,1},{1,0},{2,3},{3,2},{4,5},{5,4},{6,7},{7,6},{8,9},{9,8},{10,11... | collective-permute-start | bytes 245768 | tf_op jit(solution)/shard_map/ppermute | solution.py:220
  73.8 5.3 %collective-permute-start.19 = (f32[160,128]{1,0:T(8,128)S(1)}, f32[160,128]{1,0:T(8,128)S(1)}, u32[]{:S(2)}, u32[]{:S(2)}) collective-permute-start(f32[160,128]{1,0:T(8,128)S(1)} %get-tuple-element.74), channel_id=1, source_target_pairs={{0,17},{1,16},{2,19},{3,18},{4,21},{5,20},{6,23},{7,22},{8,25},{9,... | collective-permute-start | bytes 245768 | tf_op jit(solution)/shard_map/ppermute | solution.py:220
  79.1 4.5 %collective-permute-start.20 = (f32[160,128]{1,0:T(8,128)S(1)}, f32[160,128]{1,0:T(8,128)S(1)}, u32[]{:S(2)}, u32[]{:S(2)}) collective-permute-start(f32[160,128]{1,0:T(8,128)S(1)} %fusion.5), channel_id=1, source_target_pairs={{0,2},{1,3},{2,0},{3,1},{4,6},{5,7},{6,4},{7,5},{8,10},{9,11},{10,... | collective-permute-start | bytes 245768 | tf_op jit(solution)/shard_map/ppermute | solution.py:220
  79.3 8.3 %collective-permute-start.21 = (f32[160,128]{1,0:T(8,128)S(1)}, f32[160,128]{1,0:T(8,128)S(1)}, u32[]{:S(2)}, u32[]{:S(2)}) collective-permute-start(f32[160,128]{1,0:T(8,128)S(1)} %fusion.5), channel_id=1, source_target_pairs={{0,4},{1,5},{2,6},{3,7},{4,0},{5,1},{6,2},{7,3},{8,12},{9,13},{10,... | collective-permute-start | bytes 245768 | tf_op jit(solution)/shard_map/ppermute | solution.py:220
  81.2 6.4 %collective-permute-start.22 = (f32[160,128]{1,0:T(8,128)S(1)}, f32[160,128]{1,0:T(8,128)S(1)}, u32[]{:S(2)}, u32[]{:S(2)}) collective-permute-start(f32[160,128]{1,0:T(8,128)S(1)} %fusion.5), channel_id=1, source_target_pairs={{0,6},{1,7},{2,4},{3,5},{4,2},{5,3},{6,0},{7,1},{8,14},{9,15},{10,... | collective-permute-start | bytes 245768 | tf_op jit(solution)/shard_map/ppermute | solution.py:220
  87.6 4.5 %collective-permute-start.23 = (f32[160,128]{1,0:T(8,128)S(1)}, f32[160,128]{1,0:T(8,128)S(1)}, u32[]{:S(2)}, u32[]{:S(2)}) collective-permute-start(f32[160,128]{1,0:T(8,128)S(1)} %add_add_fusion), channel_id=1, source_target_pairs={{0,16},{1,17},{2,18},{3,19},{4,20},{5,21},{6,22},{7,23},{8,24},{9,... | collective-permute-start | bytes 245768 | tf_op jit(solution)/shard_map/ppermute | solution.py:220
  89.1 4.4 %collective-permute-start.24 = (f32[160,128]{1,0:T(8,128)S(1)}, f32[160,128]{1,0:T(8,128)S(1)}, u32[]{:S(2)}, u32[]{:S(2)}) collective-permute-start(f32[160,128]{1,0:T(8,128)S(1)} %add_add_fusion), channel_id=1, source_target_pairs={{0,1},{1,0},{2,3},{3,2},{4,5},{5,4},{6,7},{7,6},{8,9},{9,8},{10,11... | collective-permute-start | bytes 245768 | tf_op jit(solution)/shard_map/ppermute | solution.py:220
  90.0 5.3 %collective-permute-start.25 = (f32[160,128]{1,0:T(8,128)S(1)}, f32[160,128]{1,0:T(8,128)S(1)}, u32[]{:S(2)}, u32[]{:S(2)}) collective-permute-start(f32[160,128]{1,0:T(8,128)S(1)} %add_add_fusion), channel_id=1, source_target_pairs={{0,17},{1,16},{2,19},{3,18},{4,21},{5,20},{6,23},{7,22},{8,25},{9,... | collective-permute-start | bytes 245768 | tf_op jit(solution)/shard_map/ppermute | solution.py:220
  95.5 1.7 %collective-permute-start.26 = (f32[640,128]{1,0:T(8,128)S(1)}, f32[640,128]{1,0:T(8,128)S(1)}, u32[]{:S(2)}, u32[]{:S(2)}) collective-permute-start(f32[640,128]{1,0:T(8,128)S(1)} %get-tuple-element.67), channel_id=1, source_target_pairs={{0,8},{1,9},{2,10},{3,11},{4,12},{5,13},{6,14},{7,15},{8,0},{9,1},... | collective-permute-start | bytes 983048 | tf_op jit(solution)/shard_map/ppermute | solution.py:220
where the time goes:
time: 99.4 us; the launch traced here: 99.1 us
  waiting for transfers between devices  46.9 us (47%)
  starting transfers between devices  22.4 us (23%)
  Pallas kernels  21.3 us (21%)
  local copies, waits for them, and re-layouts  5.41 us (5%)
  between operations  1.69 us (2%)
  other arithmetic  1.32 us (1%)
    ppermute x8, waiting for transfers between devices, exchange(): lax.ppermute(far, 'narrow', far_pairs)  19.7 us
    ppermute x11, waiting for transfers between devices, swap(): return lax.ppermute(x, ('narrow', 'wide'), pair_perm(mask))  15.3 us
    pallas_call x8, Pallas kernels, local_part(): pl.pallas_call(functools.partial(local_kernel, first_step), in_specs=[SM,...  14.3 us
    all_to_all x1, waiting for transfers between devices, regroup(): lax.all_to_all(parts, 'wide', split_axis=0, concat_axis=0, tiled=True)  12 us
    ppermute x11, starting transfers between devices, swap(): return lax.ppermute(x, ('narrow', 'wide'), pair_perm(mask))  11.7 us
    all_to_all x1, starting transfers between devices, regroup(): lax.all_to_all(parts, 'wide', split_axis=0, concat_axis=0, tiled=True)  5.86 us
    pallas_call x7, Pallas kernels, halo_part(): pl.pallas_call(functools.partial(halo_kernel, first_step), in_specs=[VM]...  3.07 us
    ppermute x8, starting transfers between devices, exchange(): lax.ppermute(far, 'narrow', far_pairs)  3.01 us
  transfers between devices with their start and end apart: 28, of which 18 were waited for; matrix products, arithmetic and copies ran while one was open for 1% of the time, Pallas kernels for 17%

commit v1 on v0

v1 whole, which is shorter than its diff:
```python
import functools

import jax
import jax.numpy as jnp
from jax import lax
from jax.experimental import pallas as pl
from jax.experimental.pallas import tpu as pltpu
from jax.sharding import PartitionSpec as P

REACH = 3
STEPS = 8
TILE = 128
VM = pl.BlockSpec(memory_space=pltpu.VMEM)
SM = pl.BlockSpec(memory_space=pltpu.SMEM)
HBM = pl.BlockSpec(memory_space=pltpu.HBM)
NT = (((1,), (1,)), ((), ()))
NN = (((1,), (0,)), ((), ()))
F32 = jnp.float32
BF16 = jnp.bfloat16


def params():
    return pltpu.CompilerParams(vmem_limit_bytes=40 * 1024 * 1024)


def split(x):
    hi = x.astype(BF16)
    return hi, (x - hi.astype(F32)).astype(BF16)


def in_hbm(x):
    return pltpu.with_memory_space_constraint(x, pltpu.HBM)


def odd_device():
    return lax.rem(lax.axis_index("narrow"), 2) == 1


def dot(a, b, dims):
    return lax.dot_general(a, b, dims, preferred_element_type=F32)


def dot_split(a_hi, a_both, b_hi, b_lo, dims):
    rows = a_hi.shape[0]
    upper = dot(a_both, b_hi, dims)
    return upper[:rows] + (upper[rows:] + dot(a_hi, b_lo, dims))


def spread_kernel(total_blocks, columns_hbm, vectors_hbm, blocks_hbm, far_ref, near_ref, vectors_ref, hi_ref, lo_ref, held, columns_ref, sems, row_sems):
    rows, slots, size, _ = blocks_hbm.shape
    edge = far_ref.shape[1]
    begin = vectors_hbm.shape[1] - edge
    odd = odd_device()

    def edge_at(at):
        return vectors_hbm.at[:, pl.ds(pl.multiple_of(at, size), edge)]

    small = [
        (columns_hbm, columns_ref),
        (edge_at(jnp.where(odd, begin, 0)), far_ref),
        (edge_at(jnp.where(odd, 0, begin)), near_ref),
        (vectors_hbm, vectors_ref),
    ]
    small = [pltpu.make_async_copy(here, there, sems.at[k]) for k, (here, there) in enumerate(small)]
    large = [pltpu.make_async_copy(blocks_hbm.at[row], held.at[row], row_sems.at[row]) for row in range(rows)]
    for copy in small[:1] + large + small[1:]:
        copy.start()
    hi_ref[...] = jnp.zeros_like(hi_ref)
    lo_ref[...] = jnp.zeros_like(lo_ref)
    first = lax.axis_index("narrow") * rows
    small[0].wait()
    for row in range(rows):
        large[row].wait()
        pair, half = divmod(row, 2)
        here = slice(half * size, half * size + size)
        for slot in range(slots):
            place = columns_ref[slot, row] - first + REACH
            place = jnp.where(place < 0, place + total_blocks, place)
            place = jnp.where(place >= total_blocks, place - total_blocks, place) - 2 * pair
            hi, lo = split(held[row, slot])
            there = pl.ds(pl.multiple_of(place * size, size), size)
            hi_ref[pair, here, there] = hi
            lo_ref[pair, here, there] = lo
    for copy in small[1:]:
        copy.wait()


def spread_part(columns, vectors, blocks, total_blocks):
    rows, slots, size, _ = blocks.shape
    spread = jax.ShapeDtypeStruct((rows // 2, 2 * size, (2 * REACH + 2) * size), BF16)
    edge = jax.ShapeDtypeStruct((vectors.shape[0], REACH * size), F32)
    return pl.pallas_call(
        functools.partial(spread_kernel, total_blocks),
        in_specs=[HBM, HBM, HBM],
        out_specs=[VM] * 5,
        out_shape=[edge, edge, jax.ShapeDtypeStruct(vectors.shape, F32), spread, spread],
        scratch_shapes=[
            pltpu.VMEM(blocks.shape, F32),
            pltpu.SMEM((slots, rows), jnp.int32),
            pltpu.SemaphoreType.DMA((4,)),
            pltpu.SemaphoreType.DMA((rows,)),
        ],
        compiler_params=params(),
        name="spread_part",
    )(in_hbm(columns.T), in_hbm(vectors), in_hbm(blocks))


def local_sum(pair, hi, both, hi_ref, lo_ref):
    pairs, width, window = hi_ref.shape
    size = width // 2
    start = 2 * pair - REACH
    begin, end = max(start, 0), min(start + window // size, 2 * pairs)
    there = slice(begin * size, end * size)
    inside = slice((begin - start) * size, (end - start) * size)
    return dot_split(hi[:, there], both[:, there], hi_ref[pair, :, inside], lo_ref[pair, :, inside], NT)


def local_kernel(first_step, terms_ref, mid_ref, *refs):
    if first_step:
        hi_ref, lo_ref, out_ref = refs
        current = mid_ref[...]
    else:
        far_ref, near_ref, previous_ref, hi_ref, lo_ref, out_ref, *full_ref = refs
        edge = far_ref.shape[1]
        odd = odd_device()
        left = jnp.where(odd, near_ref[...], far_ref[...])
        right = jnp.where(odd, far_ref[...], near_ref[...])
        current = jnp.concatenate([left, mid_ref[:, edge:-edge], right], axis=1)
        if full_ref:
            full_ref[0][...] = current
    pairs, width, _ = hi_ref.shape
    scale, diag = terms_ref[0:1, :], terms_ref[1:2, :]
    hi, lo = split(current)
    both = jnp.concatenate([hi, lo], axis=0)
    for pair in range(pairs):
        here = slice(pair * width, pair * width + width)
        total = scale * local_sum(pair, hi, both, hi_ref, lo_ref) + diag * current[:, here]
        out_ref[:, here] = 0.5 * total if first_step else total - previous_ref[:, here]


def local_part(terms, state, previous, operator, last):
    mid = state[0]
    shape = jax.ShapeDtypeStruct(mid.shape, F32)
    width = operator[0].shape[1]
    first_step = previous is None
    operands = (terms, *state, *(() if first_step else (previous,)), *operator)
    outs = 1 if first_step or last else 2
    return pl.pallas_call(
        functools.partial(local_kernel, first_step),
        in_specs=[VM] * len(operands),
        out_specs=[VM] * outs,
        out_shape=[shape] * outs,
        compiler_params=params(),
        cost_estimate=pl.CostEstimate(flops=24 * mid.size * width, bytes_accessed=8 * mid.size, transcendentals=0),
        name="local_part",
    )(*operands)


def edge_sum(factor, at_right, terms_ref, mid_ref, halo_ref, hi_ref, lo_ref):
    pairs, width, window = hi_ref.shape
    size = width // 2
    edge = REACH * size
    hi, lo = split(halo_ref[...])
    both = jnp.concatenate([hi, lo], axis=0)

    def reach_into(pair, length, hi, both):
        inside = pl.ds(pl.multiple_of(jnp.where(at_right, window - length, 0), size), length)
        return dot_split(hi, both, hi_ref[pair, :, inside], lo_ref[pair, :, inside], NT)

    outer = reach_into(jnp.where(at_right, pairs - 1, 0), edge, hi, both)
    close_hi = jnp.where(at_right, hi[:, :size], hi[:, -size:])
    close_both = jnp.where(at_right, both[:, :size], both[:, -size:])
    inner = reach_into(jnp.where(at_right, pairs - 2, 1), size, close_hi, close_both)
    added = jnp.where(
        at_right,
        jnp.concatenate([inner[:, size:], outer], axis=1),
        jnp.concatenate([outer, inner[:, :size]], axis=1),
    )
    here = pl.ds(pl.multiple_of(jnp.where(at_right, mid_ref.shape[1] - edge, 0), size), edge)
    return mid_ref[:, here] + (factor * terms_ref[0:1, 0:1]) * added


def edge_kernel(factor, far, terms_ref, mid_ref, halo_ref, hi_ref, lo_ref, out_ref):
    at_right = odd_device() if far else jnp.logical_not(odd_device())
    out_ref[...] = edge_sum(factor, at_right, terms_ref, mid_ref, halo_ref, hi_ref, lo_ref)


def edge_part(factor, far, terms, mid, halo, operator):
    width = operator[0].shape[1]
    return pl.pallas_call(
        functools.partial(edge_kernel, factor, far),
        in_specs=[VM] * 5,
        out_specs=VM,
        out_shape=jax.ShapeDtypeStruct(halo.shape, F32),
        compiler_params=params(),
        cost_estimate=pl.CostEstimate(flops=12 * halo.size * width, bytes_accessed=8 * halo.size, transcendentals=0),
        name="far_part" if far else "near_part",
    )(terms, mid, halo, *operator)


def packs(count, own):
    return own % TILE == TILE // 2 and own > TILE and count % 16 == 0


def last_kernel(parts, terms_ref, mid_ref, far_ref, near_ref, hi_ref, lo_ref, out_ref):
    odd = odd_device()
    far = edge_sum(1.0, odd, terms_ref, mid_ref, far_ref, hi_ref, lo_ref)
    near = near_ref[...]
    edge = far.shape[1]
    left, right = jnp.where(odd, near, far), jnp.where(odd, far, near)
    whole = jnp.concatenate([left, mid_ref[:, edge:-edge], right], axis=1)
    if out_ref.ndim == 2:
        out_ref[...] = whole
        return
    count, own, half = whole.shape[0], whole.shape[1] // parts, TILE // 2
    for part in range(parts):
        begin = part * own
        head, tail = (begin, begin + own - half) if part % 2 == 0 else (begin + half, begin)
        at = 0
        for column in range(head, head + own - half, TILE):
            out_ref[part, at : at + count, :] = whole[:, column : column + TILE]
            at += count
        tails = whole[:, tail : tail + half]
        out_ref[part, at:, :] = jnp.concatenate([tails[: count // 2], tails[count // 2 :]], axis=1)


def last_part(terms, mid, far, near, operator, parts):
    count, length = mid.shape
    shape = (parts, count * length // parts // TILE, TILE) if packs(count, length // parts) else mid.shape
    return pl.pallas_call(
        functools.partial(last_kernel, parts),
        in_specs=[VM] * 6,
        out_specs=VM,
        out_shape=jax.ShapeDtypeStruct(shape, F32),
        compiler_params=params(),
        name="last_part",
    )(terms, mid, far, near, *operator)


def exchange(far, near):
    size = lax.axis_size("narrow")
    far_pairs = [(i, (i + 1) % size if i % 2 else (i - 1) % size) for i in range(size)]
    near_pairs = [(i, i ^ 1) for i in range(size)]
    return lax.ppermute(far, "narrow", far_pairs), lax.ppermute(near, "narrow", near_pairs)


def filtered_parts(vectors, blocks, columns, lower_bound, upper_bound):
    total_blocks = blocks.shape[0] * lax.axis_size("narrow")
    width = 2 * blocks.shape[2]
    half_width = (upper_bound - lower_bound) * 0.5
    scale = 2.0 / half_width
    diag = scale * (1.0 - (upper_bound + lower_bound) * 0.5)
    terms = jnp.concatenate([jnp.broadcast_to(scale, (1, width)), jnp.broadcast_to(diag, (1, width))])
    far, near, vectors, *operator = spread_part(columns, vectors, blocks, total_blocks)
    state, previous = (vectors,), None
    for step in range(STEPS):
        far_halo, near_halo = exchange(far, near)
        mid, *full = local_part(terms, state, previous, operator, step == STEPS - 1)
        previous = full[0] if full else vectors
        factor = 0.5 if step == 0 else 1.0
        near = edge_part(factor, False, terms, mid, near_halo, operator)
        if step < STEPS - 1:
            far = edge_part(factor, True, terms, mid, far_halo, operator)
        state = (mid, far, near)
    return last_part(terms, mid, far_halo, near, operator, lax.axis_size("wide"))


def pair_perm(mask):
    narrow, wide = lax.axis_size("narrow"), lax.axis_size("wide")
    return [(n * wide + w, (n ^ mask[0]) * wide + (w ^ mask[1])) for n in range(narrow) for w in range(wide)]


def swap(x, mask):
    return lax.ppermute(x, ("narrow", "wide"), pair_perm(mask))


def bit_groups():
    narrow = [(1 << b, 0) for b in range(lax.axis_size("narrow").bit_length() - 1)]
    wide = [(0, 1 << b) for b in range(lax.axis_size("wide").bit_length() - 1)]
    rest = wide[1:] + narrow[2:]
    return [narrow[:1], narrow[1:2] + wide[:1]] + [rest[i : i + 2] for i in range(0, len(rest), 2)]


def masks(bits):
    out = []
    for d in range(1 << len(bits)):
        chosen = [b for k, b in enumerate(bits) if d >> k & 1]
        out.append((sum(b[0] for b in chosen), sum(b[1] for b in chosen)))
    return out


def place_in(bits):
    n, w = lax.axis_index("narrow"), lax.axis_index("wide")
    place = 0
    for k, b in enumerate(bits):
        bit = lax.rem(lax.div(n, b[0]), 2) if b[0] else lax.rem(lax.div(w, b[1]), 2)
        place = place + bit * (1 << k)
    return place


def relative(place, d, count):
    out = 0
    for k in range(count.bit_length() - 1):
        bit = lax.rem(lax.div(place, 1 << k), 2)
        out = out + (1 << k) * (1 - bit if d >> k & 1 else bit)
    return out


def chunk_at(place, d, count, rows):
    return pl.ds(pl.multiple_of(relative(place, d, count) * rows, 8), rows)


def fold_kernel(bits, *refs):
    count = 1 << len(bits)
    parts, outs = refs[:-count], refs[-count:]
    place = place_in(bits)
    rows = outs[0].shape[0]
    for d in range(count):
        here = chunk_at(place, d, count, rows)
        total = parts[0][here, :]
        for part in parts[1:]:
            total = total + part[here, :]
        outs[d][...] = total


def fold(parts, bits):
    count = 1 << len(bits)
    rows, width = parts[0].shape
    return pl.pallas_call(
        functools.partial(fold_kernel, bits),
        in_specs=[VM] * len(parts),
        out_specs=[VM] * count,
        out_shape=[jax.ShapeDtypeStruct((rows // count, width), F32)] * count,
        compiler_params=params(),
        name="fold",
    )(*parts)


def fan(parts, bits):
    members = masks(bits)
    got = {d: swap(parts[d], members[d]) for d in reversed(range(1, len(members)))}
    return [parts[0]] + [got[d] for d in range(1, len(members))]


def all_sum(halves):
    groups = bit_groups()
    parts = fan(halves, groups[0])
    for bits in groups[1:-1]:
        parts = fan(fold(parts, bits), bits)
    x = sum(parts)
    x = sum(fan([x] * (1 << len(groups[-1])), groups[-1]))
    for bits in groups[1:-1][::-1]:
        blocks = fan([x] * (1 << len(bits)), bits)
        x = jnp.concatenate(blocks)
    return x, swap(x, masks(groups[0])[1])


def sum_order():
    groups = bit_groups()
    return groups[1:-1]


def tile_pairs(count):
    return [(i, j) for i in range(count) for j in range(i + 1, count)]


def packed_rows(count):
    rows = len(tile_pairs(count)) * TILE + count * TILE // 2 + count // 2 * TILE // 2
    blocks = 8
    for bits in bit_groups()[:-1]:
        blocks <<= len(bits)
    return -(-rows // blocks) * blocks


def gram_kernel(own, parts_ref, keep_ref, send_ref, rows_ref, packed):
    if parts_ref.ndim == 2:
        rows = parts_ref[...]
    else:
        parts, length, _ = parts_ref.shape
        count, half = length * TILE // own, TILE // 2
        heads = (own - half) // TILE
        odd = lax.rem(lax.axis_index("wide"), 2) == 1
        pieces = []
        for part in range(parts):
            head = [parts_ref[part, h * count : (h + 1) * count, :] for h in range(heads)]
            tails = parts_ref[part, heads * count :, :]
            swapped = pltpu.roll(tails, half, 1)
            low = lax.broadcasted_iota(jnp.int32, tails.shape, 1) < half
            tail = jnp.concatenate([jnp.where(low, tails, swapped), jnp.where(low, swapped, tails)], axis=0)
            whole = jnp.concatenate(head + [tail], axis=1)
            pieces.append(jnp.where(odd, pltpu.roll(whole, half, 1), whole)[:, :own])
        rows = jnp.concatenate(pieces, axis=0)
    rows_ref[...] = rows.T
    tiles, half = rows.shape[0] // TILE, TILE // 2
    hi, lo = split(rows)
    at, tops = 0, len(tile_pairs(tiles)) * TILE
    lasts = tops + tiles * half
    for i in range(tiles):
        here, there = slice(i * TILE, (i + 1) * TILE), slice(i * TILE, None)
        both = jnp.concatenate([hi[here], lo[here]], axis=0)
        strip = dot_split(hi[here], both, hi[there], lo[there], NT)
        packed[tops + i * half : tops + (i + 1) * half, :] = strip[:half, :TILE]
        last = strip[half:, half:TILE]
        if i % 2 == 0:
            held = last
        else:
            packed[lasts + i // 2 * half : lasts + (i // 2 + 1) * half, :] = jnp.concatenate([held, last], axis=1)
        for j in range(i + 1, tiles):
            packed[at : at + TILE, :] = strip[:, (j - i) * TILE : (j - i + 1) * TILE]
            at += TILE
    used = lasts + tiles // 2 * half
    if used < packed.shape[0]:
        packed[used:, :] = jnp.zeros((packed.shape[0] - used, TILE), F32)
    odd, size = odd_device(), keep_ref.shape[0]
    keep_ref[...] = packed[pl.ds(pl.multiple_of(jnp.where(odd, size, 0), 8), size), :]
    send_ref[...] = packed[pl.ds(pl.multiple_of(jnp.where(odd, 0, size), 8), size), :]


def gram(parts, own):
    total = parts.size // own
    size = packed_rows(total // TILE)
    half = jax.ShapeDtypeStruct((size // 2, TILE), F32)
    return pl.pallas_call(
        functools.partial(gram_kernel, own),
        in_specs=[VM],
        out_specs=[VM] * 3,
        out_shape=[half, half, jax.ShapeDtypeStruct((own, total), F32)],
        scratch_shapes=[pltpu.VMEM((size, TILE), F32)],
        compiler_params=params(),
        name="gram",
    )(parts)


def rotate_kernel(total_rows, groups, own_ref, other_ref, rows_ref, out_ref, packed, hi_ref, lo_ref, held, sems):
    size = own_ref.shape[0]
    places = [place_in(bits) for bits in groups]
    blocks = 1
    for bits in groups:
        blocks <<= len(bits)
    length = size // blocks
    odd = odd_device()
    for block in range(blocks):
        at, rest, step = 0, block, blocks
        for bits, place in zip(groups, places):
            count = 1 << len(bits)
            step //= count
            at = at + relative(place, rest // step, count) * (step * length)
            rest %= step
        here = slice(block * length, (block + 1) * length)
        packed[pl.ds(pl.multiple_of(jnp.where(odd, size, 0) + at, 8), length), :] = own_ref[here, :]
        packed[pl.ds(pl.multiple_of(jnp.where(odd, 0, size) + at, 8), length), :] = other_ref[here, :]
    tiles, half = rows_ref.shape[1] // TILE, TILE // 2
    order = tile_pairs(tiles)
    tops = len(order) * TILE
    lasts = tops + tiles * half
    above = packed[:tops, :].reshape(len(order), TILE, TILE)
    squares = jnp.sum(above * above, axis=0) * 2.0
    top = packed[tops:lasts, :].reshape(tiles, half, TILE)
    weight = jnp.where(lax.broadcasted_iota(jnp.int32, (half, TILE), 1) < half, 1.0, 2.0)
    last = packed[lasts : lasts + tiles // 2 * half, :].reshape(tiles // 2, half, TILE)
    squares = squares[:half] + squares[half:] + jnp.sum(top * top, axis=0) * weight + jnp.sum(last * last, axis=0)
    frob = jnp.sqrt(jnp.sum(squares, axis=(0, 1), keepdims=True) + 1e-06)
    factor = 0.5 / frob
    gain = jnp.sqrt(total_rows / frob)
    for at, (i, j) in enumerate(order):
        hi, lo = split(packed[at * TILE : (at + 1) * TILE, :] * factor)
        one, two = slice(i * TILE, (i + 1) * TILE), slice(j * TILE, (j + 1) * TILE)
        hi_ref[one, two] = hi
        lo_ref[one, two] = lo
        hi_ref[two, one] = hi.T
        lo_ref[two, one] = lo.T
    for i in range(tiles):
        upper = packed[tops + i * half : tops + (i + 1) * half, :]
        quarter = packed[lasts + i // 2 * half : lasts + (i // 2 + 1) * half, :][:, i % 2 * half : (i % 2 + 1) * half]
        lower = jnp.concatenate([upper[:, half:].T, quarter], axis=1)
        hi, lo = split(jnp.concatenate([upper, lower], axis=0) * factor)
        one = slice(i * TILE, (i + 1) * TILE)
        hi_ref[one, one] = hi
        lo_ref[one, one] = lo
    rows = rows_ref[...]
    rows_hi, rows_lo = split(rows)
    both = jnp.concatenate([rows_hi, rows_lo], axis=0)
    copies = []
    for strip in range(tiles // 2):
        here = slice(strip * 2 * TILE, (strip + 1) * 2 * TILE)
        turned = dot_split(rows_hi, both, hi_ref[:, here], lo_ref[:, here], NN)
        held[:, here] = gain * (1.5 * rows[:, here] - turned)
        copies.append(pltpu.make_async_copy(held.at[:, here], out_ref.at[:, here], sems.at[strip]))
        copies[-1].start()
    for copy in copies:
        copy.wait()


def rotate(halves, rows, total_rows):
    own, total = rows.shape
    return pl.pallas_call(
        functools.partial(rotate_kernel, float(total_rows), sum_order()),
        in_specs=[VM, VM, VM],
        out_specs=HBM,
        out_shape=pltpu.HBM(rows.shape, F32),
        scratch_shapes=[
            pltpu.VMEM((packed_rows(total // TILE), TILE), F32),
            pltpu.VMEM((total, total), BF16),
            pltpu.VMEM((total, total), BF16),
            pltpu.VMEM(rows.shape, F32),
            pltpu.SemaphoreType.DMA((total // TILE // 2,)),
        ],
        compiler_params=params(),
        name="rotate",
    )(*halves, rows).T


def regroup(parts):
    size = lax.axis_size("wide")
    if parts.ndim == 3:
        return lax.all_to_all(parts, "wide", split_axis=0, concat_axis=0, tiled=True)
    count, length = parts.shape
    own = length // size
    parts = parts.reshape(count, size, own).transpose(1, 0, 2).reshape(size, count * own // TILE, TILE)
    parts = lax.all_to_all(parts, "wide", split_axis=0, concat_axis=0, tiled=True)
    return parts.reshape(size * count, own)


def on_device(vectors, blocks, columns, lower_bound, upper_bound):
    length = vectors.shape[1]
    parts = regroup(filtered_parts(vectors, blocks, columns, lower_bound, upper_bound))
    *halves, rows = gram(parts, length // lax.axis_size("wide"))
    return rotate(all_sum(halves), rows, length * lax.axis_size("narrow"))


def solution(mesh):
    return jax.shard_map(
        on_device,
        mesh=mesh,
        in_specs=(P("wide", "narrow"), P("narrow", None, None, None), P("narrow", None), P(), P()),
        out_specs=P(None, ("narrow", "wide")),
        check_vma=False,
    )
```

time: 99.4 us -> 91.7 us (0.923)
  waiting for transfers between devices: 46.9 us -> 23.5 us
  blocking collectives: 0 us -> 18 us
  local copies, waits for them, and re-layouts: 5.41 us -> 0.07 us
  starting transfers between devices: 22.4 us -> 24.7 us
  Pallas kernels: 21.3 us -> 23.4 us
  other arithmetic: 1.32 us -> 0.06 us
    all_to_all x0 -> x1, blocking collectives: none -> 18 us  [regroup(): lax.all_to_all(parts, 'wide', split_axis=0, concat_axis=0, tiled=True)]
    all_to_all x1 -> x0, waiting for transfers between devices: 12 us -> none  [regroup(): lax.all_to_all(parts, 'wide', split_axis=0, concat_axis=0, tiled=True)]
    ppermute x8, waiting for transfers between devices: 19.7 us -> 8.89 us  [exchange(): lax.ppermute(far, 'narrow', far_pairs)]
    ppermute x8, starting transfers between devices: 3.01 us -> 10.6 us  [exchange(): lax.ppermute(far, 'narrow', far_pairs)]
    all_to_all x1 -> x0, starting transfers between devices: 5.86 us -> none  [regroup(): lax.all_to_all(parts, 'wide', split_axis=0, concat_axis=0, tiled=True)]
    unnamed x5 -> x0, local copies, waits for them, and re-layouts: 2.89 us -> none
    pallas_call x19 -> x28, Pallas kernels: 21.3 us -> 23.4 us  [the longest x8 13.7 us: local_part(): pl.pallas_call(functools.partial(local_kernel, first_step), in_specs=[VM]...]
    reshape x3 -> x0, local copies, waits for them, and re-layouts: 1.32 us -> none  [the longest x2 1.18 us: regroup(): rows.reshape(count, size, own).transpose(1, 0, 2)]
  transfers between devices with their start and end apart: 28 -> 27, of which waited for: 18 -> 17; matrix products, arithmetic and copies ran while one was open for 1% -> 0% of each run, Pallas kernels for 17% -> 20%
where the time goes in v1:
time: 91.7 us; the launch traced here: 91.5 us
  starting transfers between devices  24.7 us (27%)
  waiting for transfers between devices  23.5 us (26%)
  Pallas kernels  23.4 us (26%)
  blocking collectives  18 us (20%)
  between operations  1.82 us (2%)
    all_to_all x1, blocking collectives, regroup(): lax.all_to_all(parts, 'wide', split_axis=0, concat_axis=0, tiled=True)  18 us
    ppermute x11, waiting for transfers between devices, swap(): return lax.ppermute(x, ('narrow', 'wide'), pair_perm(mask))  14.6 us
    pallas_call x8, Pallas kernels, local_part(): pl.pallas_call(functools.partial(local_kernel, first_step), in_specs=[VM]...  13.7 us
    ppermute x11, starting transfers between devices, swap(): return lax.ppermute(x, ('narrow', 'wide'), pair_perm(mask))  11.7 us
    ppermute x8, starting transfers between devices, exchange(): lax.ppermute(far, 'narrow', far_pairs)  10.6 us
    ppermute x8, waiting for transfers between devices, exchange(): lax.ppermute(far, 'narrow', far_pairs)  8.89 us
    pallas_call x15, Pallas kernels, edge_part(): pl.pallas_call(functools.partial(edge_kernel, factor, far), in_specs=[VM]...  4.34 us
    pallas_call x1, Pallas kernels, spread_part(): pl.pallas_call(functools.partial(spread_kernel, total_blocks), in_specs=[...  2.48 us
  transfers between devices with their start and end apart: 27, of which 17 were waited for; matrix products, arithmetic and copies ran while one was open for 0% of the time, Pallas kernels for 20%

profile of v1, /device:TPU:0, one launch (start us, length us, event | category | flops | bytes accessed | tf_op | source)
XLA Modules:
  0.0 91.5 jit_solution(13482776844174304126)
XLA Ops:
  0.0 2.5 %spread_part.1 = (f32[64,384]{1,0:T(8,128)S(1)}, f32[64,384]{1,0:T(8,128)S(1)}, f32[64,1536]{1,0:T(8,128)S(1)}, bf16[6,256,1024]{2,1,0:T(8,128)(2,1)S(1)}, bf16[6,256,1024]{2,1,0:T(8,128)(2,1)S(1)}) custom-call(s32[5,12]{1,0:T(8,128)} %bitcast.3, f32[64,1536]{1,0:T(8,128)} %vectors_hbm.1, f32[12,5,128,128]{3,2,1,0:T(8,128)} %blocks_hbm.1), custom_call_target="tpu_custom_call" | custom-call | tf_op jit(solution)/shard_map/spread_part/pallas_call | solution.py:92
  2.5 0.5 collective-permute-start.1
  3.0 2.6 %collective-permute-start = (f32[64,384]{1,0:T(8,128)S(1)}, f32[64,384]{1,0:T(8,128)S(1)}, u32[]{:S(2)}, u32[]{:S(2)}) collective-permute-start(f32[64,384]{1,0:T(8,128)S(1)} %get-tuple-element.32), channel_id=1, source_target_pairs={{0,24},{8,16},{16,8},{24,0},{1,25},{9,17},{17,9},{25,1},{2,26},{10... | collective-permute-start | bytes 294920 | tf_op jit(solution)/shard_map/ppermute | solution.py:244
  7.0 1.7 %local_part.8.mid_ref = f32[64,1536]{1,0:T(8,128)S(1)} custom-call(f32[2,256]{1,0:T(2,128)S(1)} %concatenate.9.terms_ref, f32[64,1536]{1,0:T(8,128)S(1)} %get-tuple-element.29.mid_ref.refs_2_, bf16[6,256,1024]{2,1,0:T(8,128)(2,1)S(1)} %get-tuple-element.30.refs_0_.hi_ref.refs_3_, bf16[6,256,1024]{2,1,0:T(8,128)(2,1)S(1)} %get-tuple-element.31.refs_1_.lo_ref.refs_4_), custom_call_target="tpu_custom_call" | custom-call | flops 603979776 | bytes 786432 | tf_op jit(solution)/shard_map/local_part/pallas_call | solution.py:148
  9.5 1.0 %collective-permute-start.2 = (f32[64,384]{1,0:T(8,128)S(1)}, f32[64,384]{1,0:T(8,128)S(1)}, u32[]{:S(2)}, u32[]{:S(2)}) collective-permute-start(f32[64,384]{1,0:T(8,128)S(1)} %far_part.7.refs_0_), channel_id=1, source_target_pairs={{0,24},{8,16},{16,8},{24,0},{1,25},{9,17},{17,9},{25,1},{2,26},{10... | collective-permute-start | bytes 294920 | tf_op jit(solution)/shard_map/ppermute | solution.py:244
  10.5 1.7 %local_part.9 = (f32[64,1536]{1,0:T(8,128)S(1)}, f32[64,1536]{1,0:T(8,128)S(1)}) custom-call(f32[2,256]{1,0:T(2,128)S(1)} %concatenate.9.terms_ref, f32[64,1536]{1,0:T(8,128)S(1)} %local_part.8.mid_ref, f32[64,384]{1,0:T(8,128)S(1)} %far_part.7.refs_0_, f32[64,384]{1,0:T(8,128)S(1)} %near_part.8.refs_1_, f32[64,1536]{1,0:T(8,128)S(1)} %get-tuple-element.29.mid_ref.refs_2_, ...), custom_call_target="tpu_custom_call" | custom-call | flops 603979776 | bytes 786432 | tf_op jit(solution)/shard_map/local_part/pallas_call | solution.py:148
  12.6 1.4 %collective-permute-done.2.halo_ref = f32[64,384]{1,0:T(8,128)S(1)} collective-permute-done((f32[64,384]{1,0:T(8,128)S(1)}, f32[64,384]{1,0:T(8,128)S(1)}, u32[]{:S(2)}, u32[]{:S(2)}) %collective-permute-start.2) | collective-permute-done | bytes 98336 | tf_op jit(solution)/shard_map/ppermute | solution.py:244
  14.3 1.0 %collective-permute-start.4 = (f32[64,384]{1,0:T(8,128)S(1)}, f32[64,384]{1,0:T(8,128)S(1)}, u32[]{:S(2)}, u32[]{:S(2)}) collective-permute-start(f32[64,384]{1,0:T(8,128)S(1)} %far_part.8.refs_0_), channel_id=1, source_target_pairs={{0,24},{8,16},{16,8},{24,0},{1,25},{9,17},{17,9},{25,1},{2,26},{10... | collective-permute-start | bytes 294920 | tf_op jit(solution)/shard_map/ppermute | solution.py:244
  15.3 1.7 %local_part.10 = (f32[64,1536]{1,0:T(8,128)S(1)}, f32[64,1536]{1,0:T(8,128)S(1)}) custom-call(f32[2,256]{1,0:T(2,128)S(1)} %concatenate.9.terms_ref, f32[64,1536]{1,0:T(8,128)S(1)} %get-tuple-element.34.mid_ref, f32[64,384]{1,0:T(8,128)S(1)} %far_part.8.refs_0_, f32[64,384]{1,0:T(8,128)S(1)} %near_part.9.refs_1_, f32[64,1536]{1,0:T(8,128)S(1)} %get-tuple-element.35.refs_2_, ...), custom_call_target="tpu_custom_call" | custom-call | flops 603979776 | bytes 786432 | tf_op jit(solution)/shard_map/local_part/pallas_call | solution.py:148
  17.6 1.4 %collective-permute-done.4.halo_ref = f32[64,384]{1,0:T(8,128)S(1)} collective-permute-done((f32[64,384]{1,0:T(8,128)S(1)}, f32[64,384]{1,0:T(8,128)S(1)}, u32[]{:S(2)}, u32[]{:S(2)}) %collective-permute-start.4) | collective-permute-done | bytes 98336 | tf_op jit(solution)/shard_map/ppermute | solution.py:244
  19.2 1.0 %collective-permute-start.6 = (f32[64,384]{1,0:T(8,128)S(1)}, f32[64,384]{1,0:T(8,128)S(1)}, u32[]{:S(2)}, u32[]{:S(2)}) collective-permute-start(f32[64,384]{1,0:T(8,128)S(1)} %far_part.9.refs_0_), channel_id=1, source_target_pairs={{0,24},{8,16},{16,8},{24,0},{1,25},{9,17},{17,9},{25,1},{2,26},{10... | collective-permute-start | bytes 294920 | tf_op jit(solution)/shard_map/ppermute | solution.py:244
  20.2 1.7 %local_part.11 = (f32[64,1536]{1,0:T(8,128)S(1)}, f32[64,1536]{1,0:T(8,128)S(1)}) custom-call(f32[2,256]{1,0:T(2,128)S(1)} %concatenate.9.terms_ref, f32[64,1536]{1,0:T(8,128)S(1)} %get-tuple-element.36.mid_ref, f32[64,384]{1,0:T(8,128)S(1)} %far_part.9.refs_0_, f32[64,384]{1,0:T(8,128)S(1)} %near_part.10.refs_1_, f32[64,1536]{1,0:T(8,128)S(1)} %get-tuple-element.37.refs_2_, ...), custom_call_target="tpu_custom_call" | custom-call | flops 603979776 | bytes 786432 | tf_op jit(solution)/shard_map/local_part/pallas_call | solution.py:148
  22.5 1.3 %collective-permute-done.6.halo_ref = f32[64,384]{1,0:T(8,128)S(1)} collective-permute-done((f32[64,384]{1,0:T(8,128)S(1)}, f32[64,384]{1,0:T(8,128)S(1)}, u32[]{:S(2)}, u32[]{:S(2)}) %collective-permute-start.6) | collective-permute-done | bytes 98336 | tf_op jit(solution)/shard_map/ppermute | solution.py:244
  24.1 1.1 %collective-permute-start.8 = (f32[64,384]{1,0:T(8,128)S(1)}, f32[64,384]{1,0:T(8,128)S(1)}, u32[]{:S(2)}, u32[]{:S(2)}) collective-permute-start(f32[64,384]{1,0:T(8,128)S(1)} %far_part.10.refs_0_), channel_id=1, source_target_pairs={{0,24},{8,16},{16,8},{24,0},{1,25},{9,17},{17,9},{25,1},{2,26},{10... | collective-permute-start | bytes 294920 | tf_op jit(solution)/shard_map/ppermute | solution.py:244
  25.2 1.7 %local_part.12 = (f32[64,1536]{1,0:T(8,128)S(1)}, f32[64,1536]{1,0:T(8,128)S(1)}) custom-call(f32[2,256]{1,0:T(2,128)S(1)} %concatenate.9.terms_ref, f32[64,1536]{1,0:T(8,128)S(1)} %get-tuple-element.38.mid_ref, f32[64,384]{1,0:T(8,128)S(1)} %far_part.10.refs_0_, f32[64,384]{1,0:T(8,128)S(1)} %near_part.11.refs_1_, ...), custom_call_target="tpu_custom_call" | custom-call | flops 603979776 | bytes 786432 | tf_op jit(solution)/shard_map/local_part/pallas_call | solution.py:148
  27.6 1.2 %collective-permute-done.8.halo_ref = f32[64,384]{1,0:T(8,128)S(1)} collective-permute-done((f32[64,384]{1,0:T(8,128)S(1)}, f32[64,384]{1,0:T(8,128)S(1)}, u32[]{:S(2)}, u32[]{:S(2)}) %collective-permute-start.8) | collective-permute-done | bytes 98336 | tf_op jit(solution)/shard_map/ppermute | solution.py:244
  29.1 1.2 %collective-permute-start.10 = (f32[64,384]{1,0:T(8,128)S(1)}, f32[64,384]{1,0:T(8,128)S(1)}, u32[]{:S(2)}, u32[]{:S(2)}) collective-permute-start(f32[64,384]{1,0:T(8,128)S(1)} %far_part.11.refs_0_), channel_id=1, source_target_pairs={{0,24},{8,16},{16,8},{24,0},{1,25},{9,17},{17,9},{25,1},{2,26},{10... | collective-permute-start | bytes 294920 | tf_op jit(solution)/shard_map/ppermute | solution.py:244
  30.2 1.7 %local_part.13 = (f32[64,1536]{1,0:T(8,128)S(1)}, f32[64,1536]{1,0:T(8,128)S(1)}) custom-call(f32[2,256]{1,0:T(2,128)S(1)} %concatenate.9.terms_ref, f32[64,1536]{1,0:T(8,128)S(1)} %get-tuple-element.40.mid_ref, f32[64,384]{1,0:T(8,128)S(1)} %far_part.11.refs_0_, f32[64,384]{1,0:T(8,128)S(1)} %near_part.12.refs_1_, ...), custom_call_target="tpu_custom_call" | custom-call | flops 603979776 | bytes 786432 | tf_op jit(solution)/shard_map/local_part/pallas_call | solution.py:148
  32.7 1.2 %collective-permute-done.10.halo_ref = f32[64,384]{1,0:T(8,128)S(1)} collective-permute-done((f32[64,384]{1,0:T(8,128)S(1)}, f32[64,384]{1,0:T(8,128)S(1)}, u32[]{:S(2)}, u32[]{:S(2)}) %collective-permute-start.10) | collective-permute-done | bytes 98336 | tf_op jit(solution)/shard_map/ppermute | solution.py:244
  34.1 1.3 %collective-permute-start.12 = (f32[64,384]{1,0:T(8,128)S(1)}, f32[64,384]{1,0:T(8,128)S(1)}, u32[]{:S(2)}, u32[]{:S(2)}) collective-permute-start(f32[64,384]{1,0:T(8,128)S(1)} %far_part.12.refs_0_), channel_id=1, source_target_pairs={{0,24},{8,16},{16,8},{24,0},{1,25},{9,17},{17,9},{25,1},{2,26},{10... | collective-permute-start | bytes 294920 | tf_op jit(solution)/shard_map/ppermute | solution.py:244
  35.4 1.7 %local_part.14 = (f32[64,1536]{1,0:T(8,128)S(1)}, f32[64,1536]{1,0:T(8,128)S(1)}) custom-call(f32[2,256]{1,0:T(2,128)S(1)} %concatenate.9.terms_ref, f32[64,1536]{1,0:T(8,128)S(1)} %get-tuple-element.42.mid_ref, f32[64,384]{1,0:T(8,128)S(1)} %far_part.12.refs_0_, f32[64,384]{1,0:T(8,128)S(1)} %near_part.13.refs_1_, ...), custom_call_target="tpu_custom_call" | custom-call | flops 603979776 | bytes 786432 | tf_op jit(solution)/shard_map/local_part/pallas_call | solution.py:148
  37.4 0.4 collective-permute-start.15
  37.9 1.1 %collective-permute-done.12.halo_ref = f32[64,384]{1,0:T(8,128)S(1)} collective-permute-done((f32[64,384]{1,0:T(8,128)S(1)}, f32[64,384]{1,0:T(8,128)S(1)}, u32[]{:S(2)}, u32[]{:S(2)}) %collective-permute-start.12) | collective-permute-done | bytes 98336 | tf_op jit(solution)/shard_map/ppermute | solution.py:244
  39.2 1.3 %collective-permute-start.14 = (f32[64,384]{1,0:T(8,128)S(1)}, f32[64,384]{1,0:T(8,128)S(1)}, u32[]{:S(2)}, u32[]{:S(2)}) collective-permute-start(f32[64,384]{1,0:T(8,128)S(1)} %far_part.13.refs_0_), channel_id=1, source_target_pairs={{0,24},{8,16},{16,8},{24,0},{1,25},{9,17},{17,9},{25,1},{2,26},{10... | collective-permute-start | bytes 294920 | tf_op jit(solution)/shard_map/ppermute | solution.py:244
  40.5 1.9 %local_part.15.mid_ref = f32[64,1536]{1,0:T(8,128)S(1)} custom-call(f32[2,256]{1,0:T(2,128)S(1)} %concatenate.9.terms_ref, f32[64,1536]{1,0:T(8,128)S(1)} %get-tuple-element.44.mid_ref, f32[64,384]{1,0:T(8,128)S(1)} %far_part.13.refs_0_, f32[64,384]{1,0:T(8,128)S(1)} %near_part.14.refs_1_, f32[64,1536]{1,0:T(8,128)S(1)} %get-tuple-element.45.refs_2_, ...), custom_call_target="tpu_custom_call" | custom-call | flops 603979776 | bytes 786432 | tf_op jit(solution)/shard_map/local_part/pallas_call | solution.py:148
  42.7 1.4 %collective-permute-done.14.far_ref = f32[64,384]{1,0:T(8,128)S(1)} collective-permute-done((f32[64,384]{1,0:T(8,128)S(1)}, f32[64,384]{1,0:T(8,128)S(1)}, u32[]{:S(2)}, u32[]{:S(2)}) %collective-permute-start.14) | collective-permute-done | bytes 98336 | tf_op jit(solution)/shard_map/ppermute | solution.py:244
  44.5 18.0 %all_to_all.5.parts_ref = f32[8,96,128]{2,1,0:T(8,128)S(1)} all-to-all(f32[8,96,128]{2,1,0:T(8,128)S(1)} %last_part.1), channel_id=1, replica_groups=mesh['narrow'=4,'wide'=8] {'wide'}, dimensions={0} | all-to-all | bytes 786432 | tf_op jit(solution)/shard_map/all_to_all | solution.py:516
  62.5 0.8 gram.1
  63.4 1.6 %collective-permute-done.16.refs_1_ = f32[576,128]{1,0:T(8,128)S(1)} collective-permute-done((f32[576,128]{1,0:T(8,128)S(1)}, f32[576,128]{1,0:T(8,128)S(1)}, u32[]{:S(2)}, u32[]{:S(2)}) %collective-permute-start.16) | collective-permute-done | bytes 294944 | tf_op jit(solution)/shard_map/ppermute | solution.py:274
  65.0 1.5 %collective-permute-start.17 = (f32[144,128]{1,0:T(8,128)S(1)}, f32[144,128]{1,0:T(8,128)S(1)}, u32[]{:S(2)}, u32[]{:S(2)}) collective-permute-start(f32[144,128]{1,0:T(8,128)S(1)} %get-tuple-element.49), channel_id=1, source_target_pairs={{0,16},{1,17},{2,18},{3,19},{4,20},{5,21},{6,22},{7,23},{8,24},{9,... | collective-permute-start | bytes 221192 | tf_op jit(solution)/shard_map/ppermute | solution.py:274
  66.5 1.1 %collective-permute-start.18 = (f32[144,128]{1,0:T(8,128)S(1)}, f32[144,128]{1,0:T(8,128)S(1)}, u32[]{:S(2)}, u32[]{:S(2)}) collective-permute-start(f32[144,128]{1,0:T(8,128)S(1)} %get-tuple-element.50), channel_id=1, source_target_pairs={{0,1},{1,0},{2,3},{3,2},{4,5},{5,4},{6,7},{7,6},{8,9},{9,8},{10,11... | collective-permute-start | bytes 221192 | tf_op jit(solution)/shard_map/ppermute | solution.py:274
  67.6 0.9 collective-permute-start.19
  68.5 0.9 collective-permute-done.17
  69.4 2.3 %collective-permute-done.18 = f32[144,128]{1,0:T(8,128)S(1)} collective-permute-done((f32[144,128]{1,0:T(8,128)S(1)}, f32[144,128]{1,0:T(8,128)S(1)}, u32[]{:S(2)}, u32[]{:S(2)}) %collective-permute-start.18) | collective-permute-done | bytes 73760 | tf_op jit(solution)/shard_map/ppermute | solution.py:274
  71.7 1.2 %collective-permute-done.19 = f32[144,128]{1,0:T(8,128)S(1)} collective-permute-done((f32[144,128]{1,0:T(8,128)S(1)}, f32[144,128]{1,0:T(8,128)S(1)}, u32[]{:S(2)}, u32[]{:S(2)}) %collective-permute-start.19) | collective-permute-done | bytes 73760 | tf_op jit(solution)/shard_map/ppermute | solution.py:274
  72.9 0.5 collective-permute-start.20
  73.3 1.6 %collective-permute-start.21 = (f32[144,128]{1,0:T(8,128)S(1)}, f32[144,128]{1,0:T(8,128)S(1)}, u32[]{:S(2)}, u32[]{:S(2)}) collective-permute-start(f32[144,128]{1,0:T(8,128)S(1)} %add_add_fusion.1), channel_id=1, source_target_pairs={{0,4},{1,5},{2,6},{3,7},{4,0},{5,1},{6,2},{7,3},{8,12},{9,13},{10,... | collective-permute-start | bytes 221192 | tf_op jit(solution)/shard_map/ppermute | solution.py:274
  75.0 2.4 %collective-permute-start.22 = (f32[144,128]{1,0:T(8,128)S(1)}, f32[144,128]{1,0:T(8,128)S(1)}, u32[]{:S(2)}, u32[]{:S(2)}) collective-permute-start(f32[144,128]{1,0:T(8,128)S(1)} %add_add_fusion.1), channel_id=1, source_target_pairs={{0,6},{1,7},{2,4},{3,5},{4,2},{5,3},{6,0},{7,1},{8,14},{9,15},{10,... | collective-permute-start | bytes 221192 | tf_op jit(solution)/shard_map/ppermute | solution.py:274
  77.3 2.7 %collective-permute-done.21 = f32[144,128]{1,0:T(8,128)S(1)} collective-permute-done((f32[144,128]{1,0:T(8,128)S(1)}, f32[144,128]{1,0:T(8,128)S(1)}, u32[]{:S(2)}, u32[]{:S(2)}) %collective-permute-start.21) | collective-permute-done | bytes 73760 | tf_op jit(solution)/shard_map/ppermute | solution.py:274
  80.0 1.2 %collective-permute-done.22 = f32[144,128]{1,0:T(8,128)S(1)} collective-permute-done((f32[144,128]{1,0:T(8,128)S(1)}, f32[144,128]{1,0:T(8,128)S(1)}, u32[]{:S(2)}, u32[]{:S(2)}) %collective-permute-start.22) | collective-permute-done | bytes 73760 | tf_op jit(solution)/shard_map/ppermute | solution.py:274
  81.3 0.6 collective-permute-start.23
  81.9 0.9 %collective-permute-start.24 = (f32[144,128]{1,0:T(8,128)S(1)}, f32[144,128]{1,0:T(8,128)S(1)}, u32[]{:S(2)}, u32[]{:S(2)}) collective-permute-start(f32[144,128]{1,0:T(8,128)S(1)} %add_add_fusion), channel_id=1, source_target_pairs={{0,1},{1,0},{2,3},{3,2},{4,5},{5,4},{6,7},{7,6},{8,9},{9,8},{10,11... | collective-permute-start | bytes 221192 | tf_op jit(solution)/shard_map/ppermute | solution.py:274
  82.8 2.0 %collective-permute-start.25 = (f32[144,128]{1,0:T(8,128)S(1)}, f32[144,128]{1,0:T(8,128)S(1)}, u32[]{:S(2)}, u32[]{:S(2)}) collective-permute-start(f32[144,128]{1,0:T(8,128)S(1)} %add_add_fusion), channel_id=1, source_target_pairs={{0,17},{1,16},{2,19},{3,18},{4,21},{5,20},{6,23},{7,22},{8,25},{9,... | collective-permute-start | bytes 221192 | tf_op jit(solution)/shard_map/ppermute | solution.py:274
  84.8 0.9 collective-permute-done.23
  85.7 0.5 collective-permute-done.24
  86.2 1.8 %collective-permute-done.25 = f32[144,128]{1,0:T(8,128)S(1)} collective-permute-done((f32[144,128]{1,0:T(8,128)S(1)}, f32[144,128]{1,0:T(8,128)S(1)}, u32[]{:S(2)}, u32[]{:S(2)}) %collective-permute-start.25) | collective-permute-done | bytes 73760 | tf_op jit(solution)/shard_map/ppermute | solution.py:274
  88.1 1.6 %collective-permute-done.26.other_ref = f32[576,128]{1,0:T(8,128)S(1)} collective-permute-done((f32[576,128]{1,0:T(8,128)S(1)}, f32[576,128]{1,0:T(8,128)S(1)}, u32[]{:S(2)}, u32[]{:S(2)}) %collective-permute-start.26) | collective-permute-done | bytes 294944 | tf_op jit(solution)/shard_map/ppermute | solution.py:274
  89.7 1.6 %rotate.1 = f32[192,512]{1,0:T(8,128)} custom-call(f32[576,128]{1,0:T(8,128)S(1)} %pad_maximum_fusion.own_ref, f32[576,128]{1,0:T(8,128)S(1)} %collective-permute-done.26.other_ref, f32[192,512]{1,0:T(8,128)S(1)} %get-tuple-element.52.rows_ref), custom_call_target="tpu_custom_call" | custom-call | tf_op jit(solution)/shard_map/rotate/pallas_call | solution.py:496
  (40 shorter events, 6.5 us)
Async XLA Ops:
  2.5 6.3 %collective-permute-start.1 = (f32[64,384]{1,0:T(8,128)S(1)}, f32[64,384]{1,0:T(8,128)S(1)}, u32[]{:S(2)}, u32[]{:S(2)}) collective-permute-start(f32[64,384]{1,0:T(8,128)S(1)} %get-tuple-element.33), channel_id=1, source_target_pairs={{0,8},{8,0},{16,24},{24,16},{1,9},{9,1},{17,25},{25,17},{2,10},{10... | collective-permute-start | bytes 294920 | tf_op jit(solution)/shard_map/ppermute | solution.py:244
  3.0 6.2 %collective-permute-start = (f32[64,384]{1,0:T(8,128)S(1)}, f32[64,384]{1,0:T(8,128)S(1)}, u32[]{:S(2)}, u32[]{:S(2)}) collective-permute-start(f32[64,384]{1,0:T(8,128)S(1)} %get-tuple-element.32), channel_id=1, source_target_pairs={{0,24},{8,16},{16,8},{24,0},{1,25},{9,17},{17,9},{25,1},{2,26},{10... | collective-permute-start | bytes 294920 | tf_op jit(solution)/shard_map/ppermute | solution.py:244
  9.1 3.1 %collective-permute-start.3 = (f32[64,384]{1,0:T(8,128)S(1)}, f32[64,384]{1,0:T(8,128)S(1)}, u32[]{:S(2)}, u32[]{:S(2)}) collective-permute-start(f32[64,384]{1,0:T(8,128)S(1)} %near_part.8.refs_1_), channel_id=1, source_target_pairs={{0,8},{8,0},{16,24},{24,16},{1,9},{9,1},{17,25},{25,17},{2,10},{10... | collective-permute-start | bytes 294920 | tf_op jit(solution)/shard_map/ppermute | solution.py:244
  9.5 4.6 %collective-permute-start.2 = (f32[64,384]{1,0:T(8,128)S(1)}, f32[64,384]{1,0:T(8,128)S(1)}, u32[]{:S(2)}, u32[]{:S(2)}) collective-permute-start(f32[64,384]{1,0:T(8,128)S(1)} %far_part.7.refs_0_), channel_id=1, source_target_pairs={{0,24},{8,16},{16,8},{24,0},{1,25},{9,17},{17,9},{25,1},{2,26},{10... | collective-permute-start | bytes 294920 | tf_op jit(solution)/shard_map/ppermute | solution.py:244
  12.5 4.5 %collective-permute-start.5 = (f32[64,384]{1,0:T(8,128)S(1)}, f32[64,384]{1,0:T(8,128)S(1)}, u32[]{:S(2)}, u32[]{:S(2)}) collective-permute-start(f32[64,384]{1,0:T(8,128)S(1)} %near_part.9.refs_1_), channel_id=1, source_target_pairs={{0,8},{8,0},{16,24},{24,16},{1,9},{9,1},{17,25},{25,17},{2,10},{10... | collective-permute-start | bytes 294920 | tf_op jit(solution)/shard_map/ppermute | solution.py:244
  14.3 4.6 %collective-permute-start.4 = (f32[64,384]{1,0:T(8,128)S(1)}, f32[64,384]{1,0:T(8,128)S(1)}, u32[]{:S(2)}, u32[]{:S(2)}) collective-permute-start(f32[64,384]{1,0:T(8,128)S(1)} %far_part.8.refs_0_), channel_id=1, source_target_pairs={{0,24},{8,16},{16,8},{24,0},{1,25},{9,17},{17,9},{25,1},{2,26},{10... | collective-permute-start | bytes 294920 | tf_op jit(solution)/shard_map/ppermute | solution.py:244
  17.3 4.6 %collective-permute-start.7 = (f32[64,384]{1,0:T(8,128)S(1)}, f32[64,384]{1,0:T(8,128)S(1)}, u32[]{:S(2)}, u32[]{:S(2)}) collective-permute-start(f32[64,384]{1,0:T(8,128)S(1)} %near_part.10.refs_1_), channel_id=1, source_target_pairs={{0,8},{8,0},{16,24},{24,16},{1,9},{9,1},{17,25},{25,17},{2,10},{10... | collective-permute-start | bytes 294920 | tf_op jit(solution)/shard_map/ppermute | solution.py:244
  19.2 4.6 %collective-permute-start.6 = (f32[64,384]{1,0:T(8,128)S(1)}, f32[64,384]{1,0:T(8,128)S(1)}, u32[]{:S(2)}, u32[]{:S(2)}) collective-permute-start(f32[64,384]{1,0:T(8,128)S(1)} %far_part.9.refs_0_), channel_id=1, source_target_pairs={{0,24},{8,16},{16,8},{24,0},{1,25},{9,17},{17,9},{25,1},{2,26},{10... | collective-permute-start | bytes 294920 | tf_op jit(solution)/shard_map/ppermute | solution.py:244
  22.3 4.7 %collective-permute-start.9 = (f32[64,384]{1,0:T(8,128)S(1)}, f32[64,384]{1,0:T(8,128)S(1)}, u32[]{:S(2)}, u32[]{:S(2)}) collective-permute-start(f32[64,384]{1,0:T(8,128)S(1)} %near_part.11.refs_1_), channel_id=1, source_target_pairs={{0,8},{8,0},{16,24},{24,16},{1,9},{9,1},{17,25},{25,17},{2,10},{10... | collective-permute-start | bytes 294920 | tf_op jit(solution)/shard_map/ppermute | solution.py:244
  24.1 4.7 %collective-permute-start.8 = (f32[64,384]{1,0:T(8,128)S(1)}, f32[64,384]{1,0:T(8,128)S(1)}, u32[]{:S(2)}, u32[]{:S(2)}) collective-permute-start(f32[64,384]{1,0:T(8,128)S(1)} %far_part.10.refs_0_), channel_id=1, source_target_pairs={{0,24},{8,16},{16,8},{24,0},{1,25},{9,17},{17,9},{25,1},{2,26},{10... | collective-permute-start | bytes 294920 | tf_op jit(solution)/shard_map/ppermute | solution.py:244
  27.2 4.7 %collective-permute-start.11 = (f32[64,384]{1,0:T(8,128)S(1)}, f32[64,384]{1,0:T(8,128)S(1)}, u32[]{:S(2)}, u32[]{:S(2)}) collective-permute-start(f32[64,384]{1,0:T(8,128)S(1)} %near_part.12.refs_1_), channel_id=1, source_target_pairs={{0,8},{8,0},{16,24},{24,16},{1,9},{9,1},{17,25},{25,17},{2,10},{10... | collective-permute-start | bytes 294920 | tf_op jit(solution)/shard_map/ppermute | solution.py:244
  29.1 4.7 %collective-permute-start.10 = (f32[64,384]{1,0:T(8,128)S(1)}, f32[64,384]{1,0:T(8,128)S(1)}, u32[]{:S(2)}, u32[]{:S(2)}) collective-permute-start(f32[64,384]{1,0:T(8,128)S(1)} %far_part.11.refs_0_), channel_id=1, source_target_pairs={{0,24},{8,16},{16,8},{24,0},{1,25},{9,17},{17,9},{25,1},{2,26},{10... | collective-permute-start | bytes 294920 | tf_op jit(solution)/shard_map/ppermute | solution.py:244
  32.3 4.8 %collective-permute-start.13 = (f32[64,384]{1,0:T(8,128)S(1)}, f32[64,384]{1,0:T(8,128)S(1)}, u32[]{:S(2)}, u32[]{:S(2)}) collective-permute-start(f32[64,384]{1,0:T(8,128)S(1)} %near_part.13.refs_1_), channel_id=1, source_target_pairs={{0,8},{8,0},{16,24},{24,16},{1,9},{9,1},{17,25},{25,17},{2,10},{10... | collective-permute-start | bytes 294920 | tf_op jit(solution)/shard_map/ppermute | solution.py:244
  34.1 4.8 %collective-permute-start.12 = (f32[64,384]{1,0:T(8,128)S(1)}, f32[64,384]{1,0:T(8,128)S(1)}, u32[]{:S(2)}, u32[]{:S(2)}) collective-permute-start(f32[64,384]{1,0:T(8,128)S(1)} %far_part.12.refs_0_), channel_id=1, source_target_pairs={{0,24},{8,16},{16,8},{24,0},{1,25},{9,17},{17,9},{25,1},{2,26},{10... | collective-permute-start | bytes 294920 | tf_op jit(solution)/shard_map/ppermute | solution.py:244
  37.4 5.0 %collective-permute-start.15 = (f32[64,384]{1,0:T(8,128)S(1)}, f32[64,384]{1,0:T(8,128)S(1)}, u32[]{:S(2)}, u32[]{:S(2)}) collective-permute-start(f32[64,384]{1,0:T(8,128)S(1)} %near_part.14.refs_1_), channel_id=1, source_target_pairs={{0,8},{8,0},{16,24},{24,16},{1,9},{9,1},{17,25},{25,17},{2,10},{10... | collective-permute-start | bytes 294920 | tf_op jit(solution)/shard_map/ppermute | solution.py:244
  39.2 4.9 %collective-permute-start.14 = (f32[64,384]{1,0:T(8,128)S(1)}, f32[64,384]{1,0:T(8,128)S(1)}, u32[]{:S(2)}, u32[]{:S(2)}) collective-permute-start(f32[64,384]{1,0:T(8,128)S(1)} %far_part.13.refs_0_), channel_id=1, source_target_pairs={{0,24},{8,16},{16,8},{24,0},{1,25},{9,17},{17,9},{25,1},{2,26},{10... | collective-permute-start | bytes 294920 | tf_op jit(solution)/shard_map/ppermute | solution.py:244
  63.3 1.6 %collective-permute-start.16 = (f32[576,128]{1,0:T(8,128)S(1)}, f32[576,128]{1,0:T(8,128)S(1)}, u32[]{:S(2)}, u32[]{:S(2)}) collective-permute-start(f32[576,128]{1,0:T(8,128)S(1)} %get-tuple-element.47), channel_id=1, source_target_pairs={{0,8},{1,9},{2,10},{3,11},{4,12},{5,13},{6,14},{7,15},{8,0},{9,1},... | collective-permute-start | bytes 884744 | tf_op jit(solution)/shard_map/ppermute | solution.py:274
  65.0 4.4 %collective-permute-start.17 = (f32[144,128]{1,0:T(8,128)S(1)}, f32[144,128]{1,0:T(8,128)S(1)}, u32[]{:S(2)}, u32[]{:S(2)}) collective-permute-start(f32[144,128]{1,0:T(8,128)S(1)} %get-tuple-element.49), channel_id=1, source_target_pairs={{0,16},{1,17},{2,18},{3,19},{4,20},{5,21},{6,22},{7,23},{8,24},{9,... | collective-permute-start | bytes 221192 | tf_op jit(solution)/shard_map/ppermute | solution.py:274
  66.5 5.1 %collective-permute-start.18 = (f32[144,128]{1,0:T(8,128)S(1)}, f32[144,128]{1,0:T(8,128)S(1)}, u32[]{:S(2)}, u32[]{:S(2)}) collective-permute-start(f32[144,128]{1,0:T(8,128)S(1)} %get-tuple-element.50), channel_id=1, source_target_pairs={{0,1},{1,0},{2,3},{3,2},{4,5},{5,4},{6,7},{7,6},{8,9},{9,8},{10,11... | collective-permute-start | bytes 221192 | tf_op jit(solution)/shard_map/ppermute | solution.py:274
  67.6 5.3 %collective-permute-start.19 = (f32[144,128]{1,0:T(8,128)S(1)}, f32[144,128]{1,0:T(8,128)S(1)}, u32[]{:S(2)}, u32[]{:S(2)}) collective-permute-start(f32[144,128]{1,0:T(8,128)S(1)} %get-tuple-element.51), channel_id=1, source_target_pairs={{0,17},{1,16},{2,19},{3,18},{4,21},{5,20},{6,23},{7,22},{8,25},{9,... | collective-permute-start | bytes 221192 | tf_op jit(solution)/shard_map/ppermute | solution.py:274
  72.9 4.5 %collective-permute-start.20 = (f32[144,128]{1,0:T(8,128)S(1)}, f32[144,128]{1,0:T(8,128)S(1)}, u32[]{:S(2)}, u32[]{:S(2)}) collective-permute-start(f32[144,128]{1,0:T(8,128)S(1)} %add_add_fusion.1), channel_id=1, source_target_pairs={{0,2},{1,3},{2,0},{3,1},{4,6},{5,7},{6,4},{7,5},{8,10},{9,11},{10,... | collective-permute-start | bytes 221192 | tf_op jit(solution)/shard_map/ppermute | solution.py:274
  73.3 6.7 %collective-permute-start.21 = (f32[144,128]{1,0:T(8,128)S(1)}, f32[144,128]{1,0:T(8,128)S(1)}, u32[]{:S(2)}, u32[]{:S(2)}) collective-permute-start(f32[144,128]{1,0:T(8,128)S(1)} %add_add_fusion.1), channel_id=1, source_target_pairs={{0,4},{1,5},{2,6},{3,7},{4,0},{5,1},{6,2},{7,3},{8,12},{9,13},{10,... | collective-permute-start | bytes 221192 | tf_op jit(solution)/shard_map/ppermute | solution.py:274
  75.0 6.3 %collective-permute-start.22 = (f32[144,128]{1,0:T(8,128)S(1)}, f32[144,128]{1,0:T(8,128)S(1)}, u32[]{:S(2)}, u32[]{:S(2)}) collective-permute-start(f32[144,128]{1,0:T(8,128)S(1)} %add_add_fusion.1), channel_id=1, source_target_pairs={{0,6},{1,7},{2,4},{3,5},{4,2},{5,3},{6,0},{7,1},{8,14},{9,15},{10,... | collective-permute-start | bytes 221192 | tf_op jit(solution)/shard_map/ppermute | solution.py:274
  81.3 4.4 %collective-permute-start.23 = (f32[144,128]{1,0:T(8,128)S(1)}, f32[144,128]{1,0:T(8,128)S(1)}, u32[]{:S(2)}, u32[]{:S(2)}) collective-permute-start(f32[144,128]{1,0:T(8,128)S(1)} %add_add_fusion), channel_id=1, source_target_pairs={{0,16},{1,17},{2,18},{3,19},{4,20},{5,21},{6,22},{7,23},{8,24},{9,... | collective-permute-start | bytes 221192 | tf_op jit(solution)/shard_map/ppermute | solution.py:274
  81.9 4.4 %collective-permute-start.24 = (f32[144,128]{1,0:T(8,128)S(1)}, f32[144,128]{1,0:T(8,128)S(1)}, u32[]{:S(2)}, u32[]{:S(2)}) collective-permute-start(f32[144,128]{1,0:T(8,128)S(1)} %add_add_fusion), channel_id=1, source_target_pairs={{0,1},{1,0},{2,3},{3,2},{4,5},{5,4},{6,7},{7,6},{8,9},{9,8},{10,11... | collective-permute-start | bytes 221192 | tf_op jit(solution)/shard_map/ppermute | solution.py:274
  82.8 5.3 %collective-permute-start.25 = (f32[144,128]{1,0:T(8,128)S(1)}, f32[144,128]{1,0:T(8,128)S(1)}, u32[]{:S(2)}, u32[]{:S(2)}) collective-permute-start(f32[144,128]{1,0:T(8,128)S(1)} %add_add_fusion), channel_id=1, source_target_pairs={{0,17},{1,16},{2,19},{3,18},{4,21},{5,20},{6,23},{7,22},{8,25},{9,... | collective-permute-start | bytes 221192 | tf_op jit(solution)/shard_map/ppermute | solution.py:274
  88.1 1.6 %collective-permute-start.26 = (f32[576,128]{1,0:T(8,128)S(1)}, f32[576,128]{1,0:T(8,128)S(1)}, u32[]{:S(2)}, u32[]{:S(2)}) collective-permute-start(f32[576,128]{1,0:T(8,128)S(1)} %pad_maximum_fusion.own_ref), channel_id=1, source_target_pairs={{0,8},{1,9},{2,10},{3,11},{4,12},{5,13},{6,14},{7,15},{8,0},{9,1},... | collective-permute-start | bytes 884744 | tf_op jit(solution)/shard_map/ppermute | solution.py:274

commit v2 on v1

--- a/solution.py
+++ b/solution.py
@@ -8,6 +8,7 @@
 from jax.sharding import PartitionSpec as P
 
 REACH = 3
+CROSS_PARTS = 4
 STEPS = 8
 TILE = 128
 VM = pl.BlockSpec(memory_space=pltpu.VMEM)
@@ -32,8 +33,12 @@
     return pltpu.with_memory_space_constraint(x, pltpu.HBM)
 
 
+def odd_place(axis):
+    return lax.rem(lax.axis_index(axis), 2) == 1
+
+
 def odd_device():
-    return lax.rem(lax.axis_index("narrow"), 2) == 1
+    return odd_place("narrow")
 
 
 def dot(a, b, dims):
@@ -46,58 +51,72 @@
     return upper[:rows] + (upper[rows:] + dot(a_hi, b_lo, dims))
 
 
-def spread_kernel(total_blocks, columns_hbm, vectors_hbm, blocks_hbm, far_ref, near_ref, vectors_ref, hi_ref, lo_ref, held, columns_ref, sems, row_sems):
+def cross_at(row, place):
+    return sum(REACH - r for r in range(row)) + place + REACH - row
+
+
+def spread_kernel(total_blocks, columns_hbm, vectors_hbm, blocks_hbm, far_ref, near_ref, vectors_ref, part_ref, hi_ref, lo_ref, held, cross_ref, columns_ref, sem, vector_sems, row_sems):
     rows, slots, size, _ = blocks_hbm.shape
     edge = far_ref.shape[1]
-    begin = vectors_hbm.shape[1] - edge
     odd = odd_device()
-
-    def edge_at(at):
-        return vectors_hbm.at[:, pl.ds(pl.multiple_of(at, size), edge)]
-
-    small = [
-        (columns_hbm, columns_ref),
-        (edge_at(jnp.where(odd, begin, 0)), far_ref),
-        (edge_at(jnp.where(odd, 0, begin)), near_ref),
-        (vectors_hbm, vectors_ref),
-    ]
-    small = [pltpu.make_async_copy(here, there, sems.at[k]) for k, (here, there) in enumerate(small)]
-    large = [pltpu.make_async_copy(blocks_hbm.at[row], held.at[row], row_sems.at[row]) for row in range(rows)]
-    for copy in small[:1] + large + small[1:]:
+    source = [jnp.where(odd, rows - 1 - row, row) for row in range(rows)]
+    copies = [pltpu.make_async_copy(columns_hbm, columns_ref, sem)]
+    for row in range(rows):
+        here = vectors_hbm.at[:, pl.ds(pl.multiple_of(source[row] * size, size), size)]
+        copies.append(pltpu.make_async_copy(here, vectors_ref.at[:, pl.ds(row * size, size)], vector_sems.at[row]))
+    large = [pltpu.make_async_copy(blocks_hbm.at[source[row]], held.at[row], row_sems.at[row]) for row in range(rows)]
+    for copy in copies + large:
         copy.start()
     hi_ref[...] = jnp.zeros_like(hi_ref)
     lo_ref[...] = jnp.zeros_like(lo_ref)
+    cross_ref[...] = jnp.zeros_like(cross_ref)
     first = lax.axis_index("narrow") * rows
-    small[0].wait()
+    copies[0].wait()
     for row in range(rows):
         large[row].wait()
         pair, half = divmod(row, 2)
         here = slice(half * size, half * size + size)
         for slot in range(slots):
-            place = columns_ref[slot, row] - first + REACH
-            place = jnp.where(place < 0, place + total_blocks, place)
-            place = jnp.where(place >= total_blocks, place - total_blocks, place) - 2 * pair
+            offset = columns_ref[slot, source[row]] - (first + source[row])
+            offset = jnp.where(offset > REACH, offset - total_blocks, offset)
+            offset = jnp.where(offset < -REACH, offset + total_blocks, offset)
+            offset = jnp.where(odd, -offset, offset)
             hi, lo = split(held[row, slot])
-            there = pl.ds(pl.multiple_of(place * size, size), size)
+            there = pl.ds(pl.multiple_of((half + offset + REACH) * size, size), size)
             hi_ref[pair, here, there] = hi
             lo_ref[pair, here, there] = lo
-    for copy in small[1:]:
+            if row < REACH:
+
+                @pl.when(row + offset < 0)
+                def _():
+                    at = pl.multiple_of(cross_at(row, row + offset) * size, size)
+                    cross_ref[pl.ds(at, size), :] = held[row, slot]
+
+    count = part_ref.shape[0]
+    part_ref[...] = cross_ref[pl.ds(pl.multiple_of(lax.rem(lax.axis_index("wide"), CROSS_PARTS) * count, 8), count), :]
+    for copy in copies[1:]:
         copy.wait()
+    far_ref[...] = vectors_ref[:, :edge]
+    near_ref[...] = vectors_ref[:, -edge:]
 
 
 def spread_part(columns, vectors, blocks, total_blocks):
     rows, slots, size, _ = blocks.shape
     spread = jax.ShapeDtypeStruct((rows // 2, 2 * size, (2 * REACH + 2) * size), BF16)
     edge = jax.ShapeDtypeStruct((vectors.shape[0], REACH * size), F32)
+    crossing = REACH * (REACH + 1) // 2 * size
+    cross = jax.ShapeDtypeStruct((crossing // CROSS_PARTS, size), F32)
     return pl.pallas_call(
         functools.partial(spread_kernel, total_blocks),
         in_specs=[HBM, HBM, HBM],
-        out_specs=[VM] * 5,
-        out_shape=[edge, edge, jax.ShapeDtypeStruct(vectors.shape, F32), spread, spread],
+        out_specs=[VM] * 6,
+        out_shape=[edge, edge, jax.ShapeDtypeStruct(vectors.shape, F32), cross, spread, spread],
         scratch_shapes=[
             pltpu.VMEM(blocks.shape, F32),
+            pltpu.VMEM((crossing, size), F32),
             pltpu.SMEM((slots, rows), jnp.int32),
-            pltpu.SemaphoreType.DMA((4,)),
+            pltpu.SemaphoreType.DMA,
+            pltpu.SemaphoreType.DMA((rows,)),
             pltpu.SemaphoreType.DMA((rows,)),
         ],
         compiler_params=params(),
@@ -105,111 +124,192 @@
     )(in_hbm(columns.T), in_hbm(vectors), in_hbm(blocks))
 
 
-def local_sum(pair, hi, both, hi_ref, lo_ref):
-    pairs, width, window = hi_ref.shape
-    size = width // 2
-    start = 2 * pair - REACH
-    begin, end = max(start, 0), min(start + window // size, 2 * pairs)
-    there = slice(begin * size, end * size)
-    inside = slice((begin - start) * size, (end - start) * size)
-    return dot_split(hi[:, there], both[:, there], hi_ref[pair, :, inside], lo_ref[pair, :, inside], NT)
-
-
-def local_kernel(first_step, terms_ref, mid_ref, *refs):
-    if first_step:
-        hi_ref, lo_ref, out_ref = refs
-        current = mid_ref[...]
-    else:
-        far_ref, near_ref, previous_ref, hi_ref, lo_ref, out_ref, *full_ref = refs
-        edge = far_ref.shape[1]
-        odd = odd_device()
-        left = jnp.where(odd, near_ref[...], far_ref[...])
-        right = jnp.where(odd, far_ref[...], near_ref[...])
-        current = jnp.concatenate([left, mid_ref[:, edge:-edge], right], axis=1)
-        if full_ref:
-            full_ref[0][...] = current
+class Strip:
+    def __init__(self, values, at, size):
+        self.hi, lo = split(values)
+        self.both = jnp.concatenate([self.hi, lo], axis=0)
+        self.at, self.size = at, size
+
+    def band(self, operator, pair, begin, end):
+        hi_ref, lo_ref = operator
+        size, start = self.size, 2 * pair - REACH
+        there = slice((begin - self.at) * size, (end - self.at) * size)
+        inside = slice((begin - start) * size, (end - start) * size)
+        return dot_split(self.hi[:, there], self.both[:, there], hi_ref[pair, :, inside], lo_ref[pair, :, inside], NT)
+
+
+def reversed_blocks(edge, size):
+    return [edge[:, k * size : (k + 1) * size] for k in reversed(range(edge.shape[1] // size))]
+
+
+def far_sum(operator, halo, size):
+    strip = Strip(jnp.concatenate(reversed_blocks(halo, size), axis=1), -REACH, size)
+    outer = strip.band(operator, 0, -REACH, 0)
+    inner = strip.band(operator, 1, -1, 0)
+    return jnp.concatenate([outer, inner[:, :size]], axis=1)
+
+
+def near_sum(operator, halo, size):
+    pairs = operator[0].shape[0]
+    strip = Strip(jnp.concatenate(reversed_blocks(halo, size), axis=1), 2 * pairs, size)
+    outer = strip.band(operator, pairs - 1, 2 * pairs, 2 * pairs + REACH)
+    inner = strip.band(operator, pairs - 2, 2 * pairs, 2 * pairs + 1)
+    return jnp.concatenate([inner[:, size:], outer], axis=1)
+
+
+def own_sum(operator, strip, pair, lowest=0):
+    pairs = operator[0].shape[0]
+    return strip.band(operator, pair, max(2 * pair - REACH, lowest), min(2 * pair + REACH + 2, 2 * pairs))
+
+
+def first_kernel(terms_ref, vectors_ref, hi_ref, lo_ref, out_ref):
     pairs, width, _ = hi_ref.shape
     scale, diag = terms_ref[0:1, :], terms_ref[1:2, :]
-    hi, lo = split(current)
-    both = jnp.concatenate([hi, lo], axis=0)
+    strip = Strip(vectors_ref[...], 0, width // 2)
     for pair in range(pairs):
         here = slice(pair * width, pair * width + width)
-        total = scale * local_sum(pair, hi, both, hi_ref, lo_ref) + diag * current[:, here]
-        out_ref[:, here] = 0.5 * total if first_step else total - previous_ref[:, here]
-
-
-def local_part(terms, state, previous, operator, last):
-    mid = state[0]
-    shape = jax.ShapeDtypeStruct(mid.shape, F32)
-    width = operator[0].shape[1]
-    first_step = previous is None
-    operands = (terms, *state, *(() if first_step else (previous,)), *operator)
-    outs = 1 if first_step or last else 2
-    return pl.pallas_call(
-        functools.partial(local_kernel, first_step),
-        in_specs=[VM] * len(operands),
-        out_specs=[VM] * outs,
-        out_shape=[shape] * outs,
-        compiler_params=params(),
-        cost_estimate=pl.CostEstimate(flops=24 * mid.size * width, bytes_accessed=8 * mid.size, transcendentals=0),
-        name="local_part",
-    )(*operands)
-
-
-def edge_sum(factor, at_right, terms_ref, mid_ref, halo_ref, hi_ref, lo_ref):
-    pairs, width, window = hi_ref.shape
-    size = width // 2
-    edge = REACH * size
-    hi, lo = split(halo_ref[...])
-    both = jnp.concatenate([hi, lo], axis=0)
-
-    def reach_into(pair, length, hi, both):
-        inside = pl.ds(pl.multiple_of(jnp.where(at_right, window - length, 0), size), length)
-        return dot_split(hi, both, hi_ref[pair, :, inside], lo_ref[pair, :, inside], NT)
-
-    outer = reach_into(jnp.where(at_right, pairs - 1, 0), edge, hi, both)
-    close_hi = jnp.where(at_right, hi[:, :size], hi[:, -size:])
-    close_both = jnp.where(at_right, both[:, :size], both[:, -size:])
-    inner = reach_into(jnp.where(at_right, pairs - 2, 1), size, close_hi, close_both)
-    added = jnp.where(
-        at_right,
-        jnp.concatenate([inner[:, size:], outer], axis=1),
-        jnp.concatenate([outer, inner[:, :size]], axis=1),
-    )
-    here = pl.ds(pl.multiple_of(jnp.where(at_right, mid_ref.shape[1] - edge, 0), size), edge)
-    return mid_ref[:, here] + (factor * terms_ref[0:1, 0:1]) * added
-
-
-def edge_kernel(factor, far, terms_ref, mid_ref, halo_ref, hi_ref, lo_ref, out_ref):
-    at_right = odd_device() if far else jnp.logical_not(odd_device())
-    out_ref[...] = edge_sum(factor, at_right, terms_ref, mid_ref, halo_ref, hi_ref, lo_ref)
-
-
-def edge_part(factor, far, terms, mid, halo, operator):
+        total = scale * own_sum((hi_ref, lo_ref), strip, pair) + diag * vectors_ref[:, here]
+        out_ref[:, here] = 0.5 * total
+
+
+def local_kernel(first_pair, terms_ref, far_ref, mid_ref, near_ref, far_before_ref, mid_before_ref, near_before_ref, hi_ref, lo_ref, out_ref, *full_ref):
+    pairs, width, _ = hi_ref.shape
+    edge, start = near_ref.shape[1], far_ref.shape[1]
+    scale, diag = terms_ref[0:1, :], terms_ref[1:2, :]
+    current = jnp.concatenate([far_ref[...], mid_ref[:, start:-edge], near_ref[...]], axis=1)
+    before = jnp.concatenate([far_before_ref[...], mid_before_ref[:, edge:-edge], near_before_ref[...]], axis=1)
+    if full_ref:
+        full_ref[0][...] = current
+    strip = Strip(current, 0, width // 2)
+    for pair in range(first_pair, pairs):
+        here = slice(pair * width, pair * width + width)
+        total = scale * own_sum((hi_ref, lo_ref), strip, pair) + diag * current[:, here]
+        out_ref[:, here] = total - before[:, here]
+
+
+def second_kernel(terms_ref, mid_ref, near_ref, before_ref, hi_ref, lo_ref, out_ref):
+    pairs, width, _ = hi_ref.shape
+    edge = near_ref.shape[1]
+    scale, diag = terms_ref[0:1, :], terms_ref[1:2, :]
+    current = jnp.concatenate([mid_ref[:, edge:-edge], near_ref[...]], axis=1)
+    padded = jnp.concatenate([jnp.zeros(near_ref.shape, F32), current], axis=1)
+    strip = Strip(current, REACH, width // 2)
+    for pair in range(pairs):
+        here = slice(pair * width, pair * width + width)
+        total = scale * own_sum((hi_ref, lo_ref), strip, pair, REACH) + diag * padded[:, here]
+        out_ref[:, here] = total - before_ref[:, here]
+
+
+def step_call(kernel, name, operands, operator, outs):
+    size = operands[1].size
     width = operator[0].shape[1]
     return pl.pallas_call(
-        functools.partial(edge_kernel, factor, far),
-        in_specs=[VM] * 5,
-        out_specs=VM,
-        out_shape=jax.ShapeDtypeStruct(halo.shape, F32),
+        kernel,
+        in_specs=[VM] * (len(operands) + 2),
+        out_specs=[VM] * len(outs),
+        out_shape=[jax.ShapeDtypeStruct(shape, F32) for shape in outs],
         compiler_params=params(),
-        cost_estimate=pl.CostEstimate(flops=12 * halo.size * width, bytes_accessed=8 * halo.size, transcendentals=0),
-        name="far_part" if far else "near_part",
-    )(terms, mid, halo, *operator)
+        cost_estimate=pl.CostEstimate(flops=24 * size * width, bytes_accessed=8 * size, transcendentals=0),
+        name=name,
+    )(*operands, *operator)
+
+
+def near_kernel(factor, terms_ref, mid_ref, halo_ref, hi_ref, lo_ref, out_ref):
+    size, edge = hi_ref.shape[1] // 2, halo_ref.shape[1]
+    scale = factor * terms_ref[0:1, 0:1]
+    out_ref[...] = mid_ref[:, -edge:] + scale * near_sum((hi_ref, lo_ref), halo_ref[...], size)
+
+
+def edge_ahead(operator, scale, diag, far, before, size):
+    strip = Strip(far, 0, size)
+    outer = strip.band(operator, 0, 0, REACH + 2)
+    inner = strip.band(operator, 1, 0, 2 * REACH)
+    total = jnp.concatenate([outer, inner[:, :size]], axis=1)
+    return scale * total + diag * far[:, : total.shape[1]] - before
+
+
+def far_kernel(terms_ref, mid_ref, halo_ref, hi_ref, lo_ref, far_ref):
+    size, edge = hi_ref.shape[1] // 2, halo_ref.shape[1]
+    far_ref[...] = mid_ref[:, :edge] + 0.5 * terms_ref[0:1, 0:1] * far_sum((hi_ref, lo_ref), halo_ref[...], size)
+
+
+def turn_one_kernel(terms_ref, mid_ref, halo_ref, before_ref, hi_ref, lo_ref, far_ref, send_ref):
+    operator = (hi_ref, lo_ref)
+    size, edge = hi_ref.shape[1] // 2, halo_ref.shape[1]
+    scale, diag = terms_ref[0:1, 0:1], terms_ref[1:2, 0:1]
+    edge_rows = mid_ref[:, :edge] + scale * far_sum(operator, halo_ref[...], size)
+    far = jnp.concatenate([edge_rows, mid_ref[:, edge : 2 * edge]], axis=1)
+    far_ref[...] = far
+    send_ref[0] = edge_rows
+    send_ref[1] = edge_ahead(operator, scale, diag, far, before_ref[...], size)
+
+
+def turn(terms_ref, mid_ref, sent_ref, got_ref, cross_hi_ref, cross_lo_ref, operator):
+    size, edge = operator[0].shape[1] // 2, sent_ref.shape[2]
+    scale, diag = terms_ref[0:1, 0:1], terms_ref[1:2, 0:1]
+    between = sent_ref[1] + scale * far_sum(operator, got_ref[0], size)
+    def cross(ref, row):
+        rows = [slice(at * size, (at + 1) * size) for at in (cross_at(row, -1 - place) for place in range(REACH - row))]
+        return jnp.concatenate([ref[here, :] for here in rows], axis=1)
+
+    own = Strip(sent_ref[0], 0, size)
+    pieces = []
+    for row in range(REACH):
+        there = slice(0, (REACH - row) * size)
+        hi, lo = cross(cross_hi_ref, row), cross(cross_lo_ref, row)
+        pieces.append(dot_split(own.hi[:, there], own.both[:, there], hi, lo, NT))
+    beyond = got_ref[1] + scale * jnp.concatenate(pieces, axis=1)
+    strip = Strip(jnp.concatenate(reversed_blocks(beyond, size) + [between], axis=1), -REACH, size)
+    total = [strip.band(operator, pair, 2 * pair - REACH, REACH) for pair in range(REACH)]
+    known = jnp.concatenate([diag * between, jnp.zeros_like(between)], axis=1)
+    return between, mid_ref[:, : 2 * edge] + scale * jnp.concatenate(total, axis=1) + known
+
+
+def cross_kernel(mine_ref, one_ref, two_ref, hi_ref, lo_ref):
+    rows = mine_ref.shape[0]
+    place = lax.rem(lax.axis_index("wide"), CROSS_PARTS)
+    for d, part in enumerate([mine_ref[...], one_ref[...], two_ref[:rows, :], two_ref[rows:, :]]):
+        here = chunk_at(place, d, CROSS_PARTS, rows)
+        hi, lo = split(part)
+        hi_ref[here, :] = hi
+        lo_ref[here, :] = lo
+
+
+def cross_part(mine):
+    one = wide_swap(mine, 1)
+    two = wide_swap(jnp.concatenate([mine, one]), 2)
+    rows, width = mine.shape
+    return pl.pallas_call(
+        cross_kernel,
+        in_specs=[VM] * 3,
+        out_specs=[VM] * 2,
+        out_shape=[jax.ShapeDtypeStruct((CROSS_PARTS * rows, width), BF16)] * 2,
+        compiler_params=params(),
+        name="cross_part",
+    )(mine, one, two)
+
+
+def turn_two_kernel(terms_ref, mid_ref, sent_ref, got_ref, cross_hi_ref, cross_lo_ref, hi_ref, lo_ref, between_ref, far_ref, send_ref):
+    operator = (hi_ref, lo_ref)
+    size, edge = hi_ref.shape[1] // 2, between_ref.shape[1]
+    between, far = turn(terms_ref, mid_ref, sent_ref, got_ref, cross_hi_ref, cross_lo_ref, operator)
+    between_ref[...] = between
+    far_ref[...] = far
+    send_ref[0] = far[:, :edge]
+    send_ref[1] = edge_ahead(operator, terms_ref[0:1, 0:1], terms_ref[1:2, 0:1], far, between, size)
 
 
 def packs(count, own):
     return own % TILE == TILE // 2 and own > TILE and count % 16 == 0
 
 
-def last_kernel(parts, terms_ref, mid_ref, far_ref, near_ref, hi_ref, lo_ref, out_ref):
-    odd = odd_device()
-    far = edge_sum(1.0, odd, terms_ref, mid_ref, far_ref, hi_ref, lo_ref)
-    near = near_ref[...]
-    edge = far.shape[1]
-    left, right = jnp.where(odd, near, far), jnp.where(odd, far, near)
-    whole = jnp.concatenate([left, mid_ref[:, edge:-edge], right], axis=1)
-    if out_ref.ndim == 2:
+def last_kernel(parts, terms_ref, mid_ref, sent_ref, got_ref, cross_hi_ref, cross_lo_ref, near_ref, hi_ref, lo_ref, out_ref):
+    size = hi_ref.shape[1] // 2
+    _, far = turn(terms_ref, mid_ref, sent_ref, got_ref, cross_hi_ref, cross_lo_ref, (hi_ref, lo_ref))
+    whole = jnp.concatenate([far, mid_ref[:, far.shape[1] : -near_ref.shape[1]], near_ref[...]], axis=1)
+    mirrored = jnp.concatenate(reversed_blocks(whole, size), axis=1)
+    whole = jnp.where(odd_device(), mirrored, whole)
+    if len(out_ref.shape) == 2:
         out_ref[...] = whole
         return
     count, own, half = whole.shape[0], whole.shape[1] // parts, TILE // 2
@@ -224,45 +324,65 @@
         out_ref[part, at:, :] = jnp.concatenate([tails[: count // 2], tails[count // 2 :]], axis=1)
 
 
-def last_part(terms, mid, far, near, operator, parts):
-    count, length = mid.shape
-    shape = (parts, count * length // parts // TILE, TILE) if packs(count, length // parts) else mid.shape
-    return pl.pallas_call(
-        functools.partial(last_kernel, parts),
-        in_specs=[VM] * 6,
-        out_specs=VM,
-        out_shape=jax.ShapeDtypeStruct(shape, F32),
-        compiler_params=params(),
-        name="last_part",
-    )(terms, mid, far, near, *operator)
-
-
-def exchange(far, near):
+def far_swap(x):
     size = lax.axis_size("narrow")
-    far_pairs = [(i, (i + 1) % size if i % 2 else (i - 1) % size) for i in range(size)]
-    near_pairs = [(i, i ^ 1) for i in range(size)]
-    return lax.ppermute(far, "narrow", far_pairs), lax.ppermute(near, "narrow", near_pairs)
+    return lax.ppermute(x, "narrow", [(i, (i + 1) % size if i % 2 else (i - 1) % size) for i in range(size)])
+
+
+def wide_swap(x, mask):
+    return lax.ppermute(x, "wide", [(i, i ^ mask) for i in range(lax.axis_size("wide"))])
+
+
+def near_swap(x):
+    return lax.ppermute(x, "narrow", [(i, i ^ 1) for i in range(lax.axis_size("narrow"))])
 
 
 def filtered_parts(vectors, blocks, columns, lower_bound, upper_bound):
-    total_blocks = blocks.shape[0] * lax.axis_size("narrow")
-    width = 2 * blocks.shape[2]
+    size = blocks.shape[2]
+    width, edge, parts = 2 * size, REACH * size, lax.axis_size("wide")
+    count, length = vectors.shape
     half_width = (upper_bound - lower_bound) * 0.5
     scale = 2.0 / half_width
     diag = scale * (1.0 - (upper_bound + lower_bound) * 0.5)
     terms = jnp.concatenate([jnp.broadcast_to(scale, (1, width)), jnp.broadcast_to(diag, (1, width))])
-    far, near, vectors, *operator = spread_part(columns, vectors, blocks, total_blocks)
-    state, previous = (vectors,), None
-    for step in range(STEPS):
-        far_halo, near_halo = exchange(far, near)
-        mid, *full = local_part(terms, state, previous, operator, step == STEPS - 1)
-        previous = full[0] if full else vectors
-        factor = 0.5 if step == 0 else 1.0
-        near = edge_part(factor, False, terms, mid, near_halo, operator)
-        if step < STEPS - 1:
-            far = edge_part(factor, True, terms, mid, far_halo, operator)
-        state = (mid, far, near)
-    return last_part(terms, mid, far_halo, near, operator, lax.axis_size("wide"))
+    total_blocks = blocks.shape[0] * lax.axis_size("narrow")
+    far, near, vectors, cross, *operator = spread_part(columns, vectors, blocks, total_blocks)
+    whole, side, double = (count, length), (count, edge), (2, count, edge)
+
+    def near_part(factor, mid, halo):
+        kernel = functools.partial(near_kernel, factor)
+        return step_call(kernel, "near_part", (terms, mid, halo), operator, [side])[0]
+
+    def local_part(first_pair, outs):
+        kernel = functools.partial(local_kernel, first_pair)
+        return step_call(kernel, "local_part", (terms, far, mid, near, *before), operator, [whole] * outs)
+
+    halo, near_halo = far_swap(far), near_swap(near)
+    cross = cross_part(far_swap(cross))
+    (mid,) = step_call(first_kernel, "first_part", (terms, vectors), operator, [whole])
+    before = (far, vectors, near)
+    near = near_part(0.5, mid, near_halo)
+    (far,) = step_call(far_kernel, "far_part", (terms, mid, halo), operator, [side])
+    halo, near_halo = far_swap(far), near_swap(near)
+    next_mid, _ = local_part(0, 2)
+    before = (far, mid, near)
+    mid, near = next_mid, near_part(1.0, next_mid, near_halo)
+    far, send = step_call(turn_one_kernel, "turn_one", (terms, mid, halo, far), operator, [(count, 2 * edge), double])
+    for step in range(2, STEPS, 2):
+        got, near_halo = far_swap(send), near_swap(near)
+        mid, full = local_part(1, 2)
+        near = near_part(1.0, mid, near_halo)
+        near_halo = near_swap(near)
+        (next_mid,) = step_call(second_kernel, "second_part", (terms, mid, near, full), operator, [whole])
+        next_near = near_part(1.0, next_mid, near_halo)
+        operands = (terms, next_mid, send, got, *cross)
+        if step < STEPS - 2:
+            outs = [side, (count, 2 * edge), double]
+            between, far, send = step_call(turn_two_kernel, "turn_two", operands, operator, outs)
+            before = (between, mid, near)
+        mid, near = next_mid, next_near
+    shape = (parts, count * length // parts // TILE, TILE) if packs(count, length // parts) else whole
+    return step_call(functools.partial(last_kernel, parts), "last_part", (*operands, near), operator, [shape])[0]
 
 
 def pair_perm(mask):
@@ -338,8 +458,7 @@
 
 def fan(parts, bits):
     members = masks(bits)
-    got = {d: swap(parts[d], members[d]) for d in reversed(range(1, len(members)))}
-    return [parts[0]] + [got[d] for d in range(1, len(members))]
+    return [parts[0]] + [swap(parts[d], members[d]) for d in range(1, len(members))]
 
 
 def all_sum(halves):

time: 91.7 us -> 89.2 us (0.973)
  waiting for transfers between devices: 23.5 us -> 20 us
  Pallas kernels: 23.4 us -> 25.4 us
    ppermute x16, waiting for transfers between devices: 8.91 us -> 5.52 us  [the longest x6 4.35 us: far_swap(): lax.ppermute(x, 'narrow', [(i, (i + 1) % size if i % 2 else (i - 1) % siz...]
    pallas_call x24 -> x22, Pallas kernels: 18.4 us -> 20.1 us  [the longest x21 20.1 us: step_call(): pl.pallas_call(kernel, in_specs=[VM] * (len(operands) + 2), out_specs=[VM...]
  transfers between devices with their start and end apart: 27 -> 27, of which waited for: 17 -> 13; matrix products, arithmetic and copies ran while one was open for 0% -> 0% of each run, Pallas kernels for 20% -> 21%
where the time goes in v2:
time: 89.2 us; the launch traced here: 89 us
  Pallas kernels  25.4 us (28%)
  starting transfers between devices  24.5 us (27%)
  waiting for transfers between devices  20 us (22%)
  blocking collectives  17.1 us (19%)
  between operations  1.79 us (2%)
    pallas_call x21, Pallas kernels, step_call(): pl.pallas_call(kernel, in_specs=[VM] * (len(operands) + 2), out_specs=[VM...  20.1 us
    all_to_all x1, blocking collectives, regroup(): lax.all_to_all(parts, 'wide', split_axis=0, concat_axis=0, tiled=True)  17.1 us
    ppermute x11, waiting for transfers between devices, swap(): return lax.ppermute(x, ('narrow', 'wide'), pair_perm(mask))  14.5 us
    ppermute x11, starting transfers between devices, swap(): return lax.ppermute(x, ('narrow', 'wide'), pair_perm(mask))  11.7 us
    ppermute x6, starting transfers between devices, far_swap(): lax.ppermute(x, 'narrow', [(i, (i + 1) % size if i % 2 else (i - 1) % siz...  5.9 us
    ppermute x6, waiting for transfers between devices, far_swap(): lax.ppermute(x, 'narrow', [(i, (i + 1) % size if i % 2 else (i - 1) % siz...  4.35 us
    ppermute x8, starting transfers between devices, near_swap(): lax.ppermute(x, 'narrow', [(i, i ^ 1) for i in range(lax.axis_size('narro...  3.73 us
    ppermute x2, starting transfers between devices, wide_swap(): lax.ppermute(x, 'wide', [(i, i ^ mask) for i in range(lax.axis_size('wide...  3.16 us
  transfers between devices with their start and end apart: 27, of which 13 were waited for; matrix products, arithmetic and copies ran while one was open for 0% of the time, Pallas kernels for 21%

profile of v2, /device:TPU:0, one launch (start us, length us, event | category | flops | bytes accessed | tf_op | source)
XLA Modules:
  0.0 89.0 jit_solution(15950689471337343187)
XLA Ops:
  0.0 2.8 %spread_part.1 = (f32[64,384]{1,0:T(8,128)S(1)}, f32[64,384]{1,0:T(8,128)S(1)}, f32[64,1536]{1,0:T(8,128)S(1)}, f32[192,128]{1,0:T(8,128)S(1)}, bf16[6,256,1024]...) custom-call(s32[5,12]{1,0:T(8,128)} %bitcast.3, f32[64,1536]{1,0:T(8,128)} %vectors_hbm.1, f32[12,5,128,128]{3,2,1,0:T(8,128)} %blocks_hbm.1), custom_call_target="tpu_custom_call" | custom-call | tf_op jit(solution)/shard_map/spread_part/pallas_call | solution.py:109
  2.8 0.5 collective-permute-start.1
  3.3 2.6 %collective-permute-start = (f32[64,384]{1,0:T(8,128)S(1)}, f32[64,384]{1,0:T(8,128)S(1)}, u32[]{:S(2)}, u32[]{:S(2)}) collective-permute-start(f32[64,384]{1,0:T(8,128)S(1)} %get-tuple-element.38.far_before_ref), channel_id=1, source_target_pairs={{0,24},{8,16},{16,8},{24,0},{1,25},{9,17},{17,9},{25,1},{2,26},{10... | collective-permute-start | bytes 294920 | tf_op jit(solution)/shard_map/ppermute | solution.py:329
  7.4 1.7 %first_part.1.mid_ref.mid_before_ref = f32[64,1536]{1,0:T(8,128)S(1)} custom-call(f32[2,256]{1,0:T(2,128)S(1)} %concatenate.12.terms_ref, f32[64,1536]{1,0:T(8,128)S(1)} %get-tuple-element.35.vectors_ref.mid_before_ref, bf16[6,256,1024]{2,1,0:T(8,128)(2,1)S(1)} %get-tuple-element.36.hi_ref, bf16[6,256,1024]{2,1,0:T(8,128)(2,1)S(1)} %get-tuple-element.37.lo_ref), custom_call_target="tpu_custom_call" | custom-call | flops 603979776 | bytes 786432 | tf_op jit(solution)/shard_map/first_part/pallas_call | solution.py:206
  9.9 1.8 %collective-permute-start.2 = (f32[64,384]{1,0:T(8,128)S(1)}, f32[64,384]{1,0:T(8,128)S(1)}, u32[]{:S(2)}, u32[]{:S(2)}) collective-permute-start(f32[64,384]{1,0:T(8,128)S(1)} %far_part.1.far_ref.before_ref.far_before_ref), channel_id=1, source_target_pairs={{0,24},{8,16},{16,8},{24,0},{1,25},{9,17},{17,9},{25,1},{2,26},{10... | collective-permute-start | bytes 294920 | tf_op jit(solution)/shard_map/ppermute | solution.py:329
  11.6 1.5 %collective-permute-start.7 = (f32[192,128]{1,0:T(8,128)S(1)}, f32[192,128]{1,0:T(8,128)S(1)}, u32[]{:S(2)}, u32[]{:S(2)}) collective-permute-start(f32[192,128]{1,0:T(8,128)S(1)} %collective-permute-done.6.mine_ref), channel_id=1, source_target_pairs={{0,1},{1,0},{2,3},{3,2},{4,5},{5,4},{6,7},{7,6},{8,9},{9,8},{10,11... | collective-permute-start | bytes 294920 | tf_op jit(solution)/shard_map/ppermute | solution.py:333
  13.2 2.3 %local_part.4 = (f32[64,1536]{1,0:T(8,128)S(1)}, f32[64,1536]{1,0:T(8,128)}) custom-call(f32[2,256]{1,0:T(2,128)S(1)} %concatenate.12.terms_ref, f32[64,384]{1,0:T(8,128)S(1)} %far_part.1.far_ref.before_ref.far_before_ref, f32[64,1536]{1,0:T(8,128)S(1)} %first_part.1.mid_ref.mid_before_ref, f32[64,384]{1,0:T(8,128)S(1)} %near_part.8.near_ref.near_before_ref, ...), custom_call_target="tpu_custom_call" | custom-call | flops 150994944 | bytes 196608 | tf_op jit(solution)/shard_map/local_part/pallas_call | solution.py:206
  16.0 0.8 turn_one.1
  16.7 1.0 %collective-permute-start.5 = (f32[2,64,384]{2,1,0:T(8,128)S(1)}, f32[2,64,384]{2,1,0:T(8,128)S(1)}, u32[]{:S(2)}, u32[]{:S(2)}) collective-permute-start(f32[2,64,384]{2,1,0:T(8,128)S(1)} %get-tuple-element.44.sent_ref), channel_id=1, source_target_pairs={{0,24},{8,16},{16,8},{24,0},{1,25},{9,17},{17,9},{25,1},{2,26},{10... | collective-permute-start | bytes 589832 | tf_op jit(solution)/shard_map/ppermute | solution.py:329
  17.7 1.6 %collective-permute-start.8 = (f32[384,128]{1,0:T(8,128)S(1)}, f32[384,128]{1,0:T(8,128)S(1)}, u32[]{:S(2)}, u32[]{:S(2)}) collective-permute-start(f32[384,128]{1,0:T(8,128)S(1)} %pad_maximum_fusion.1), channel_id=1, source_target_pairs={{0,2},{1,3},{2,0},{3,1},{4,6},{5,7},{6,4},{7,5},{8,10},{9,11},{10,... | collective-permute-start | bytes 589832 | tf_op jit(solution)/shard_map/ppermute | solution.py:333
  19.4 1.5 %local_part.5 = (f32[64,1536]{1,0:T(8,128)S(1)}, f32[64,1536]{1,0:T(8,128)S(1)}) custom-call(f32[2,256]{1,0:T(2,128)S(1)} %concatenate.12.terms_ref, f32[64,768]{1,0:T(8,128)S(1)} %get-tuple-element.41.far_ref, f32[64,1536]{1,0:T(8,128)S(1)} %get-tuple-element.40.mid_ref, f32[64,384]{1,0:T(8,128)S(1)} %near_part.9.near_ref, ...), custom_call_target="tpu_custom_call" | custom-call | flops 301989888 | bytes 393216 | tf_op jit(solution)/shard_map/local_part/pallas_call | solution.py:206
  21.2 1.4 %second_part.3.mid_ref = f32[64,1536]{1,0:T(8,128)S(1)} custom-call(f32[2,256]{1,0:T(2,128)S(1)} %concatenate.12.terms_ref, f32[64,1536]{1,0:T(8,128)S(1)} %get-tuple-element.42.mid_ref.mid_before_ref, f32[64,384]{1,0:T(8,128)S(1)} %near_part.10.near_ref.near_before_ref, f32[64,1536]{1,0:T(8,128)S(1)} %get-tuple-element.43.before_ref, ...), custom_call_target="tpu_custom_call" | custom-call | flops 603979776 | bytes 786432 | tf_op jit(solution)/shard_map/second_part/pallas_call | solution.py:206
  23.0 0.6 collective-permute-start.10
  23.5 1.1 %collective-permute-done.8.two_ref = f32[384,128]{1,0:T(8,128)S(1)} collective-permute-done((f32[384,128]{1,0:T(8,128)S(1)}, f32[384,128]{1,0:T(8,128)S(1)}, u32[]{:S(2)}, u32[]{:S(2)}) %collective-permute-start.8) | collective-permute-done | bytes 196640 | tf_op jit(solution)/shard_map/ppermute | solution.py:333
  24.7 1.5 %turn_two.2 = (f32[64,384]{1,0:T(8,128)S(1)}, f32[64,768]{1,0:T(8,128)S(1)}, f32[2,64,384]{2,1,0:T(8,128)S(1)}) custom-call(f32[2,256]{1,0:T(2,128)S(1)} %concatenate.12.terms_ref, f32[64,1536]{1,0:T(8,128)S(1)} %second_part.3.mid_ref, f32[2,64,384]{2,1,0:T(8,128)S(1)} %get-tuple-element.44.sent_ref, f32[2,64,384]{2,1,0:T(8,128)S(1)} %collective-permute-done.5.got_ref, ...), custom_call_target="tpu_custom_call" | custom-call | flops 603979776 | bytes 786432 | tf_op jit(solution)/shard_map/turn_two/pallas_call | solution.py:206
  26.4 1.5 %local_part.6 = (f32[64,1536]{1,0:T(8,128)S(1)}, f32[64,1536]{1,0:T(8,128)S(1)}) custom-call(f32[2,256]{1,0:T(2,128)S(1)} %concatenate.12.terms_ref, f32[64,768]{1,0:T(8,128)S(1)} %get-tuple-element.48.far_ref, f32[64,1536]{1,0:T(8,128)S(1)} %second_part.3.mid_ref, f32[64,384]{1,0:T(8,128)S(1)} %near_part.11.near_ref, ...), custom_call_target="tpu_custom_call" | custom-call | flops 301989888 | bytes 393216 | tf_op jit(solution)/shard_map/local_part/pallas_call | solution.py:206
  28.2 1.2 %collective-permute-start.12 = (f32[64,384]{1,0:T(8,128)S(1)}, f32[64,384]{1,0:T(8,128)S(1)}, u32[]{:S(2)}, u32[]{:S(2)}) collective-permute-start(f32[64,384]{1,0:T(8,128)S(1)} %near_part.12.near_ref.near_before_ref), channel_id=1, source_target_pairs={{0,8},{8,0},{16,24},{24,16},{1,9},{9,1},{17,25},{25,17},{2,10},{10... | collective-permute-start | bytes 294920 | tf_op jit(solution)/shard_map/ppermute | solution.py:337
  29.4 1.4 %second_part.4.mid_ref = f32[64,1536]{1,0:T(8,128)S(1)} custom-call(f32[2,256]{1,0:T(2,128)S(1)} %concatenate.12.terms_ref, f32[64,1536]{1,0:T(8,128)S(1)} %get-tuple-element.50.mid_ref.mid_before_ref, f32[64,384]{1,0:T(8,128)S(1)} %near_part.12.near_ref.near_before_ref, f32[64,1536]{1,0:T(8,128)S(1)} %get-tuple-element.51.before_ref, ...), custom_call_target="tpu_custom_call" | custom-call | flops 603979776 | bytes 786432 | tf_op jit(solution)/shard_map/second_part/pallas_call | solution.py:206
  31.2 2.0 %collective-permute-done.11.got_ref = f32[2,64,384]{2,1,0:T(8,128)S(1)} collective-permute-done((f32[2,64,384]{2,1,0:T(8,128)S(1)}, f32[2,64,384]{2,1,0:T(8,128)S(1)}, u32[]{:S(2)}, u32[]{:S(2)}) %collective-permute-start.11) | collective-permute-done | bytes 196640 | tf_op jit(solution)/shard_map/ppermute | solution.py:329
  33.2 1.5 %turn_two.3 = (f32[64,384]{1,0:T(8,128)S(1)}, f32[64,768]{1,0:T(8,128)S(1)}, f32[2,64,384]{2,1,0:T(8,128)S(1)}) custom-call(f32[2,256]{1,0:T(2,128)S(1)} %concatenate.12.terms_ref, f32[64,1536]{1,0:T(8,128)S(1)} %second_part.4.mid_ref, f32[2,64,384]{2,1,0:T(8,128)S(1)} %get-tuple-element.52.sent_ref, f32[2,64,384]{2,1,0:T(8,128)S(1)} %collective-permute-done.11.got_ref, ...), custom_call_target="tpu_custom_call" | custom-call | flops 603979776 | bytes 786432 | tf_op jit(solution)/shard_map/turn_two/pallas_call | solution.py:206
  34.7 0.3 collective-permute-start.14
  35.0 1.5 %local_part.7 = (f32[64,1536]{1,0:T(8,128)S(1)}, f32[64,1536]{1,0:T(8,128)S(1)}) custom-call(f32[2,256]{1,0:T(2,128)S(1)} %concatenate.12.terms_ref, f32[64,768]{1,0:T(8,128)S(1)} %get-tuple-element.53.far_ref, f32[64,1536]{1,0:T(8,128)S(1)} %second_part.4.mid_ref, f32[64,384]{1,0:T(8,128)S(1)} %near_part.13.near_ref, ...), custom_call_target="tpu_custom_call" | custom-call | flops 301989888 | bytes 393216 | tf_op jit(solution)/shard_map/local_part/pallas_call | solution.py:206
  36.8 0.9 collective-permute-start.15
  37.7 1.6 %second_part.5.mid_ref = f32[64,1536]{1,0:T(8,128)S(1)} custom-call(f32[2,256]{1,0:T(2,128)S(1)} %concatenate.12.terms_ref, f32[64,1536]{1,0:T(8,128)S(1)} %get-tuple-element.55.mid_ref, f32[64,384]{1,0:T(8,128)S(1)} %near_part.14.near_ref, f32[64,1536]{1,0:T(8,128)S(1)} %get-tuple-element.56.before_ref, bf16[6,256,1024]{2,1,0:T(8,128)(2,1)S(1)} %get-tuple-element.36.hi_ref, ...), custom_call_target="tpu_custom_call" | custom-call | flops 603979776 | bytes 786432 | tf_op jit(solution)/shard_map/second_part/pallas_call | solution.py:206
  39.6 2.4 %collective-permute-done.14.got_ref = f32[2,64,384]{2,1,0:T(8,128)S(1)} collective-permute-done((f32[2,64,384]{2,1,0:T(8,128)S(1)}, f32[2,64,384]{2,1,0:T(8,128)S(1)}, u32[]{:S(2)}, u32[]{:S(2)}) %collective-permute-start.14) | collective-permute-done | bytes 196640 | tf_op jit(solution)/shard_map/ppermute | solution.py:329
  41.9 1.0 %last_part.1 = f32[8,96,128]{2,1,0:T(8,128)S(1)} custom-call(f32[2,256]{1,0:T(2,128)S(1)} %concatenate.12.terms_ref, f32[64,1536]{1,0:T(8,128)S(1)} %second_part.5.mid_ref, f32[2,64,384]{2,1,0:T(8,128)S(1)} %get-tuple-element.57.sent_ref, f32[2,64,384]{2,1,0:T(8,128)S(1)} %collective-permute-done.14.got_ref, ...), custom_call_target="tpu_custom_call" | custom-call | flops 603979776 | bytes 786432 | tf_op jit(solution)/shard_map/last_part/pallas_call | solution.py:206
  42.9 17.1 %all_to_all.5.parts_ref = f32[8,96,128]{2,1,0:T(8,128)S(1)} all-to-all(f32[8,96,128]{2,1,0:T(8,128)S(1)} %last_part.1), channel_id=1, replica_groups=mesh['narrow'=4,'wide'=8] {'wide'}, dimensions={0} | all-to-all | bytes 786432 | tf_op jit(solution)/shard_map/all_to_all | solution.py:635
  60.1 0.8 gram.1
  61.0 1.6 %collective-permute-done.16.refs_1_ = f32[576,128]{1,0:T(8,128)S(1)} collective-permute-done((f32[576,128]{1,0:T(8,128)S(1)}, f32[576,128]{1,0:T(8,128)S(1)}, u32[]{:S(2)}, u32[]{:S(2)}) %collective-permute-start.16) | collective-permute-done | bytes 294944 | tf_op jit(solution)/shard_map/ppermute | solution.py:394
  62.6 1.3 %collective-permute-start.17 = (f32[144,128]{1,0:T(8,128)S(1)}, f32[144,128]{1,0:T(8,128)S(1)}, u32[]{:S(2)}, u32[]{:S(2)}) collective-permute-start(f32[144,128]{1,0:T(8,128)S(1)} %get-tuple-element.61), channel_id=1, source_target_pairs={{0,16},{1,17},{2,18},{3,19},{4,20},{5,21},{6,22},{7,23},{8,24},{9,... | collective-permute-start | bytes 221192 | tf_op jit(solution)/shard_map/ppermute | solution.py:394
  63.8 1.1 %collective-permute-start.18 = (f32[144,128]{1,0:T(8,128)S(1)}, f32[144,128]{1,0:T(8,128)S(1)}, u32[]{:S(2)}, u32[]{:S(2)}) collective-permute-start(f32[144,128]{1,0:T(8,128)S(1)} %get-tuple-element.62), channel_id=1, source_target_pairs={{0,1},{1,0},{2,3},{3,2},{4,5},{5,4},{6,7},{7,6},{8,9},{9,8},{10,11... | collective-permute-start | bytes 221192 | tf_op jit(solution)/shard_map/ppermute | solution.py:394
  64.9 1.2 %collective-permute-start.19 = (f32[144,128]{1,0:T(8,128)S(1)}, f32[144,128]{1,0:T(8,128)S(1)}, u32[]{:S(2)}, u32[]{:S(2)}) collective-permute-start(f32[144,128]{1,0:T(8,128)S(1)} %get-tuple-element.63), channel_id=1, source_target_pairs={{0,17},{1,16},{2,19},{3,18},{4,21},{5,20},{6,23},{7,22},{8,25},{9,... | collective-permute-start | bytes 221192 | tf_op jit(solution)/shard_map/ppermute | solution.py:394
  66.1 0.9 collective-permute-done.17
  67.0 2.0 %collective-permute-done.18 = f32[144,128]{1,0:T(8,128)S(1)} collective-permute-done((f32[144,128]{1,0:T(8,128)S(1)}, f32[144,128]{1,0:T(8,128)S(1)}, u32[]{:S(2)}, u32[]{:S(2)}) %collective-permute-start.18) | collective-permute-done | bytes 73760 | tf_op jit(solution)/shard_map/ppermute | solution.py:394
  69.0 1.2 %collective-permute-done.19 = f32[144,128]{1,0:T(8,128)S(1)} collective-permute-done((f32[144,128]{1,0:T(8,128)S(1)}, f32[144,128]{1,0:T(8,128)S(1)}, u32[]{:S(2)}, u32[]{:S(2)}) %collective-permute-start.19) | collective-permute-done | bytes 73760 | tf_op jit(solution)/shard_map/ppermute | solution.py:394
  70.2 0.5 collective-permute-start.20
  70.7 1.6 %collective-permute-start.21 = (f32[144,128]{1,0:T(8,128)S(1)}, f32[144,128]{1,0:T(8,128)S(1)}, u32[]{:S(2)}, u32[]{:S(2)}) collective-permute-start(f32[144,128]{1,0:T(8,128)S(1)} %add_add_fusion.1), channel_id=1, source_target_pairs={{0,4},{1,5},{2,6},{3,7},{4,0},{5,1},{6,2},{7,3},{8,12},{9,13},{10,... | collective-permute-start | bytes 221192 | tf_op jit(solution)/shard_map/ppermute | solution.py:394
  72.3 2.4 %collective-permute-start.22 = (f32[144,128]{1,0:T(8,128)S(1)}, f32[144,128]{1,0:T(8,128)S(1)}, u32[]{:S(2)}, u32[]{:S(2)}) collective-permute-start(f32[144,128]{1,0:T(8,128)S(1)} %add_add_fusion.1), channel_id=1, source_target_pairs={{0,6},{1,7},{2,4},{3,5},{4,2},{5,3},{6,0},{7,1},{8,14},{9,15},{10,... | collective-permute-start | bytes 221192 | tf_op jit(solution)/shard_map/ppermute | solution.py:394
  74.7 2.7 %collective-permute-done.21 = f32[144,128]{1,0:T(8,128)S(1)} collective-permute-done((f32[144,128]{1,0:T(8,128)S(1)}, f32[144,128]{1,0:T(8,128)S(1)}, u32[]{:S(2)}, u32[]{:S(2)}) %collective-permute-start.21) | collective-permute-done | bytes 73760 | tf_op jit(solution)/shard_map/ppermute | solution.py:394
  77.4 1.2 %collective-permute-done.22 = f32[144,128]{1,0:T(8,128)S(1)} collective-permute-done((f32[144,128]{1,0:T(8,128)S(1)}, f32[144,128]{1,0:T(8,128)S(1)}, u32[]{:S(2)}, u32[]{:S(2)}) %collective-permute-start.22) | collective-permute-done | bytes 73760 | tf_op jit(solution)/shard_map/ppermute | solution.py:394
  78.6 0.9 collective-permute-start.23
  79.5 0.8 collective-permute-start.24
  80.3 1.8 %collective-permute-start.25 = (f32[144,128]{1,0:T(8,128)S(1)}, f32[144,128]{1,0:T(8,128)S(1)}, u32[]{:S(2)}, u32[]{:S(2)}) collective-permute-start(f32[144,128]{1,0:T(8,128)S(1)} %add_add_fusion), channel_id=1, source_target_pairs={{0,17},{1,16},{2,19},{3,18},{4,21},{5,20},{6,23},{7,22},{8,25},{9,... | collective-permute-start | bytes 221192 | tf_op jit(solution)/shard_map/ppermute | solution.py:394
  82.1 0.9 collective-permute-done.23
  83.0 0.8 collective-permute-done.24
  83.8 1.7 %collective-permute-done.25 = f32[144,128]{1,0:T(8,128)S(1)} collective-permute-done((f32[144,128]{1,0:T(8,128)S(1)}, f32[144,128]{1,0:T(8,128)S(1)}, u32[]{:S(2)}, u32[]{:S(2)}) %collective-permute-start.25) | collective-permute-done | bytes 73760 | tf_op jit(solution)/shard_map/ppermute | solution.py:394
  85.7 1.6 %collective-permute-done.26.other_ref = f32[576,128]{1,0:T(8,128)S(1)} collective-permute-done((f32[576,128]{1,0:T(8,128)S(1)}, f32[576,128]{1,0:T(8,128)S(1)}, u32[]{:S(2)}, u32[]{:S(2)}) %collective-permute-start.26) | collective-permute-done | bytes 294944 | tf_op jit(solution)/shard_map/ppermute | solution.py:394
  87.2 1.6 %rotate.1 = f32[192,512]{1,0:T(8,128)} custom-call(f32[576,128]{1,0:T(8,128)S(1)} %pad_maximum_fusion.own_ref, f32[576,128]{1,0:T(8,128)S(1)} %collective-permute-done.26.other_ref, f32[192,512]{1,0:T(8,128)S(1)} %get-tuple-element.64.rows_ref), custom_call_target="tpu_custom_call" | custom-call | tf_op jit(solution)/shard_map/rotate/pallas_call | solution.py:615
  (39 shorter events, 3.6 us)
Async XLA Ops:
  2.8 6.3 %collective-permute-start.1 = (f32[64,384]{1,0:T(8,128)S(1)}, f32[64,384]{1,0:T(8,128)S(1)}, u32[]{:S(2)}, u32[]{:S(2)}) collective-permute-start(f32[64,384]{1,0:T(8,128)S(1)} %get-tuple-element.39.near_before_ref), channel_id=1, source_target_pairs={{0,8},{8,0},{16,24},{24,16},{1,9},{9,1},{17,25},{25,17},{2,10},{10... | collective-permute-start | bytes 294920 | tf_op jit(solution)/shard_map/ppermute | solution.py:337
  3.3 6.2 %collective-permute-start = (f32[64,384]{1,0:T(8,128)S(1)}, f32[64,384]{1,0:T(8,128)S(1)}, u32[]{:S(2)}, u32[]{:S(2)}) collective-permute-start(f32[64,384]{1,0:T(8,128)S(1)} %get-tuple-element.38.far_before_ref), channel_id=1, source_target_pairs={{0,24},{8,16},{16,8},{24,0},{1,25},{9,17},{17,9},{25,1},{2,26},{10... | collective-permute-start | bytes 294920 | tf_op jit(solution)/shard_map/ppermute | solution.py:329
  6.0 5.7 %collective-permute-start.6 = (f32[192,128]{1,0:T(8,128)S(1)}, f32[192,128]{1,0:T(8,128)S(1)}, u32[]{:S(2)}, u32[]{:S(2)}) collective-permute-start(f32[192,128]{1,0:T(8,128)S(1)} %get-tuple-element.45), channel_id=1, source_target_pairs={{0,24},{8,16},{16,8},{24,0},{1,25},{9,17},{17,9},{25,1},{2,26},{10... | collective-permute-start | bytes 294920 | tf_op jit(solution)/shard_map/ppermute | solution.py:329
  9.4 6.1 %collective-permute-start.3 = (f32[64,384]{1,0:T(8,128)S(1)}, f32[64,384]{1,0:T(8,128)S(1)}, u32[]{:S(2)}, u32[]{:S(2)}) collective-permute-start(f32[64,384]{1,0:T(8,128)S(1)} %near_part.8.near_ref.near_before_ref), channel_id=1, source_target_pairs={{0,8},{8,0},{16,24},{24,16},{1,9},{9,1},{17,25},{25,17},{2,10},{10... | collective-permute-start | bytes 294920 | tf_op jit(solution)/shard_map/ppermute | solution.py:337
  9.9 6.1 %collective-permute-start.2 = (f32[64,384]{1,0:T(8,128)S(1)}, f32[64,384]{1,0:T(8,128)S(1)}, u32[]{:S(2)}, u32[]{:S(2)}) collective-permute-start(f32[64,384]{1,0:T(8,128)S(1)} %far_part.1.far_ref.before_ref.far_before_ref), channel_id=1, source_target_pairs={{0,24},{8,16},{16,8},{24,0},{1,25},{9,17},{17,9},{25,1},{2,26},{10... | collective-permute-start | bytes 294920 | tf_op jit(solution)/shard_map/ppermute | solution.py:329
  11.6 6.1 %collective-permute-start.7 = (f32[192,128]{1,0:T(8,128)S(1)}, f32[192,128]{1,0:T(8,128)S(1)}, u32[]{:S(2)}, u32[]{:S(2)}) collective-permute-start(f32[192,128]{1,0:T(8,128)S(1)} %collective-permute-done.6.mine_ref), channel_id=1, source_target_pairs={{0,1},{1,0},{2,3},{3,2},{4,5},{5,4},{6,7},{7,6},{8,9},{9,8},{10,11... | collective-permute-start | bytes 294920 | tf_op jit(solution)/shard_map/ppermute | solution.py:333
  15.7 5.1 %collective-permute-start.4 = (f32[64,384]{1,0:T(8,128)S(1)}, f32[64,384]{1,0:T(8,128)S(1)}, u32[]{:S(2)}, u32[]{:S(2)}) collective-permute-start(f32[64,384]{1,0:T(8,128)S(1)} %near_part.9.near_ref), channel_id=1, source_target_pairs={{0,8},{8,0},{16,24},{24,16},{1,9},{9,1},{17,25},{25,17},{2,10},{10... | collective-permute-start | bytes 294920 | tf_op jit(solution)/shard_map/ppermute | solution.py:337
  16.7 8.0 %collective-permute-start.5 = (f32[2,64,384]{2,1,0:T(8,128)S(1)}, f32[2,64,384]{2,1,0:T(8,128)S(1)}, u32[]{:S(2)}, u32[]{:S(2)}) collective-permute-start(f32[2,64,384]{2,1,0:T(8,128)S(1)} %get-tuple-element.44.sent_ref), channel_id=1, source_target_pairs={{0,24},{8,16},{16,8},{24,0},{1,25},{9,17},{17,9},{25,1},{2,26},{10... | collective-permute-start | bytes 589832 | tf_op jit(solution)/shard_map/ppermute | solution.py:329
  17.7 6.9 %collective-permute-start.8 = (f32[384,128]{1,0:T(8,128)S(1)}, f32[384,128]{1,0:T(8,128)S(1)}, u32[]{:S(2)}, u32[]{:S(2)}) collective-permute-start(f32[384,128]{1,0:T(8,128)S(1)} %pad_maximum_fusion.1), channel_id=1, source_target_pairs={{0,2},{1,3},{2,0},{3,1},{4,6},{5,7},{6,4},{7,5},{8,10},{9,11},{10,... | collective-permute-start | bytes 589832 | tf_op jit(solution)/shard_map/ppermute | solution.py:333
  21.2 1.5 %collective-permute-start.9 = (f32[64,384]{1,0:T(8,128)S(1)}, f32[64,384]{1,0:T(8,128)S(1)}, u32[]{:S(2)}, u32[]{:S(2)}) collective-permute-start(f32[64,384]{1,0:T(8,128)S(1)} %near_part.10.near_ref.near_before_ref), channel_id=1, source_target_pairs={{0,8},{8,0},{16,24},{24,16},{1,9},{9,1},{17,25},{25,17},{2,10},{10... | collective-permute-start | bytes 294920 | tf_op jit(solution)/shard_map/ppermute | solution.py:337
  23.0 4.9 %collective-permute-start.10 = (f32[64,384]{1,0:T(8,128)S(1)}, f32[64,384]{1,0:T(8,128)S(1)}, u32[]{:S(2)}, u32[]{:S(2)}) collective-permute-start(f32[64,384]{1,0:T(8,128)S(1)} %near_part.11.near_ref), channel_id=1, source_target_pairs={{0,8},{8,0},{16,24},{24,16},{1,9},{9,1},{17,25},{25,17},{2,10},{10... | collective-permute-start | bytes 294920 | tf_op jit(solution)/shard_map/ppermute | solution.py:337
  26.2 7.0 %collective-permute-start.11 = (f32[2,64,384]{2,1,0:T(8,128)S(1)}, f32[2,64,384]{2,1,0:T(8,128)S(1)}, u32[]{:S(2)}, u32[]{:S(2)}) collective-permute-start(f32[2,64,384]{2,1,0:T(8,128)S(1)} %get-tuple-element.52.sent_ref), channel_id=1, source_target_pairs={{0,24},{8,16},{16,8},{24,0},{1,25},{9,17},{17,9},{25,1},{2,26},{10... | collective-permute-start | bytes 589832 | tf_op jit(solution)/shard_map/ppermute | solution.py:329
  28.2 2.7 %collective-permute-start.12 = (f32[64,384]{1,0:T(8,128)S(1)}, f32[64,384]{1,0:T(8,128)S(1)}, u32[]{:S(2)}, u32[]{:S(2)}) collective-permute-start(f32[64,384]{1,0:T(8,128)S(1)} %near_part.12.near_ref.near_before_ref), channel_id=1, source_target_pairs={{0,8},{8,0},{16,24},{24,16},{1,9},{9,1},{17,25},{25,17},{2,10},{10... | collective-permute-start | bytes 294920 | tf_op jit(solution)/shard_map/ppermute | solution.py:337
  31.1 5.4 %collective-permute-start.13 = (f32[64,384]{1,0:T(8,128)S(1)}, f32[64,384]{1,0:T(8,128)S(1)}, u32[]{:S(2)}, u32[]{:S(2)}) collective-permute-start(f32[64,384]{1,0:T(8,128)S(1)} %near_part.13.near_ref), channel_id=1, source_target_pairs={{0,8},{8,0},{16,24},{24,16},{1,9},{9,1},{17,25},{25,17},{2,10},{10... | collective-permute-start | bytes 294920 | tf_op jit(solution)/shard_map/ppermute | solution.py:337
  34.7 7.2 %collective-permute-start.14 = (f32[2,64,384]{2,1,0:T(8,128)S(1)}, f32[2,64,384]{2,1,0:T(8,128)S(1)}, u32[]{:S(2)}, u32[]{:S(2)}) collective-permute-start(f32[2,64,384]{2,1,0:T(8,128)S(1)} %get-tuple-element.57.sent_ref), channel_id=1, source_target_pairs={{0,24},{8,16},{16,8},{24,0},{1,25},{9,17},{17,9},{25,1},{2,26},{10... | collective-permute-start | bytes 589832 | tf_op jit(solution)/shard_map/ppermute | solution.py:329
  36.8 2.5 %collective-permute-start.15 = (f32[64,384]{1,0:T(8,128)S(1)}, f32[64,384]{1,0:T(8,128)S(1)}, u32[]{:S(2)}, u32[]{:S(2)}) collective-permute-start(f32[64,384]{1,0:T(8,128)S(1)} %near_part.14.near_ref), channel_id=1, source_target_pairs={{0,8},{8,0},{16,24},{24,16},{1,9},{9,1},{17,25},{25,17},{2,10},{10... | collective-permute-start | bytes 294920 | tf_op jit(solution)/shard_map/ppermute | solution.py:337
  60.9 1.6 %collective-permute-start.16 = (f32[576,128]{1,0:T(8,128)S(1)}, f32[576,128]{1,0:T(8,128)S(1)}, u32[]{:S(2)}, u32[]{:S(2)}) collective-permute-start(f32[576,128]{1,0:T(8,128)S(1)} %get-tuple-element.59), channel_id=1, source_target_pairs={{0,8},{1,9},{2,10},{3,11},{4,12},{5,13},{6,14},{7,15},{8,0},{9,1},... | collective-permute-start | bytes 884744 | tf_op jit(solution)/shard_map/ppermute | solution.py:394
  62.6 4.4 %collective-permute-start.17 = (f32[144,128]{1,0:T(8,128)S(1)}, f32[144,128]{1,0:T(8,128)S(1)}, u32[]{:S(2)}, u32[]{:S(2)}) collective-permute-start(f32[144,128]{1,0:T(8,128)S(1)} %get-tuple-element.61), channel_id=1, source_target_pairs={{0,16},{1,17},{2,18},{3,19},{4,20},{5,21},{6,22},{7,23},{8,24},{9,... | collective-permute-start | bytes 221192 | tf_op jit(solution)/shard_map/ppermute | solution.py:394
  63.8 5.1 %collective-permute-start.18 = (f32[144,128]{1,0:T(8,128)S(1)}, f32[144,128]{1,0:T(8,128)S(1)}, u32[]{:S(2)}, u32[]{:S(2)}) collective-permute-start(f32[144,128]{1,0:T(8,128)S(1)} %get-tuple-element.62), channel_id=1, source_target_pairs={{0,1},{1,0},{2,3},{3,2},{4,5},{5,4},{6,7},{7,6},{8,9},{9,8},{10,11... | collective-permute-start | bytes 221192 | tf_op jit(solution)/shard_map/ppermute | solution.py:394
  64.9 5.3 %collective-permute-start.19 = (f32[144,128]{1,0:T(8,128)S(1)}, f32[144,128]{1,0:T(8,128)S(1)}, u32[]{:S(2)}, u32[]{:S(2)}) collective-permute-start(f32[144,128]{1,0:T(8,128)S(1)} %get-tuple-element.63), channel_id=1, source_target_pairs={{0,17},{1,16},{2,19},{3,18},{4,21},{5,20},{6,23},{7,22},{8,25},{9,... | collective-permute-start | bytes 221192 | tf_op jit(solution)/shard_map/ppermute | solution.py:394
  70.2 4.5 %collective-permute-start.20 = (f32[144,128]{1,0:T(8,128)S(1)}, f32[144,128]{1,0:T(8,128)S(1)}, u32[]{:S(2)}, u32[]{:S(2)}) collective-permute-start(f32[144,128]{1,0:T(8,128)S(1)} %add_add_fusion.1), channel_id=1, source_target_pairs={{0,2},{1,3},{2,0},{3,1},{4,6},{5,7},{6,4},{7,5},{8,10},{9,11},{10,... | collective-permute-start | bytes 221192 | tf_op jit(solution)/shard_map/ppermute | solution.py:394
  70.7 6.7 %collective-permute-start.21 = (f32[144,128]{1,0:T(8,128)S(1)}, f32[144,128]{1,0:T(8,128)S(1)}, u32[]{:S(2)}, u32[]{:S(2)}) collective-permute-start(f32[144,128]{1,0:T(8,128)S(1)} %add_add_fusion.1), channel_id=1, source_target_pairs={{0,4},{1,5},{2,6},{3,7},{4,0},{5,1},{6,2},{7,3},{8,12},{9,13},{10,... | collective-permute-start | bytes 221192 | tf_op jit(solution)/shard_map/ppermute | solution.py:394
  72.3 6.3 %collective-permute-start.22 = (f32[144,128]{1,0:T(8,128)S(1)}, f32[144,128]{1,0:T(8,128)S(1)}, u32[]{:S(2)}, u32[]{:S(2)}) collective-permute-start(f32[144,128]{1,0:T(8,128)S(1)} %add_add_fusion.1), channel_id=1, source_target_pairs={{0,6},{1,7},{2,4},{3,5},{4,2},{5,3},{6,0},{7,1},{8,14},{9,15},{10,... | collective-permute-start | bytes 221192 | tf_op jit(solution)/shard_map/ppermute | solution.py:394
  78.6 4.4 %collective-permute-start.23 = (f32[144,128]{1,0:T(8,128)S(1)}, f32[144,128]{1,0:T(8,128)S(1)}, u32[]{:S(2)}, u32[]{:S(2)}) collective-permute-start(f32[144,128]{1,0:T(8,128)S(1)} %add_add_fusion), channel_id=1, source_target_pairs={{0,16},{1,17},{2,18},{3,19},{4,20},{5,21},{6,22},{7,23},{8,24},{9,... | collective-permute-start | bytes 221192 | tf_op jit(solution)/shard_map/ppermute | solution.py:394
  79.5 4.4 %collective-permute-start.24 = (f32[144,128]{1,0:T(8,128)S(1)}, f32[144,128]{1,0:T(8,128)S(1)}, u32[]{:S(2)}, u32[]{:S(2)}) collective-permute-start(f32[144,128]{1,0:T(8,128)S(1)} %add_add_fusion), channel_id=1, source_target_pairs={{0,1},{1,0},{2,3},{3,2},{4,5},{5,4},{6,7},{7,6},{8,9},{9,8},{10,11... | collective-permute-start | bytes 221192 | tf_op jit(solution)/shard_map/ppermute | solution.py:394
  80.3 5.3 %collective-permute-start.25 = (f32[144,128]{1,0:T(8,128)S(1)}, f32[144,128]{1,0:T(8,128)S(1)}, u32[]{:S(2)}, u32[]{:S(2)}) collective-permute-start(f32[144,128]{1,0:T(8,128)S(1)} %add_add_fusion), channel_id=1, source_target_pairs={{0,17},{1,16},{2,19},{3,18},{4,21},{5,20},{6,23},{7,22},{8,25},{9,... | collective-permute-start | bytes 221192 | tf_op jit(solution)/shard_map/ppermute | solution.py:394
  85.6 1.6 %collective-permute-start.26 = (f32[576,128]{1,0:T(8,128)S(1)}, f32[576,128]{1,0:T(8,128)S(1)}, u32[]{:S(2)}, u32[]{:S(2)}) collective-permute-start(f32[576,128]{1,0:T(8,128)S(1)} %pad_maximum_fusion.own_ref), channel_id=1, source_target_pairs={{0,8},{1,9},{2,10},{3,11},{4,12},{5,13},{6,14},{7,15},{8,0},{9,1},... | collective-permute-start | bytes 884744 | tf_op jit(solution)/shard_map/ppermute | solution.py:394

commit v3 on v2

--- a/solution.py
+++ b/solution.py
@@ -130,12 +130,14 @@
         self.both = jnp.concatenate([self.hi, lo], axis=0)
         self.at, self.size = at, size
 
-    def band(self, operator, pair, begin, end):
+    def band(self, operator, pair, begin, end, half=None):
         hi_ref, lo_ref = operator
         size, start = self.size, 2 * pair - REACH
         there = slice((begin - self.at) * size, (end - self.at) * size)
         inside = slice((begin - start) * size, (end - start) * size)
-        return dot_split(self.hi[:, there], self.both[:, there], hi_ref[pair, :, inside], lo_ref[pair, :, inside], NT)
+        rows = slice(None) if half is None else slice(half * size, (half + 1) * size)
+        hi, lo = hi_ref[pair, rows, inside], lo_ref[pair, rows, inside]
+        return dot_split(self.hi[:, there], self.both[:, there], hi, lo, NT)
 
 
 def reversed_blocks(edge, size):
@@ -145,16 +147,16 @@
 def far_sum(operator, halo, size):
     strip = Strip(jnp.concatenate(reversed_blocks(halo, size), axis=1), -REACH, size)
     outer = strip.band(operator, 0, -REACH, 0)
-    inner = strip.band(operator, 1, -1, 0)
-    return jnp.concatenate([outer, inner[:, :size]], axis=1)
+    inner = strip.band(operator, 1, -1, 0, 0)
+    return jnp.concatenate([outer, inner], axis=1)
 
 
 def near_sum(operator, halo, size):
     pairs = operator[0].shape[0]
     strip = Strip(jnp.concatenate(reversed_blocks(halo, size), axis=1), 2 * pairs, size)
     outer = strip.band(operator, pairs - 1, 2 * pairs, 2 * pairs + REACH)
-    inner = strip.band(operator, pairs - 2, 2 * pairs, 2 * pairs + 1)
-    return jnp.concatenate([inner[:, size:], outer], axis=1)
+    inner = strip.band(operator, pairs - 2, 2 * pairs, 2 * pairs + 1, 1)
+    return jnp.concatenate([inner, outer], axis=1)
 
 
 def own_sum(operator, strip, pair, lowest=0):
@@ -223,8 +225,8 @@
 def edge_ahead(operator, scale, diag, far, before, size):
     strip = Strip(far, 0, size)
     outer = strip.band(operator, 0, 0, REACH + 2)
-    inner = strip.band(operator, 1, 0, 2 * REACH)
-    total = jnp.concatenate([outer, inner[:, :size]], axis=1)
+    inner = strip.band(operator, 1, 0, 2 * REACH, 0)
+    total = jnp.concatenate([outer, inner], axis=1)
     return scale * total + diag * far[:, : total.shape[1]] - before
 
 
@@ -244,10 +246,9 @@
     send_ref[1] = edge_ahead(operator, scale, diag, far, before_ref[...], size)
 
 
-def turn(terms_ref, mid_ref, sent_ref, got_ref, cross_hi_ref, cross_lo_ref, operator):
-    size, edge = operator[0].shape[1] // 2, sent_ref.shape[2]
-    scale, diag = terms_ref[0:1, 0:1], terms_ref[1:2, 0:1]
-    between = sent_ref[1] + scale * far_sum(operator, got_ref[0], size)
+def beyond_sum(terms_ref, sent_ref, cross_hi_ref, cross_lo_ref):
+    size = cross_hi_ref.shape[1]
+
     def cross(ref, row):
         rows = [slice(at * size, (at + 1) * size) for at in (cross_at(row, -1 - place) for place in range(REACH - row))]
         return jnp.concatenate([ref[here, :] for here in rows], axis=1)
@@ -258,7 +259,19 @@
         there = slice(0, (REACH - row) * size)
         hi, lo = cross(cross_hi_ref, row), cross(cross_lo_ref, row)
         pieces.append(dot_split(own.hi[:, there], own.both[:, there], hi, lo, NT))
-    beyond = got_ref[1] + scale * jnp.concatenate(pieces, axis=1)
+    return terms_ref[0:1, 0:1] * jnp.concatenate(pieces, axis=1)
+
+
+def beyond_kernel(terms_ref, sent_ref, cross_hi_ref, cross_lo_ref, out_ref):
+    out_ref[...] = beyond_sum(terms_ref, sent_ref, cross_hi_ref, cross_lo_ref)
+
+
+def turn(terms_ref, mid_ref, sent_ref, got_ref, beyond_refs, operator):
+    size, edge = operator[0].shape[1] // 2, sent_ref.shape[2]
+    scale, diag = terms_ref[0:1, 0:1], terms_ref[1:2, 0:1]
+    between = sent_ref[1] + scale * far_sum(operator, got_ref[0], size)
+    beyond = beyond_refs[0][...] if len(beyond_refs) == 1 else beyond_sum(terms_ref, sent_ref, *beyond_refs)
+    beyond = got_ref[1] + beyond
     strip = Strip(jnp.concatenate(reversed_blocks(beyond, size) + [between], axis=1), -REACH, size)
     total = [strip.band(operator, pair, 2 * pair - REACH, REACH) for pair in range(REACH)]
     known = jnp.concatenate([diag * between, jnp.zeros_like(between)], axis=1)
@@ -289,10 +302,11 @@
     )(mine, one, two)
 
 
-def turn_two_kernel(terms_ref, mid_ref, sent_ref, got_ref, cross_hi_ref, cross_lo_ref, hi_ref, lo_ref, between_ref, far_ref, send_ref):
+def turn_two_kernel(terms_ref, mid_ref, sent_ref, got_ref, *refs):
+    *beyond_refs, hi_ref, lo_ref, between_ref, far_ref, send_ref = refs
     operator = (hi_ref, lo_ref)
     size, edge = hi_ref.shape[1] // 2, between_ref.shape[1]
-    between, far = turn(terms_ref, mid_ref, sent_ref, got_ref, cross_hi_ref, cross_lo_ref, operator)
+    between, far = turn(terms_ref, mid_ref, sent_ref, got_ref, beyond_refs, operator)
     between_ref[...] = between
     far_ref[...] = far
     send_ref[0] = far[:, :edge]
@@ -303,9 +317,9 @@
     return own % TILE == TILE // 2 and own > TILE and count % 16 == 0
 
 
-def last_kernel(parts, terms_ref, mid_ref, sent_ref, got_ref, cross_hi_ref, cross_lo_ref, near_ref, hi_ref, lo_ref, out_ref):
+def last_kernel(parts, terms_ref, mid_ref, sent_ref, got_ref, beyond_ref, near_ref, hi_ref, lo_ref, out_ref):
     size = hi_ref.shape[1] // 2
-    _, far = turn(terms_ref, mid_ref, sent_ref, got_ref, cross_hi_ref, cross_lo_ref, (hi_ref, lo_ref))
+    _, far = turn(terms_ref, mid_ref, sent_ref, got_ref, (beyond_ref,), (hi_ref, lo_ref))
     whole = jnp.concatenate([far, mid_ref[:, far.shape[1] : -near_ref.shape[1]], near_ref[...]], axis=1)
     mirrored = jnp.concatenate(reversed_blocks(whole, size), axis=1)
     whole = jnp.where(odd_device(), mirrored, whole)
@@ -364,7 +378,7 @@
     near = near_part(0.5, mid, near_halo)
     (far,) = step_call(far_kernel, "far_part", (terms, mid, halo), operator, [side])
     halo, near_halo = far_swap(far), near_swap(near)
-    next_mid, _ = local_part(0, 2)
+    (next_mid,) = local_part(0, 1)
     before = (far, mid, near)
     mid, near = next_mid, near_part(1.0, next_mid, near_halo)
     far, send = step_call(turn_one_kernel, "turn_one", (terms, mid, halo, far), operator, [(count, 2 * edge), double])
@@ -375,7 +389,10 @@
         near_halo = near_swap(near)
         (next_mid,) = step_call(second_kernel, "second_part", (terms, mid, near, full), operator, [whole])
         next_near = near_part(1.0, next_mid, near_halo)
-        operands = (terms, next_mid, send, got, *cross)
+        beyond = cross
+        if step > 2:
+            beyond = step_call(beyond_kernel, "beyond_part", (terms, send), cross, [side])
+        operands = (terms, next_mid, send, got, *beyond)
         if step < STEPS - 2:
             outs = [side, (count, 2 * edge), double]
             between, far, send = step_call(turn_two_kernel, "turn_two", operands, operator, outs)
@@ -498,7 +515,6 @@
         parts, length, _ = parts_ref.shape
         count, half = length * TILE // own, TILE // 2
         heads = (own - half) // TILE
-        odd = lax.rem(lax.axis_index("wide"), 2) == 1
         pieces = []
         for part in range(parts):
             head = [parts_ref[part, h * count : (h + 1) * count, :] for h in range(heads)]
@@ -506,10 +522,9 @@
             swapped = pltpu.roll(tails, half, 1)
             low = lax.broadcasted_iota(jnp.int32, tails.shape, 1) < half
             tail = jnp.concatenate([jnp.where(low, tails, swapped), jnp.where(low, swapped, tails)], axis=0)
-            whole = jnp.concatenate(head + [tail], axis=1)
-            pieces.append(jnp.where(odd, pltpu.roll(whole, half, 1), whole)[:, :own])
+            pieces.append(jnp.concatenate(head + [tail], axis=1)[:, :own])
         rows = jnp.concatenate(pieces, axis=0)
-    rows_ref[...] = rows.T
+    rows_ref[...] = rows
     tiles, half = rows.shape[0] // TILE, TILE // 2
     hi, lo = split(rows)
     at, tops = 0, len(tile_pairs(tiles)) * TILE
@@ -543,11 +558,30 @@
         functools.partial(gram_kernel, own),
         in_specs=[VM],
         out_specs=[VM] * 3,
-        out_shape=[half, half, jax.ShapeDtypeStruct((own, total), F32)],
+        out_shape=[half, half, jax.ShapeDtypeStruct((total, own), F32)],
         scratch_shapes=[pltpu.VMEM((size, TILE), F32)],
         compiler_params=params(),
         name="gram",
     )(parts)
+
+
+def turned_kernel(packed, rows_ref, out_ref):
+    rows = rows_ref[...].T
+    if packed:
+        half = TILE // 2
+        rows = jnp.where(odd_place("wide"), jnp.concatenate([rows[-half:], rows[:-half]], axis=0), rows)
+    out_ref[...] = rows
+
+
+def turned(rows, packed):
+    return pl.pallas_call(
+        functools.partial(turned_kernel, packed),
+        in_specs=[VM],
+        out_specs=VM,
+        out_shape=jax.ShapeDtypeStruct(rows.shape[::-1], F32),
+        compiler_params=params(),
+        name="turned",
+    )(rows)
 
 
 def rotate_kernel(total_rows, groups, own_ref, other_ref, rows_ref, out_ref, packed, hi_ref, lo_ref, held, sems):
@@ -644,7 +678,7 @@
     length = vectors.shape[1]
     parts = regroup(filtered_parts(vectors, blocks, columns, lower_bound, upper_bound))
     *halves, rows = gram(parts, length // lax.axis_size("wide"))
-    return rotate(all_sum(halves), rows, length * lax.axis_size("narrow"))
+    return rotate(all_sum(halves), turned(rows, parts.ndim == 3), length * lax.axis_size("narrow"))
 
 
 def solution(mesh):

time: 89.2 us -> 88.6 us (level)
  waiting for transfers between devices: 20 us -> 19.1 us
    pallas_call x21 -> x23, Pallas kernels: 20.1 us -> 19.6 us  [step_call(): pl.pallas_call(kernel, in_specs=[VM] * (len(operands) + 2), out_specs=[VM...]
where the time goes in v3:
time: 88.6 us; the launch traced here: 88.5 us
  Pallas kernels  25 us (28%)
  starting transfers between devices  24.7 us (28%)
  waiting for transfers between devices  19.1 us (22%)
  blocking collectives  17.7 us (20%)
  between operations  1.84 us (2%)
    pallas_call x23, Pallas kernels, step_call(): pl.pallas_call(kernel, in_specs=[VM] * (len(operands) + 2), out_specs=[VM...  19.6 us
    all_to_all x1, blocking collectives, regroup(): lax.all_to_all(parts, 'wide', split_axis=0, concat_axis=0, tiled=True)  17.7 us
    ppermute x11, waiting for transfers between devices, swap(): return lax.ppermute(x, ('narrow', 'wide'), pair_perm(mask))  14.3 us
    ppermute x11, starting transfers between devices, swap(): return lax.ppermute(x, ('narrow', 'wide'), pair_perm(mask))  11.7 us
    ppermute x6, starting transfers between devices, far_swap(): lax.ppermute(x, 'narrow', [(i, (i + 1) % size if i % 2 else (i - 1) % siz...  6.77 us
    ppermute x6, waiting for transfers between devices, far_swap(): lax.ppermute(x, 'narrow', [(i, (i + 1) % size if i % 2 else (i - 1) % siz...  3.59 us
    ppermute x2, starting transfers between devices, wide_swap(): lax.ppermute(x, 'wide', [(i, i ^ mask) for i in range(lax.axis_size('wide...  3.16 us
    ppermute x8, starting transfers between devices, near_swap(): lax.ppermute(x, 'narrow', [(i, i ^ 1) for i in range(lax.axis_size('narro...  3.02 us
  transfers between devices with their start and end apart: 27, of which 13 were waited for; matrix products, arithmetic and copies ran while one was open for 0% of the time, Pallas kernels for 21%

profile of v3, /device:TPU:0, one launch (start us, length us, event | category | flops | bytes accessed | tf_op | source)
XLA Modules:
  0.0 88.5 jit_solution(363014179335562711)
XLA Ops:
  0.0 2.8 %spread_part.1 = (f32[64,384]{1,0:T(8,128)S(1)}, f32[64,384]{1,0:T(8,128)S(1)}, f32[64,1536]{1,0:T(8,128)S(1)}, f32[192,128]{1,0:T(8,128)S(1)}, bf16[6,256,1024]...) custom-call(s32[5,12]{1,0:T(8,128)} %bitcast.3, f32[64,1536]{1,0:T(8,128)} %vectors_hbm.1, f32[12,5,128,128]{3,2,1,0:T(8,128)} %blocks_hbm.1), custom_call_target="tpu_custom_call" | custom-call | tf_op jit(solution)/shard_map/spread_part/pallas_call | solution.py:109
  2.8 0.5 collective-permute-start.1
  3.3 2.6 %collective-permute-start = (f32[64,384]{1,0:T(8,128)S(1)}, f32[64,384]{1,0:T(8,128)S(1)}, u32[]{:S(2)}, u32[]{:S(2)}) collective-permute-start(f32[64,384]{1,0:T(8,128)S(1)} %get-tuple-element.37.far_before_ref), channel_id=1, source_target_pairs={{0,24},{8,16},{16,8},{24,0},{1,25},{9,17},{17,9},{25,1},{2,26},{10... | collective-permute-start | bytes 294920 | tf_op jit(solution)/shard_map/ppermute | solution.py:343
  7.4 1.7 %first_part.1.mid_ref.mid_before_ref = f32[64,1536]{1,0:T(8,128)S(1)} custom-call(f32[2,256]{1,0:T(2,128)S(1)} %concatenate.12.terms_ref, f32[64,1536]{1,0:T(8,128)S(1)} %get-tuple-element.34.vectors_ref.mid_before_ref, bf16[6,256,1024]{2,1,0:T(8,128)(2,1)S(1)} %get-tuple-element.35.hi_ref.refs_2_.refs_1_, ...), custom_call_target="tpu_custom_call" | custom-call | flops 603979776 | bytes 786432 | tf_op jit(solution)/shard_map/first_part/pallas_call | solution.py:208
  9.9 1.8 %collective-permute-start.2 = (f32[64,384]{1,0:T(8,128)S(1)}, f32[64,384]{1,0:T(8,128)S(1)}, u32[]{:S(2)}, u32[]{:S(2)}) collective-permute-start(f32[64,384]{1,0:T(8,128)S(1)} %far_part.1.far_ref.before_ref.far_before_ref), channel_id=1, source_target_pairs={{0,24},{8,16},{16,8},{24,0},{1,25},{9,17},{17,9},{25,1},{2,26},{10... | collective-permute-start | bytes 294920 | tf_op jit(solution)/shard_map/ppermute | solution.py:343
  11.6 1.5 %collective-permute-start.7 = (f32[192,128]{1,0:T(8,128)S(1)}, f32[192,128]{1,0:T(8,128)S(1)}, u32[]{:S(2)}, u32[]{:S(2)}) collective-permute-start(f32[192,128]{1,0:T(8,128)S(1)} %collective-permute-done.6.mine_ref), channel_id=1, source_target_pairs={{0,1},{1,0},{2,3},{3,2},{4,5},{5,4},{6,7},{7,6},{8,9},{9,8},{10,11... | collective-permute-start | bytes 294920 | tf_op jit(solution)/shard_map/ppermute | solution.py:347
  13.2 1.7 %local_part.4.mid_ref = f32[64,1536]{1,0:T(8,128)S(1)} custom-call(f32[2,256]{1,0:T(2,128)S(1)} %concatenate.12.terms_ref, f32[64,384]{1,0:T(8,128)S(1)} %far_part.1.far_ref.before_ref.far_before_ref, f32[64,1536]{1,0:T(8,128)S(1)} %first_part.1.mid_ref.mid_before_ref, f32[64,384]{1,0:T(8,128)S(1)} %near_part.8.near_ref.near_before_ref, ...), custom_call_target="tpu_custom_call" | custom-call | flops 150994944 | bytes 196608 | tf_op jit(solution)/shard_map/local_part/pallas_call | solution.py:208
  15.4 0.8 turn_one.1
  16.2 1.5 %collective-permute-start.5 = (f32[2,64,384]{2,1,0:T(8,128)S(1)}, f32[2,64,384]{2,1,0:T(8,128)S(1)}, u32[]{:S(2)}, u32[]{:S(2)}) collective-permute-start(f32[2,64,384]{2,1,0:T(8,128)S(1)} %get-tuple-element.42.sent_ref), channel_id=1, source_target_pairs={{0,24},{8,16},{16,8},{24,0},{1,25},{9,17},{17,9},{25,1},{2,26},{10... | collective-permute-start | bytes 589832 | tf_op jit(solution)/shard_map/ppermute | solution.py:343
  17.6 1.6 %collective-permute-start.8 = (f32[384,128]{1,0:T(8,128)S(1)}, f32[384,128]{1,0:T(8,128)S(1)}, u32[]{:S(2)}, u32[]{:S(2)}) collective-permute-start(f32[384,128]{1,0:T(8,128)S(1)} %pad_maximum_fusion.1), channel_id=1, source_target_pairs={{0,2},{1,3},{2,0},{3,1},{4,6},{5,7},{6,4},{7,5},{8,10},{9,11},{10,... | collective-permute-start | bytes 589832 | tf_op jit(solution)/shard_map/ppermute | solution.py:347
  19.3 1.5 %local_part.5 = (f32[64,1536]{1,0:T(8,128)S(1)}, f32[64,1536]{1,0:T(8,128)S(1)}) custom-call(f32[2,256]{1,0:T(2,128)S(1)} %concatenate.12.terms_ref, f32[64,768]{1,0:T(8,128)S(1)} %get-tuple-element.39.far_ref, f32[64,1536]{1,0:T(8,128)S(1)} %local_part.4.mid_ref, f32[64,384]{1,0:T(8,128)S(1)} %near_part.9.near_ref, ...), custom_call_target="tpu_custom_call" | custom-call | flops 301989888 | bytes 393216 | tf_op jit(solution)/shard_map/local_part/pallas_call | solution.py:208
  21.2 1.4 %second_part.3.mid_ref = f32[64,1536]{1,0:T(8,128)S(1)} custom-call(f32[2,256]{1,0:T(2,128)S(1)} %concatenate.12.terms_ref, f32[64,1536]{1,0:T(8,128)S(1)} %get-tuple-element.40.mid_ref.mid_before_ref, f32[64,384]{1,0:T(8,128)S(1)} %near_part.10.near_ref.near_before_ref, f32[64,1536]{1,0:T(8,128)S(1)} %get-tuple-element.41.before_ref, ...), custom_call_target="tpu_custom_call" | custom-call | flops 603979776 | bytes 786432 | tf_op jit(solution)/shard_map/second_part/pallas_call | solution.py:208
  22.9 0.6 collective-permute-start.10
  23.4 1.1 %collective-permute-done.8.two_ref = f32[384,128]{1,0:T(8,128)S(1)} collective-permute-done((f32[384,128]{1,0:T(8,128)S(1)}, f32[384,128]{1,0:T(8,128)S(1)}, u32[]{:S(2)}, u32[]{:S(2)}) %collective-permute-start.8) | collective-permute-done | bytes 196640 | tf_op jit(solution)/shard_map/ppermute | solution.py:347
  24.7 1.4 %turn_two.2 = (f32[64,384]{1,0:T(8,128)S(1)}, f32[64,768]{1,0:T(8,128)S(1)}, f32[2,64,384]{2,1,0:T(8,128)S(1)}) custom-call(f32[2,256]{1,0:T(2,128)S(1)} %concatenate.12.terms_ref, f32[64,1536]{1,0:T(8,128)S(1)} %second_part.3.mid_ref, f32[2,64,384]{2,1,0:T(8,128)S(1)} %get-tuple-element.42.sent_ref, f32[2,64,384]{2,1,0:T(8,128)S(1)} %collective-permute-done.5.got_ref, ...), custom_call_target="tpu_custom_call" | custom-call | flops 603979776 | bytes 786432 | tf_op jit(solution)/shard_map/turn_two/pallas_call | solution.py:208
  26.1 1.5 %local_part.6 = (f32[64,1536]{1,0:T(8,128)S(1)}, f32[64,1536]{1,0:T(8,128)S(1)}) custom-call(f32[2,256]{1,0:T(2,128)S(1)} %concatenate.12.terms_ref, f32[64,768]{1,0:T(8,128)S(1)} %get-tuple-element.46.far_ref, f32[64,1536]{1,0:T(8,128)S(1)} %second_part.3.mid_ref, f32[64,384]{1,0:T(8,128)S(1)} %near_part.11.near_ref, ...), custom_call_target="tpu_custom_call" | custom-call | flops 301989888 | bytes 393216 | tf_op jit(solution)/shard_map/local_part/pallas_call | solution.py:208
  27.9 0.8 collective-permute-start.12
  28.8 1.4 %second_part.4.mid_ref = f32[64,1536]{1,0:T(8,128)S(1)} custom-call(f32[2,256]{1,0:T(2,128)S(1)} %concatenate.12.terms_ref, f32[64,1536]{1,0:T(8,128)S(1)} %get-tuple-element.48.mid_ref.mid_before_ref, f32[64,384]{1,0:T(8,128)S(1)} %near_part.12.near_ref.near_before_ref, f32[64,1536]{1,0:T(8,128)S(1)} %get-tuple-element.49.before_ref, ...), custom_call_target="tpu_custom_call" | custom-call | flops 603979776 | bytes 786432 | tf_op jit(solution)/shard_map/second_part/pallas_call | solution.py:208
  30.9 1.9 %collective-permute-done.11.got_ref = f32[2,64,384]{2,1,0:T(8,128)S(1)} collective-permute-done((f32[2,64,384]{2,1,0:T(8,128)S(1)}, f32[2,64,384]{2,1,0:T(8,128)S(1)}, u32[]{:S(2)}, u32[]{:S(2)}) %collective-permute-start.11) | collective-permute-done | bytes 196640 | tf_op jit(solution)/shard_map/ppermute | solution.py:343
  32.8 1.2 %turn_two.3 = (f32[64,384]{1,0:T(8,128)S(1)}, f32[64,768]{1,0:T(8,128)S(1)}, f32[2,64,384]{2,1,0:T(8,128)S(1)}) custom-call(f32[2,256]{1,0:T(2,128)S(1)} %concatenate.12.terms_ref, f32[64,1536]{1,0:T(8,128)S(1)} %second_part.4.mid_ref, f32[2,64,384]{2,1,0:T(8,128)S(1)} %get-tuple-element.50.sent_ref, f32[2,64,384]{2,1,0:T(8,128)S(1)} %collective-permute-done.11.got_ref, ...), custom_call_target="tpu_custom_call" | custom-call | flops 603979776 | bytes 786432 | tf_op jit(solution)/shard_map/turn_two/pallas_call | solution.py:208
  34.0 0.8 collective-permute-start.14
  34.8 1.5 %local_part.7 = (f32[64,1536]{1,0:T(8,128)S(1)}, f32[64,1536]{1,0:T(8,128)S(1)}) custom-call(f32[2,256]{1,0:T(2,128)S(1)} %concatenate.12.terms_ref, f32[64,768]{1,0:T(8,128)S(1)} %get-tuple-element.51.far_ref, f32[64,1536]{1,0:T(8,128)S(1)} %second_part.4.mid_ref, f32[64,384]{1,0:T(8,128)S(1)} %near_part.13.near_ref, ...), custom_call_target="tpu_custom_call" | custom-call | flops 301989888 | bytes 393216 | tf_op jit(solution)/shard_map/local_part/pallas_call | solution.py:208
  36.6 0.6 collective-permute-start.15
  37.5 1.6 %second_part.5.mid_ref = f32[64,1536]{1,0:T(8,128)S(1)} custom-call(f32[2,256]{1,0:T(2,128)S(1)} %concatenate.12.terms_ref, f32[64,1536]{1,0:T(8,128)S(1)} %get-tuple-element.53.mid_ref, f32[64,384]{1,0:T(8,128)S(1)} %near_part.14.near_ref, f32[64,1536]{1,0:T(8,128)S(1)} %get-tuple-element.54.before_ref, ...), custom_call_target="tpu_custom_call" | custom-call | flops 603979776 | bytes 786432 | tf_op jit(solution)/shard_map/second_part/pallas_call | solution.py:208
  39.4 1.7 %collective-permute-done.14.got_ref = f32[2,64,384]{2,1,0:T(8,128)S(1)} collective-permute-done((f32[2,64,384]{2,1,0:T(8,128)S(1)}, f32[2,64,384]{2,1,0:T(8,128)S(1)}, u32[]{:S(2)}, u32[]{:S(2)}) %collective-permute-start.14) | collective-permute-done | bytes 196640 | tf_op jit(solution)/shard_map/ppermute | solution.py:343
  41.0 0.8 last_part.1
  41.9 17.7 %all_to_all.5.parts_ref = f32[8,96,128]{2,1,0:T(8,128)S(1)} all-to-all(f32[8,96,128]{2,1,0:T(8,128)S(1)} %last_part.1), channel_id=1, replica_groups=mesh['narrow'=4,'wide'=8] {'wide'}, dimensions={0} | all-to-all | bytes 786432 | tf_op jit(solution)/shard_map/all_to_all | solution.py:669
  59.6 0.7 gram.1
  60.4 1.6 %collective-permute-done.16.refs_1_ = f32[576,128]{1,0:T(8,128)S(1)} collective-permute-done((f32[576,128]{1,0:T(8,128)S(1)}, f32[576,128]{1,0:T(8,128)S(1)}, u32[]{:S(2)}, u32[]{:S(2)}) %collective-permute-start.16) | collective-permute-done | bytes 294944 | tf_op jit(solution)/shard_map/ppermute | solution.py:411
  62.0 1.3 %collective-permute-start.17 = (f32[144,128]{1,0:T(8,128)S(1)}, f32[144,128]{1,0:T(8,128)S(1)}, u32[]{:S(2)}, u32[]{:S(2)}) collective-permute-start(f32[144,128]{1,0:T(8,128)S(1)} %get-tuple-element.59), channel_id=1, source_target_pairs={{0,16},{1,17},{2,18},{3,19},{4,20},{5,21},{6,22},{7,23},{8,24},{9,... | collective-permute-start | bytes 221192 | tf_op jit(solution)/shard_map/ppermute | solution.py:411
  63.3 1.1 %collective-permute-start.18 = (f32[144,128]{1,0:T(8,128)S(1)}, f32[144,128]{1,0:T(8,128)S(1)}, u32[]{:S(2)}, u32[]{:S(2)}) collective-permute-start(f32[144,128]{1,0:T(8,128)S(1)} %get-tuple-element.60), channel_id=1, source_target_pairs={{0,1},{1,0},{2,3},{3,2},{4,5},{5,4},{6,7},{7,6},{8,9},{9,8},{10,11... | collective-permute-start | bytes 221192 | tf_op jit(solution)/shard_map/ppermute | solution.py:411
  64.4 1.2 %collective-permute-start.19 = (f32[144,128]{1,0:T(8,128)S(1)}, f32[144,128]{1,0:T(8,128)S(1)}, u32[]{:S(2)}, u32[]{:S(2)}) collective-permute-start(f32[144,128]{1,0:T(8,128)S(1)} %get-tuple-element.61), channel_id=1, source_target_pairs={{0,17},{1,16},{2,19},{3,18},{4,21},{5,20},{6,23},{7,22},{8,25},{9,... | collective-permute-start | bytes 221192 | tf_op jit(solution)/shard_map/ppermute | solution.py:411
  65.6 0.9 collective-permute-done.17
  66.4 2.0 %collective-permute-done.18 = f32[144,128]{1,0:T(8,128)S(1)} collective-permute-done((f32[144,128]{1,0:T(8,128)S(1)}, f32[144,128]{1,0:T(8,128)S(1)}, u32[]{:S(2)}, u32[]{:S(2)}) %collective-permute-start.18) | collective-permute-done | bytes 73760 | tf_op jit(solution)/shard_map/ppermute | solution.py:411
  68.5 1.2 %collective-permute-done.19 = f32[144,128]{1,0:T(8,128)S(1)} collective-permute-done((f32[144,128]{1,0:T(8,128)S(1)}, f32[144,128]{1,0:T(8,128)S(1)}, u32[]{:S(2)}, u32[]{:S(2)}) %collective-permute-start.19) | collective-permute-done | bytes 73760 | tf_op jit(solution)/shard_map/ppermute | solution.py:411
  69.7 0.5 collective-permute-start.20
  70.2 1.6 %collective-permute-start.21 = (f32[144,128]{1,0:T(8,128)S(1)}, f32[144,128]{1,0:T(8,128)S(1)}, u32[]{:S(2)}, u32[]{:S(2)}) collective-permute-start(f32[144,128]{1,0:T(8,128)S(1)} %add_add_fusion.1), channel_id=1, source_target_pairs={{0,4},{1,5},{2,6},{3,7},{4,0},{5,1},{6,2},{7,3},{8,12},{9,13},{10,... | collective-permute-start | bytes 221192 | tf_op jit(solution)/shard_map/ppermute | solution.py:411
  71.8 2.4 %collective-permute-start.22 = (f32[144,128]{1,0:T(8,128)S(1)}, f32[144,128]{1,0:T(8,128)S(1)}, u32[]{:S(2)}, u32[]{:S(2)}) collective-permute-start(f32[144,128]{1,0:T(8,128)S(1)} %add_add_fusion.1), channel_id=1, source_target_pairs={{0,6},{1,7},{2,4},{3,5},{4,2},{5,3},{6,0},{7,1},{8,14},{9,15},{10,... | collective-permute-start | bytes 221192 | tf_op jit(solution)/shard_map/ppermute | solution.py:411
  74.1 2.7 %collective-permute-done.21 = f32[144,128]{1,0:T(8,128)S(1)} collective-permute-done((f32[144,128]{1,0:T(8,128)S(1)}, f32[144,128]{1,0:T(8,128)S(1)}, u32[]{:S(2)}, u32[]{:S(2)}) %collective-permute-start.21) | collective-permute-done | bytes 73760 | tf_op jit(solution)/shard_map/ppermute | solution.py:411
  76.8 1.2 %collective-permute-done.22 = f32[144,128]{1,0:T(8,128)S(1)} collective-permute-done((f32[144,128]{1,0:T(8,128)S(1)}, f32[144,128]{1,0:T(8,128)S(1)}, u32[]{:S(2)}, u32[]{:S(2)}) %collective-permute-start.22) | collective-permute-done | bytes 73760 | tf_op jit(solution)/shard_map/ppermute | solution.py:411
  78.1 0.9 collective-permute-start.23
  78.9 0.8 collective-permute-start.24
  79.7 1.9 %collective-permute-start.25 = (f32[144,128]{1,0:T(8,128)S(1)}, f32[144,128]{1,0:T(8,128)S(1)}, u32[]{:S(2)}, u32[]{:S(2)}) collective-permute-start(f32[144,128]{1,0:T(8,128)S(1)} %add_add_fusion), channel_id=1, source_target_pairs={{0,17},{1,16},{2,19},{3,18},{4,21},{5,20},{6,23},{7,22},{8,25},{9,... | collective-permute-start | bytes 221192 | tf_op jit(solution)/shard_map/ppermute | solution.py:411
  81.6 0.9 collective-permute-done.23
  82.5 0.8 collective-permute-done.24
  83.3 1.7 %collective-permute-done.25 = f32[144,128]{1,0:T(8,128)S(1)} collective-permute-done((f32[144,128]{1,0:T(8,128)S(1)}, f32[144,128]{1,0:T(8,128)S(1)}, u32[]{:S(2)}, u32[]{:S(2)}) %collective-permute-start.25) | collective-permute-done | bytes 73760 | tf_op jit(solution)/shard_map/ppermute | solution.py:411
  85.3 1.4 %collective-permute-done.26.other_ref = f32[576,128]{1,0:T(8,128)S(1)} collective-permute-done((f32[576,128]{1,0:T(8,128)S(1)}, f32[576,128]{1,0:T(8,128)S(1)}, u32[]{:S(2)}, u32[]{:S(2)}) %collective-permute-start.26) | collective-permute-done | bytes 294944 | tf_op jit(solution)/shard_map/ppermute | solution.py:411
  86.7 1.6 %rotate.1 = f32[192,512]{1,0:T(8,128)} custom-call(f32[576,128]{1,0:T(8,128)S(1)} %pad_maximum_fusion.own_ref, f32[576,128]{1,0:T(8,128)S(1)} %collective-permute-done.26.other_ref, f32[192,512]{1,0:T(8,128)S(1)} %turned.1.rows_ref), custom_call_target="tpu_custom_call" | custom-call | tf_op jit(solution)/shard_map/rotate/pallas_call | solution.py:649
  (42 shorter events, 4.3 us)
Async XLA Ops:
  2.8 6.3 %collective-permute-start.1 = (f32[64,384]{1,0:T(8,128)S(1)}, f32[64,384]{1,0:T(8,128)S(1)}, u32[]{:S(2)}, u32[]{:S(2)}) collective-permute-start(f32[64,384]{1,0:T(8,128)S(1)} %get-tuple-element.38.near_before_ref), channel_id=1, source_target_pairs={{0,8},{8,0},{16,24},{24,16},{1,9},{9,1},{17,25},{25,17},{2,10},{10... | collective-permute-start | bytes 294920 | tf_op jit(solution)/shard_map/ppermute | solution.py:351
  3.3 6.2 %collective-permute-start = (f32[64,384]{1,0:T(8,128)S(1)}, f32[64,384]{1,0:T(8,128)S(1)}, u32[]{:S(2)}, u32[]{:S(2)}) collective-permute-start(f32[64,384]{1,0:T(8,128)S(1)} %get-tuple-element.37.far_before_ref), channel_id=1, source_target_pairs={{0,24},{8,16},{16,8},{24,0},{1,25},{9,17},{17,9},{25,1},{2,26},{10... | collective-permute-start | bytes 294920 | tf_op jit(solution)/shard_map/ppermute | solution.py:343
  6.0 5.7 %collective-permute-start.6 = (f32[192,128]{1,0:T(8,128)S(1)}, f32[192,128]{1,0:T(8,128)S(1)}, u32[]{:S(2)}, u32[]{:S(2)}) collective-permute-start(f32[192,128]{1,0:T(8,128)S(1)} %get-tuple-element.43), channel_id=1, source_target_pairs={{0,24},{8,16},{16,8},{24,0},{1,25},{9,17},{17,9},{25,1},{2,26},{10... | collective-permute-start | bytes 294920 | tf_op jit(solution)/shard_map/ppermute | solution.py:343
  9.4 5.5 %collective-permute-start.3 = (f32[64,384]{1,0:T(8,128)S(1)}, f32[64,384]{1,0:T(8,128)S(1)}, u32[]{:S(2)}, u32[]{:S(2)}) collective-permute-start(f32[64,384]{1,0:T(8,128)S(1)} %near_part.8.near_ref.near_before_ref), channel_id=1, source_target_pairs={{0,8},{8,0},{16,24},{24,16},{1,9},{9,1},{17,25},{25,17},{2,10},{10... | collective-permute-start | bytes 294920 | tf_op jit(solution)/shard_map/ppermute | solution.py:351
  9.9 5.5 %collective-permute-start.2 = (f32[64,384]{1,0:T(8,128)S(1)}, f32[64,384]{1,0:T(8,128)S(1)}, u32[]{:S(2)}, u32[]{:S(2)}) collective-permute-start(f32[64,384]{1,0:T(8,128)S(1)} %far_part.1.far_ref.before_ref.far_before_ref), channel_id=1, source_target_pairs={{0,24},{8,16},{16,8},{24,0},{1,25},{9,17},{17,9},{25,1},{2,26},{10... | collective-permute-start | bytes 294920 | tf_op jit(solution)/shard_map/ppermute | solution.py:343
  11.6 6.0 %collective-permute-start.7 = (f32[192,128]{1,0:T(8,128)S(1)}, f32[192,128]{1,0:T(8,128)S(1)}, u32[]{:S(2)}, u32[]{:S(2)}) collective-permute-start(f32[192,128]{1,0:T(8,128)S(1)} %collective-permute-done.6.mine_ref), channel_id=1, source_target_pairs={{0,1},{1,0},{2,3},{3,2},{4,5},{5,4},{6,7},{7,6},{8,9},{9,8},{10,11... | collective-permute-start | bytes 294920 | tf_op jit(solution)/shard_map/ppermute | solution.py:347
  15.2 5.6 %collective-permute-start.4 = (f32[64,384]{1,0:T(8,128)S(1)}, f32[64,384]{1,0:T(8,128)S(1)}, u32[]{:S(2)}, u32[]{:S(2)}) collective-permute-start(f32[64,384]{1,0:T(8,128)S(1)} %near_part.9.near_ref), channel_id=1, source_target_pairs={{0,8},{8,0},{16,24},{24,16},{1,9},{9,1},{17,25},{25,17},{2,10},{10... | collective-permute-start | bytes 294920 | tf_op jit(solution)/shard_map/ppermute | solution.py:351
  16.2 8.5 %collective-permute-start.5 = (f32[2,64,384]{2,1,0:T(8,128)S(1)}, f32[2,64,384]{2,1,0:T(8,128)S(1)}, u32[]{:S(2)}, u32[]{:S(2)}) collective-permute-start(f32[2,64,384]{2,1,0:T(8,128)S(1)} %get-tuple-element.42.sent_ref), channel_id=1, source_target_pairs={{0,24},{8,16},{16,8},{24,0},{1,25},{9,17},{17,9},{25,1},{2,26},{10... | collective-permute-start | bytes 589832 | tf_op jit(solution)/shard_map/ppermute | solution.py:343
  17.6 7.0 %collective-permute-start.8 = (f32[384,128]{1,0:T(8,128)S(1)}, f32[384,128]{1,0:T(8,128)S(1)}, u32[]{:S(2)}, u32[]{:S(2)}) collective-permute-start(f32[384,128]{1,0:T(8,128)S(1)} %pad_maximum_fusion.1), channel_id=1, source_target_pairs={{0,2},{1,3},{2,0},{3,1},{4,6},{5,7},{6,4},{7,5},{8,10},{9,11},{10,... | collective-permute-start | bytes 589832 | tf_op jit(solution)/shard_map/ppermute | solution.py:347
  21.1 1.5 %collective-permute-start.9 = (f32[64,384]{1,0:T(8,128)S(1)}, f32[64,384]{1,0:T(8,128)S(1)}, u32[]{:S(2)}, u32[]{:S(2)}) collective-permute-start(f32[64,384]{1,0:T(8,128)S(1)} %near_part.10.near_ref.near_before_ref), channel_id=1, source_target_pairs={{0,8},{8,0},{16,24},{24,16},{1,9},{9,1},{17,25},{25,17},{2,10},{10... | collective-permute-start | bytes 294920 | tf_op jit(solution)/shard_map/ppermute | solution.py:351
  22.9 4.8 %collective-permute-start.10 = (f32[64,384]{1,0:T(8,128)S(1)}, f32[64,384]{1,0:T(8,128)S(1)}, u32[]{:S(2)}, u32[]{:S(2)}) collective-permute-start(f32[64,384]{1,0:T(8,128)S(1)} %near_part.11.near_ref), channel_id=1, source_target_pairs={{0,8},{8,0},{16,24},{24,16},{1,9},{9,1},{17,25},{25,17},{2,10},{10... | collective-permute-start | bytes 294920 | tf_op jit(solution)/shard_map/ppermute | solution.py:351
  26.1 6.7 %collective-permute-start.11 = (f32[2,64,384]{2,1,0:T(8,128)S(1)}, f32[2,64,384]{2,1,0:T(8,128)S(1)}, u32[]{:S(2)}, u32[]{:S(2)}) collective-permute-start(f32[2,64,384]{2,1,0:T(8,128)S(1)} %get-tuple-element.50.sent_ref), channel_id=1, source_target_pairs={{0,24},{8,16},{16,8},{24,0},{1,25},{9,17},{17,9},{25,1},{2,26},{10... | collective-permute-start | bytes 589832 | tf_op jit(solution)/shard_map/ppermute | solution.py:343
  27.9 2.3 %collective-permute-start.12 = (f32[64,384]{1,0:T(8,128)S(1)}, f32[64,384]{1,0:T(8,128)S(1)}, u32[]{:S(2)}, u32[]{:S(2)}) collective-permute-start(f32[64,384]{1,0:T(8,128)S(1)} %near_part.12.near_ref.near_before_ref), channel_id=1, source_target_pairs={{0,8},{8,0},{16,24},{24,16},{1,9},{9,1},{17,25},{25,17},{2,10},{10... | collective-permute-start | bytes 294920 | tf_op jit(solution)/shard_map/ppermute | solution.py:351
  30.5 5.9 %collective-permute-start.13 = (f32[64,384]{1,0:T(8,128)S(1)}, f32[64,384]{1,0:T(8,128)S(1)}, u32[]{:S(2)}, u32[]{:S(2)}) collective-permute-start(f32[64,384]{1,0:T(8,128)S(1)} %near_part.13.near_ref), channel_id=1, source_target_pairs={{0,8},{8,0},{16,24},{24,16},{1,9},{9,1},{17,25},{25,17},{2,10},{10... | collective-permute-start | bytes 294920 | tf_op jit(solution)/shard_map/ppermute | solution.py:351
  34.0 7.0 %collective-permute-start.14 = (f32[2,64,384]{2,1,0:T(8,128)S(1)}, f32[2,64,384]{2,1,0:T(8,128)S(1)}, u32[]{:S(2)}, u32[]{:S(2)}) collective-permute-start(f32[2,64,384]{2,1,0:T(8,128)S(1)} %get-tuple-element.55.sent_ref), channel_id=1, source_target_pairs={{0,24},{8,16},{16,8},{24,0},{1,25},{9,17},{17,9},{25,1},{2,26},{10... | collective-permute-start | bytes 589832 | tf_op jit(solution)/shard_map/ppermute | solution.py:343
  36.6 2.4 %collective-permute-start.15 = (f32[64,384]{1,0:T(8,128)S(1)}, f32[64,384]{1,0:T(8,128)S(1)}, u32[]{:S(2)}, u32[]{:S(2)}) collective-permute-start(f32[64,384]{1,0:T(8,128)S(1)} %near_part.14.near_ref), channel_id=1, source_target_pairs={{0,8},{8,0},{16,24},{24,16},{1,9},{9,1},{17,25},{25,17},{2,10},{10... | collective-permute-start | bytes 294920 | tf_op jit(solution)/shard_map/ppermute | solution.py:351
  60.3 1.6 %collective-permute-start.16 = (f32[576,128]{1,0:T(8,128)S(1)}, f32[576,128]{1,0:T(8,128)S(1)}, u32[]{:S(2)}, u32[]{:S(2)}) collective-permute-start(f32[576,128]{1,0:T(8,128)S(1)} %get-tuple-element.57), channel_id=1, source_target_pairs={{0,8},{1,9},{2,10},{3,11},{4,12},{5,13},{6,14},{7,15},{8,0},{9,1},... | collective-permute-start | bytes 884744 | tf_op jit(solution)/shard_map/ppermute | solution.py:411
  62.0 4.4 %collective-permute-start.17 = (f32[144,128]{1,0:T(8,128)S(1)}, f32[144,128]{1,0:T(8,128)S(1)}, u32[]{:S(2)}, u32[]{:S(2)}) collective-permute-start(f32[144,128]{1,0:T(8,128)S(1)} %get-tuple-element.59), channel_id=1, source_target_pairs={{0,16},{1,17},{2,18},{3,19},{4,20},{5,21},{6,22},{7,23},{8,24},{9,... | collective-permute-start | bytes 221192 | tf_op jit(solution)/shard_map/ppermute | solution.py:411
  63.3 5.1 %collective-permute-start.18 = (f32[144,128]{1,0:T(8,128)S(1)}, f32[144,128]{1,0:T(8,128)S(1)}, u32[]{:S(2)}, u32[]{:S(2)}) collective-permute-start(f32[144,128]{1,0:T(8,128)S(1)} %get-tuple-element.60), channel_id=1, source_target_pairs={{0,1},{1,0},{2,3},{3,2},{4,5},{5,4},{6,7},{7,6},{8,9},{9,8},{10,11... | collective-permute-start | bytes 221192 | tf_op jit(solution)/shard_map/ppermute | solution.py:411
  64.4 5.3 %collective-permute-start.19 = (f32[144,128]{1,0:T(8,128)S(1)}, f32[144,128]{1,0:T(8,128)S(1)}, u32[]{:S(2)}, u32[]{:S(2)}) collective-permute-start(f32[144,128]{1,0:T(8,128)S(1)} %get-tuple-element.61), channel_id=1, source_target_pairs={{0,17},{1,16},{2,19},{3,18},{4,21},{5,20},{6,23},{7,22},{8,25},{9,... | collective-permute-start | bytes 221192 | tf_op jit(solution)/shard_map/ppermute | solution.py:411
  69.7 4.5 %collective-permute-start.20 = (f32[144,128]{1,0:T(8,128)S(1)}, f32[144,128]{1,0:T(8,128)S(1)}, u32[]{:S(2)}, u32[]{:S(2)}) collective-permute-start(f32[144,128]{1,0:T(8,128)S(1)} %add_add_fusion.1), channel_id=1, source_target_pairs={{0,2},{1,3},{2,0},{3,1},{4,6},{5,7},{6,4},{7,5},{8,10},{9,11},{10,... | collective-permute-start | bytes 221192 | tf_op jit(solution)/shard_map/ppermute | solution.py:411
  70.2 6.7 %collective-permute-start.21 = (f32[144,128]{1,0:T(8,128)S(1)}, f32[144,128]{1,0:T(8,128)S(1)}, u32[]{:S(2)}, u32[]{:S(2)}) collective-permute-start(f32[144,128]{1,0:T(8,128)S(1)} %add_add_fusion.1), channel_id=1, source_target_pairs={{0,4},{1,5},{2,6},{3,7},{4,0},{5,1},{6,2},{7,3},{8,12},{9,13},{10,... | collective-permute-start | bytes 221192 | tf_op jit(solution)/shard_map/ppermute | solution.py:411
  71.8 6.3 %collective-permute-start.22 = (f32[144,128]{1,0:T(8,128)S(1)}, f32[144,128]{1,0:T(8,128)S(1)}, u32[]{:S(2)}, u32[]{:S(2)}) collective-permute-start(f32[144,128]{1,0:T(8,128)S(1)} %add_add_fusion.1), channel_id=1, source_target_pairs={{0,6},{1,7},{2,4},{3,5},{4,2},{5,3},{6,0},{7,1},{8,14},{9,15},{10,... | collective-permute-start | bytes 221192 | tf_op jit(solution)/shard_map/ppermute | solution.py:411
  78.1 4.4 %collective-permute-start.23 = (f32[144,128]{1,0:T(8,128)S(1)}, f32[144,128]{1,0:T(8,128)S(1)}, u32[]{:S(2)}, u32[]{:S(2)}) collective-permute-start(f32[144,128]{1,0:T(8,128)S(1)} %add_add_fusion), channel_id=1, source_target_pairs={{0,16},{1,17},{2,18},{3,19},{4,20},{5,21},{6,22},{7,23},{8,24},{9,... | collective-permute-start | bytes 221192 | tf_op jit(solution)/shard_map/ppermute | solution.py:411
  78.9 4.4 %collective-permute-start.24 = (f32[144,128]{1,0:T(8,128)S(1)}, f32[144,128]{1,0:T(8,128)S(1)}, u32[]{:S(2)}, u32[]{:S(2)}) collective-permute-start(f32[144,128]{1,0:T(8,128)S(1)} %add_add_fusion), channel_id=1, source_target_pairs={{0,1},{1,0},{2,3},{3,2},{4,5},{5,4},{6,7},{7,6},{8,9},{9,8},{10,11... | collective-permute-start | bytes 221192 | tf_op jit(solution)/shard_map/ppermute | solution.py:411
  79.7 5.3 %collective-permute-start.25 = (f32[144,128]{1,0:T(8,128)S(1)}, f32[144,128]{1,0:T(8,128)S(1)}, u32[]{:S(2)}, u32[]{:S(2)}) collective-permute-start(f32[144,128]{1,0:T(8,128)S(1)} %add_add_fusion), channel_id=1, source_target_pairs={{0,17},{1,16},{2,19},{3,18},{4,21},{5,20},{6,23},{7,22},{8,25},{9,... | collective-permute-start | bytes 221192 | tf_op jit(solution)/shard_map/ppermute | solution.py:411
  85.0 1.6 %collective-permute-start.26 = (f32[576,128]{1,0:T(8,128)S(1)}, f32[576,128]{1,0:T(8,128)S(1)}, u32[]{:S(2)}, u32[]{:S(2)}) collective-permute-start(f32[576,128]{1,0:T(8,128)S(1)} %pad_maximum_fusion.own_ref), channel_id=1, source_target_pairs={{0,8},{1,9},{2,10},{3,11},{4,12},{5,13},{6,14},{7,15},{8,0},{9,1},... | collective-permute-start | bytes 884744 | tf_op jit(solution)/shard_map/ppermute | solution.py:411

commit v4 on v3

--- a/solution.py
+++ b/solution.py
@@ -55,16 +55,19 @@
     return sum(REACH - r for r in range(row)) + place + REACH - row
 
 
-def spread_kernel(total_blocks, columns_hbm, vectors_hbm, blocks_hbm, far_ref, near_ref, vectors_ref, part_ref, hi_ref, lo_ref, held, cross_ref, columns_ref, sem, vector_sems, row_sems):
+def spread_kernel(total_blocks, columns_hbm, vectors_hbm, blocks_hbm, far_ref, near_ref, vectors_ref, part_ref, hi_ref, lo_ref, held, straight, cross_ref, columns_ref, sems, pair_sems):
     rows, slots, size, _ = blocks_hbm.shape
     edge = far_ref.shape[1]
     odd = odd_device()
     source = [jnp.where(odd, rows - 1 - row, row) for row in range(rows)]
-    copies = [pltpu.make_async_copy(columns_hbm, columns_ref, sem)]
-    for row in range(rows):
-        here = vectors_hbm.at[:, pl.ds(pl.multiple_of(source[row] * size, size), size)]
-        copies.append(pltpu.make_async_copy(here, vectors_ref.at[:, pl.ds(row * size, size)], vector_sems.at[row]))
-    large = [pltpu.make_async_copy(blocks_hbm.at[source[row]], held.at[row], row_sems.at[row]) for row in range(rows)]
+    copies = [
+        pltpu.make_async_copy(columns_hbm, columns_ref, sems.at[0]),
+        pltpu.make_async_copy(vectors_hbm, straight, sems.at[1]),
+    ]
+    large = []
+    for pair in range(rows // 2):
+        begin = jnp.where(odd, rows - 2 - 2 * pair, 2 * pair)
+        large.append(pltpu.make_async_copy(blocks_hbm.at[pl.ds(begin, 2)], held.at[pl.ds(2 * pair, 2)], pair_sems.at[pair]))
     for copy in copies + large:
         copy.start()
     hi_ref[...] = jnp.zeros_like(hi_ref)
@@ -73,15 +76,18 @@
     first = lax.axis_index("narrow") * rows
     copies[0].wait()
     for row in range(rows):
-        large[row].wait()
         pair, half = divmod(row, 2)
+        if half == 0:
+            large[pair].wait()
+        place = 2 * pair + jnp.where(odd, 1 - half, half)
         here = slice(half * size, half * size + size)
         for slot in range(slots):
             offset = columns_ref[slot, source[row]] - (first + source[row])
             offset = jnp.where(offset > REACH, offset - total_blocks, offset)
             offset = jnp.where(offset < -REACH, offset + total_blocks, offset)
             offset = jnp.where(odd, -offset, offset)
-            hi, lo = split(held[row, slot])
+            block = held[place, slot]
+            hi, lo = split(block)
             there = pl.ds(pl.multiple_of((half + offset + REACH) * size, size), size)
             hi_ref[pair, here, there] = hi
             lo_ref[pair, here, there] = lo
@@ -90,12 +96,13 @@
                 @pl.when(row + offset < 0)
                 def _():
                     at = pl.multiple_of(cross_at(row, row + offset) * size, size)
-                    cross_ref[pl.ds(at, size), :] = held[row, slot]
+                    cross_ref[pl.ds(at, size), :] = block
 
     count = part_ref.shape[0]
     part_ref[...] = cross_ref[pl.ds(pl.multiple_of(lax.rem(lax.axis_index("wide"), CROSS_PARTS) * count, 8), count), :]
-    for copy in copies[1:]:
-        copy.wait()
+    copies[1].wait()
+    whole = straight[...]
+    vectors_ref[...] = jnp.where(odd, jnp.concatenate(reversed_blocks(whole, size), axis=1), whole)
     far_ref[...] = vectors_ref[:, :edge]
     near_ref[...] = vectors_ref[:, -edge:]
 
@@ -113,11 +120,11 @@
         out_shape=[edge, edge, jax.ShapeDtypeStruct(vectors.shape, F32), cross, spread, spread],
         scratch_shapes=[
             pltpu.VMEM(blocks.shape, F32),
+            pltpu.VMEM(vectors.shape, F32),
             pltpu.VMEM((crossing, size), F32),
             pltpu.SMEM((slots, rows), jnp.int32),
-            pltpu.SemaphoreType.DMA,
-            pltpu.SemaphoreType.DMA((rows,)),
-            pltpu.SemaphoreType.DMA((rows,)),
+            pltpu.SemaphoreType.DMA((2,)),
+            pltpu.SemaphoreType.DMA((rows // 2,)),
         ],
         compiler_params=params(),
         name="spread_part",

time: 88.6 us -> 88.4 us (level)
  no operation moved by 1% of the time
where the time goes in v4:
time: 88.4 us; the launch traced here: 88.1 us
  Pallas kernels  24.6 us (28%)
  starting transfers between devices  24.5 us (28%)
  waiting for transfers between devices  19.4 us (22%)
  blocking collectives  17.5 us (20%)
  between operations  2.02 us (2%)
    pallas_call x23, Pallas kernels, step_call(): pl.pallas_call(kernel, in_specs=[VM] * (len(operands) + 2), out_specs=[VM...  19.4 us
    all_to_all x1, blocking collectives, regroup(): lax.all_to_all(parts, 'wide', split_axis=0, concat_axis=0, tiled=True)  17.5 us
    ppermute x11, waiting for transfers between devices, swap(): return lax.ppermute(x, ('narrow', 'wide'), pair_perm(mask))  14.3 us
    ppermute x11, starting transfers between devices, swap(): return lax.ppermute(x, ('narrow', 'wide'), pair_perm(mask))  11.7 us
    ppermute x6, starting transfers between devices, far_swap(): lax.ppermute(x, 'narrow', [(i, (i + 1) % size if i % 2 else (i - 1) % siz...  6.71 us
    ppermute x6, waiting for transfers between devices, far_swap(): lax.ppermute(x, 'narrow', [(i, (i + 1) % size if i % 2 else (i - 1) % siz...  3.83 us
    ppermute x2, starting transfers between devices, wide_swap(): lax.ppermute(x, 'wide', [(i, i ^ mask) for i in range(lax.axis_size('wide...  3.18 us
    ppermute x8, starting transfers between devices, near_swap(): lax.ppermute(x, 'narrow', [(i, i ^ 1) for i in range(lax.axis_size('narro...  2.96 us
  transfers between devices with their start and end apart: 27, of which 13 were waited for; matrix products, arithmetic and copies ran while one was open for 0% of the time, Pallas kernels for 21%

profile of v4, /device:TPU:0, one launch (start us, length us, event | category | flops | bytes accessed | tf_op | source)
XLA Modules:
  0.0 88.1 jit_solution(11170784520541501081)
XLA Ops:
  0.0 2.5 %spread_part.1 = (f32[64,384]{1,0:T(8,128)S(1)}, f32[64,384]{1,0:T(8,128)S(1)}, f32[64,1536]{1,0:T(8,128)S(1)}, f32[192,128]{1,0:T(8,128)S(1)}, bf16[6,256,1024]...) custom-call(s32[5,12]{1,0:T(8,128)} %bitcast.3, f32[64,1536]{1,0:T(8,128)} %vectors_hbm.1, f32[12,5,128,128]{3,2,1,0:T(8,128)} %blocks_hbm.1), custom_call_target="tpu_custom_call" | custom-call | tf_op jit(solution)/shard_map/spread_part/pallas_call | solution.py:116
  2.5 0.5 collective-permute-start.1
  3.1 2.6 %collective-permute-start = (f32[64,384]{1,0:T(8,128)S(1)}, f32[64,384]{1,0:T(8,128)S(1)}, u32[]{:S(2)}, u32[]{:S(2)}) collective-permute-start(f32[64,384]{1,0:T(8,128)S(1)} %get-tuple-element.37.far_before_ref), channel_id=1, source_target_pairs={{0,24},{8,16},{16,8},{24,0},{1,25},{9,17},{17,9},{25,1},{2,26},{10... | collective-permute-start | bytes 294920 | tf_op jit(solution)/shard_map/ppermute | solution.py:350
  7.1 1.7 %first_part.1.mid_ref.mid_before_ref = f32[64,1536]{1,0:T(8,128)S(1)} custom-call(f32[2,256]{1,0:T(2,128)S(1)} %concatenate.12.terms_ref, f32[64,1536]{1,0:T(8,128)S(1)} %get-tuple-element.34.vectors_ref.mid_before_ref, bf16[6,256,1024]{2,1,0:T(8,128)(2,1)S(1)} %get-tuple-element.35.hi_ref.refs_2_.refs_1_, ...), custom_call_target="tpu_custom_call" | custom-call | flops 603979776 | bytes 786432 | tf_op jit(solution)/shard_map/first_part/pallas_call | solution.py:215
  9.6 1.8 %collective-permute-start.2 = (f32[64,384]{1,0:T(8,128)S(1)}, f32[64,384]{1,0:T(8,128)S(1)}, u32[]{:S(2)}, u32[]{:S(2)}) collective-permute-start(f32[64,384]{1,0:T(8,128)S(1)} %far_part.1.far_ref.before_ref.far_before_ref), channel_id=1, source_target_pairs={{0,24},{8,16},{16,8},{24,0},{1,25},{9,17},{17,9},{25,1},{2,26},{10... | collective-permute-start | bytes 294920 | tf_op jit(solution)/shard_map/ppermute | solution.py:350
  11.3 1.5 %collective-permute-start.7 = (f32[192,128]{1,0:T(8,128)S(1)}, f32[192,128]{1,0:T(8,128)S(1)}, u32[]{:S(2)}, u32[]{:S(2)}) collective-permute-start(f32[192,128]{1,0:T(8,128)S(1)} %collective-permute-done.6.mine_ref), channel_id=1, source_target_pairs={{0,1},{1,0},{2,3},{3,2},{4,5},{5,4},{6,7},{7,6},{8,9},{9,8},{10,11... | collective-permute-start | bytes 294920 | tf_op jit(solution)/shard_map/ppermute | solution.py:354
  12.9 1.7 %local_part.4.mid_ref = f32[64,1536]{1,0:T(8,128)S(1)} custom-call(f32[2,256]{1,0:T(2,128)S(1)} %concatenate.12.terms_ref, f32[64,384]{1,0:T(8,128)S(1)} %far_part.1.far_ref.before_ref.far_before_ref, f32[64,1536]{1,0:T(8,128)S(1)} %first_part.1.mid_ref.mid_before_ref, f32[64,384]{1,0:T(8,128)S(1)} %near_part.8.near_ref.near_before_ref, ...), custom_call_target="tpu_custom_call" | custom-call | flops 150994944 | bytes 196608 | tf_op jit(solution)/shard_map/local_part/pallas_call | solution.py:215
  15.1 0.8 turn_one.1
  15.9 1.4 %collective-permute-start.5 = (f32[2,64,384]{2,1,0:T(8,128)S(1)}, f32[2,64,384]{2,1,0:T(8,128)S(1)}, u32[]{:S(2)}, u32[]{:S(2)}) collective-permute-start(f32[2,64,384]{2,1,0:T(8,128)S(1)} %get-tuple-element.42.sent_ref), channel_id=1, source_target_pairs={{0,24},{8,16},{16,8},{24,0},{1,25},{9,17},{17,9},{25,1},{2,26},{10... | collective-permute-start | bytes 589832 | tf_op jit(solution)/shard_map/ppermute | solution.py:350
  17.3 1.7 %collective-permute-start.8 = (f32[384,128]{1,0:T(8,128)S(1)}, f32[384,128]{1,0:T(8,128)S(1)}, u32[]{:S(2)}, u32[]{:S(2)}) collective-permute-start(f32[384,128]{1,0:T(8,128)S(1)} %pad_maximum_fusion.1), channel_id=1, source_target_pairs={{0,2},{1,3},{2,0},{3,1},{4,6},{5,7},{6,4},{7,5},{8,10},{9,11},{10,... | collective-permute-start | bytes 589832 | tf_op jit(solution)/shard_map/ppermute | solution.py:354
  19.0 1.5 %local_part.5 = (f32[64,1536]{1,0:T(8,128)S(1)}, f32[64,1536]{1,0:T(8,128)S(1)}) custom-call(f32[2,256]{1,0:T(2,128)S(1)} %concatenate.12.terms_ref, f32[64,768]{1,0:T(8,128)S(1)} %get-tuple-element.39.far_ref, f32[64,1536]{1,0:T(8,128)S(1)} %local_part.4.mid_ref, f32[64,384]{1,0:T(8,128)S(1)} %near_part.9.near_ref, ...), custom_call_target="tpu_custom_call" | custom-call | flops 301989888 | bytes 393216 | tf_op jit(solution)/shard_map/local_part/pallas_call | solution.py:215
  20.8 1.4 %second_part.3.mid_ref = f32[64,1536]{1,0:T(8,128)S(1)} custom-call(f32[2,256]{1,0:T(2,128)S(1)} %concatenate.12.terms_ref, f32[64,1536]{1,0:T(8,128)S(1)} %get-tuple-element.40.mid_ref.mid_before_ref, f32[64,384]{1,0:T(8,128)S(1)} %near_part.10.near_ref.near_before_ref, f32[64,1536]{1,0:T(8,128)S(1)} %get-tuple-element.41.before_ref, ...), custom_call_target="tpu_custom_call" | custom-call | flops 603979776 | bytes 786432 | tf_op jit(solution)/shard_map/second_part/pallas_call | solution.py:215
  22.6 0.6 collective-permute-start.10
  23.1 1.2 %collective-permute-done.8.two_ref = f32[384,128]{1,0:T(8,128)S(1)} collective-permute-done((f32[384,128]{1,0:T(8,128)S(1)}, f32[384,128]{1,0:T(8,128)S(1)}, u32[]{:S(2)}, u32[]{:S(2)}) %collective-permute-start.8) | collective-permute-done | bytes 196640 | tf_op jit(solution)/shard_map/ppermute | solution.py:354
  24.4 1.4 %turn_two.2 = (f32[64,384]{1,0:T(8,128)S(1)}, f32[64,768]{1,0:T(8,128)S(1)}, f32[2,64,384]{2,1,0:T(8,128)S(1)}) custom-call(f32[2,256]{1,0:T(2,128)S(1)} %concatenate.12.terms_ref, f32[64,1536]{1,0:T(8,128)S(1)} %second_part.3.mid_ref, f32[2,64,384]{2,1,0:T(8,128)S(1)} %get-tuple-element.42.sent_ref, f32[2,64,384]{2,1,0:T(8,128)S(1)} %collective-permute-done.5.got_ref, ...), custom_call_target="tpu_custom_call" | custom-call | flops 603979776 | bytes 786432 | tf_op jit(solution)/shard_map/turn_two/pallas_call | solution.py:215
  25.9 1.5 %local_part.6 = (f32[64,1536]{1,0:T(8,128)S(1)}, f32[64,1536]{1,0:T(8,128)S(1)}) custom-call(f32[2,256]{1,0:T(2,128)S(1)} %concatenate.12.terms_ref, f32[64,768]{1,0:T(8,128)S(1)} %get-tuple-element.46.far_ref, f32[64,1536]{1,0:T(8,128)S(1)} %second_part.3.mid_ref, f32[64,384]{1,0:T(8,128)S(1)} %near_part.11.near_ref, ...), custom_call_target="tpu_custom_call" | custom-call | flops 301989888 | bytes 393216 | tf_op jit(solution)/shard_map/local_part/pallas_call | solution.py:215
  27.7 0.8 collective-permute-start.12
  28.5 1.4 %second_part.4.mid_ref = f32[64,1536]{1,0:T(8,128)S(1)} custom-call(f32[2,256]{1,0:T(2,128)S(1)} %concatenate.12.terms_ref, f32[64,1536]{1,0:T(8,128)S(1)} %get-tuple-element.48.mid_ref.mid_before_ref, f32[64,384]{1,0:T(8,128)S(1)} %near_part.12.near_ref.near_before_ref, f32[64,1536]{1,0:T(8,128)S(1)} %get-tuple-element.49.before_ref, ...), custom_call_target="tpu_custom_call" | custom-call | flops 603979776 | bytes 786432 | tf_op jit(solution)/shard_map/second_part/pallas_call | solution.py:215
  30.6 2.0 %collective-permute-done.11.got_ref = f32[2,64,384]{2,1,0:T(8,128)S(1)} collective-permute-done((f32[2,64,384]{2,1,0:T(8,128)S(1)}, f32[2,64,384]{2,1,0:T(8,128)S(1)}, u32[]{:S(2)}, u32[]{:S(2)}) %collective-permute-start.11) | collective-permute-done | bytes 196640 | tf_op jit(solution)/shard_map/ppermute | solution.py:350
  32.6 1.2 %turn_two.3 = (f32[64,384]{1,0:T(8,128)S(1)}, f32[64,768]{1,0:T(8,128)S(1)}, f32[2,64,384]{2,1,0:T(8,128)S(1)}) custom-call(f32[2,256]{1,0:T(2,128)S(1)} %concatenate.12.terms_ref, f32[64,1536]{1,0:T(8,128)S(1)} %second_part.4.mid_ref, f32[2,64,384]{2,1,0:T(8,128)S(1)} %get-tuple-element.50.sent_ref, f32[2,64,384]{2,1,0:T(8,128)S(1)} %collective-permute-done.11.got_ref, ...), custom_call_target="tpu_custom_call" | custom-call | flops 603979776 | bytes 786432 | tf_op jit(solution)/shard_map/turn_two/pallas_call | solution.py:215
  33.8 0.8 collective-permute-start.14
  34.6 1.5 %local_part.7 = (f32[64,1536]{1,0:T(8,128)S(1)}, f32[64,1536]{1,0:T(8,128)S(1)}) custom-call(f32[2,256]{1,0:T(2,128)S(1)} %concatenate.12.terms_ref, f32[64,768]{1,0:T(8,128)S(1)} %get-tuple-element.51.far_ref, f32[64,1536]{1,0:T(8,128)S(1)} %second_part.4.mid_ref, f32[64,384]{1,0:T(8,128)S(1)} %near_part.13.near_ref, ...), custom_call_target="tpu_custom_call" | custom-call | flops 301989888 | bytes 393216 | tf_op jit(solution)/shard_map/local_part/pallas_call | solution.py:215
  36.4 0.5 collective-permute-start.15
  37.2 1.4 %second_part.5.mid_ref = f32[64,1536]{1,0:T(8,128)S(1)} custom-call(f32[2,256]{1,0:T(2,128)S(1)} %concatenate.12.terms_ref, f32[64,1536]{1,0:T(8,128)S(1)} %get-tuple-element.53.mid_ref, f32[64,384]{1,0:T(8,128)S(1)} %near_part.14.near_ref, f32[64,1536]{1,0:T(8,128)S(1)} %get-tuple-element.54.before_ref, ...), custom_call_target="tpu_custom_call" | custom-call | flops 603979776 | bytes 786432 | tf_op jit(solution)/shard_map/second_part/pallas_call | solution.py:215
  39.1 1.8 %collective-permute-done.14.got_ref = f32[2,64,384]{2,1,0:T(8,128)S(1)} collective-permute-done((f32[2,64,384]{2,1,0:T(8,128)S(1)}, f32[2,64,384]{2,1,0:T(8,128)S(1)}, u32[]{:S(2)}, u32[]{:S(2)}) %collective-permute-start.14) | collective-permute-done | bytes 196640 | tf_op jit(solution)/shard_map/ppermute | solution.py:350
  40.9 0.8 last_part.1
  41.8 17.5 %all_to_all.5.parts_ref = f32[8,96,128]{2,1,0:T(8,128)S(1)} all-to-all(f32[8,96,128]{2,1,0:T(8,128)S(1)} %last_part.1), channel_id=1, replica_groups=mesh['narrow'=4,'wide'=8] {'wide'}, dimensions={0} | all-to-all | bytes 786432 | tf_op jit(solution)/shard_map/all_to_all | solution.py:676
  59.3 0.7 gram.1
  60.1 1.6 %collective-permute-done.16.refs_1_ = f32[576,128]{1,0:T(8,128)S(1)} collective-permute-done((f32[576,128]{1,0:T(8,128)S(1)}, f32[576,128]{1,0:T(8,128)S(1)}, u32[]{:S(2)}, u32[]{:S(2)}) %collective-permute-start.16) | collective-permute-done | bytes 294944 | tf_op jit(solution)/shard_map/ppermute | solution.py:418
  61.7 1.3 %collective-permute-start.17 = (f32[144,128]{1,0:T(8,128)S(1)}, f32[144,128]{1,0:T(8,128)S(1)}, u32[]{:S(2)}, u32[]{:S(2)}) collective-permute-start(f32[144,128]{1,0:T(8,128)S(1)} %get-tuple-element.59), channel_id=1, source_target_pairs={{0,16},{1,17},{2,18},{3,19},{4,20},{5,21},{6,22},{7,23},{8,24},{9,... | collective-permute-start | bytes 221192 | tf_op jit(solution)/shard_map/ppermute | solution.py:418
  63.0 1.1 %collective-permute-start.18 = (f32[144,128]{1,0:T(8,128)S(1)}, f32[144,128]{1,0:T(8,128)S(1)}, u32[]{:S(2)}, u32[]{:S(2)}) collective-permute-start(f32[144,128]{1,0:T(8,128)S(1)} %get-tuple-element.60), channel_id=1, source_target_pairs={{0,1},{1,0},{2,3},{3,2},{4,5},{5,4},{6,7},{7,6},{8,9},{9,8},{10,11... | collective-permute-start | bytes 221192 | tf_op jit(solution)/shard_map/ppermute | solution.py:418
  64.1 1.2 %collective-permute-start.19 = (f32[144,128]{1,0:T(8,128)S(1)}, f32[144,128]{1,0:T(8,128)S(1)}, u32[]{:S(2)}, u32[]{:S(2)}) collective-permute-start(f32[144,128]{1,0:T(8,128)S(1)} %get-tuple-element.61), channel_id=1, source_target_pairs={{0,17},{1,16},{2,19},{3,18},{4,21},{5,20},{6,23},{7,22},{8,25},{9,... | collective-permute-start | bytes 221192 | tf_op jit(solution)/shard_map/ppermute | solution.py:418
  65.3 0.9 collective-permute-done.17
  66.1 2.0 %collective-permute-done.18 = f32[144,128]{1,0:T(8,128)S(1)} collective-permute-done((f32[144,128]{1,0:T(8,128)S(1)}, f32[144,128]{1,0:T(8,128)S(1)}, u32[]{:S(2)}, u32[]{:S(2)}) %collective-permute-start.18) | collective-permute-done | bytes 73760 | tf_op jit(solution)/shard_map/ppermute | solution.py:418
  68.1 1.2 %collective-permute-done.19 = f32[144,128]{1,0:T(8,128)S(1)} collective-permute-done((f32[144,128]{1,0:T(8,128)S(1)}, f32[144,128]{1,0:T(8,128)S(1)}, u32[]{:S(2)}, u32[]{:S(2)}) %collective-permute-start.19) | collective-permute-done | bytes 73760 | tf_op jit(solution)/shard_map/ppermute | solution.py:418
  69.4 0.5 collective-permute-start.20
  69.8 1.6 %collective-permute-start.21 = (f32[144,128]{1,0:T(8,128)S(1)}, f32[144,128]{1,0:T(8,128)S(1)}, u32[]{:S(2)}, u32[]{:S(2)}) collective-permute-start(f32[144,128]{1,0:T(8,128)S(1)} %add_add_fusion.1), channel_id=1, source_target_pairs={{0,4},{1,5},{2,6},{3,7},{4,0},{5,1},{6,2},{7,3},{8,12},{9,13},{10,... | collective-permute-start | bytes 221192 | tf_op jit(solution)/shard_map/ppermute | solution.py:418
  71.5 2.4 %collective-permute-start.22 = (f32[144,128]{1,0:T(8,128)S(1)}, f32[144,128]{1,0:T(8,128)S(1)}, u32[]{:S(2)}, u32[]{:S(2)}) collective-permute-start(f32[144,128]{1,0:T(8,128)S(1)} %add_add_fusion.1), channel_id=1, source_target_pairs={{0,6},{1,7},{2,4},{3,5},{4,2},{5,3},{6,0},{7,1},{8,14},{9,15},{10,... | collective-permute-start | bytes 221192 | tf_op jit(solution)/shard_map/ppermute | solution.py:418
  73.8 2.7 %collective-permute-done.21 = f32[144,128]{1,0:T(8,128)S(1)} collective-permute-done((f32[144,128]{1,0:T(8,128)S(1)}, f32[144,128]{1,0:T(8,128)S(1)}, u32[]{:S(2)}, u32[]{:S(2)}) %collective-permute-start.21) | collective-permute-done | bytes 73760 | tf_op jit(solution)/shard_map/ppermute | solution.py:418
  76.5 1.2 %collective-permute-done.22 = f32[144,128]{1,0:T(8,128)S(1)} collective-permute-done((f32[144,128]{1,0:T(8,128)S(1)}, f32[144,128]{1,0:T(8,128)S(1)}, u32[]{:S(2)}, u32[]{:S(2)}) %collective-permute-start.22) | collective-permute-done | bytes 73760 | tf_op jit(solution)/shard_map/ppermute | solution.py:418
  77.7 0.9 collective-permute-start.23
  78.6 0.8 collective-permute-start.24
  79.4 1.9 %collective-permute-start.25 = (f32[144,128]{1,0:T(8,128)S(1)}, f32[144,128]{1,0:T(8,128)S(1)}, u32[]{:S(2)}, u32[]{:S(2)}) collective-permute-start(f32[144,128]{1,0:T(8,128)S(1)} %add_add_fusion), channel_id=1, source_target_pairs={{0,17},{1,16},{2,19},{3,18},{4,21},{5,20},{6,23},{7,22},{8,25},{9,... | collective-permute-start | bytes 221192 | tf_op jit(solution)/shard_map/ppermute | solution.py:418
  81.3 0.9 collective-permute-done.23
  82.2 0.8 collective-permute-done.24
  83.0 1.7 %collective-permute-done.25 = f32[144,128]{1,0:T(8,128)S(1)} collective-permute-done((f32[144,128]{1,0:T(8,128)S(1)}, f32[144,128]{1,0:T(8,128)S(1)}, u32[]{:S(2)}, u32[]{:S(2)}) %collective-permute-start.25) | collective-permute-done | bytes 73760 | tf_op jit(solution)/shard_map/ppermute | solution.py:418
  85.0 1.4 %collective-permute-done.26.other_ref = f32[576,128]{1,0:T(8,128)S(1)} collective-permute-done((f32[576,128]{1,0:T(8,128)S(1)}, f32[576,128]{1,0:T(8,128)S(1)}, u32[]{:S(2)}, u32[]{:S(2)}) %collective-permute-start.26) | collective-permute-done | bytes 294944 | tf_op jit(solution)/shard_map/ppermute | solution.py:418
  86.4 1.6 %rotate.1 = f32[192,512]{1,0:T(8,128)} custom-call(f32[576,128]{1,0:T(8,128)S(1)} %pad_maximum_fusion.own_ref, f32[576,128]{1,0:T(8,128)S(1)} %collective-permute-done.26.other_ref, f32[192,512]{1,0:T(8,128)S(1)} %turned.1.rows_ref), custom_call_target="tpu_custom_call" | custom-call | tf_op jit(solution)/shard_map/rotate/pallas_call | solution.py:656
  (42 shorter events, 4.3 us)
Async XLA Ops:
  2.5 6.3 %collective-permute-start.1 = (f32[64,384]{1,0:T(8,128)S(1)}, f32[64,384]{1,0:T(8,128)S(1)}, u32[]{:S(2)}, u32[]{:S(2)}) collective-permute-start(f32[64,384]{1,0:T(8,128)S(1)} %get-tuple-element.38.near_before_ref), channel_id=1, source_target_pairs={{0,8},{8,0},{16,24},{24,16},{1,9},{9,1},{17,25},{25,17},{2,10},{10... | collective-permute-start | bytes 294920 | tf_op jit(solution)/shard_map/ppermute | solution.py:358
  3.1 6.2 %collective-permute-start = (f32[64,384]{1,0:T(8,128)S(1)}, f32[64,384]{1,0:T(8,128)S(1)}, u32[]{:S(2)}, u32[]{:S(2)}) collective-permute-start(f32[64,384]{1,0:T(8,128)S(1)} %get-tuple-element.37.far_before_ref), channel_id=1, source_target_pairs={{0,24},{8,16},{16,8},{24,0},{1,25},{9,17},{17,9},{25,1},{2,26},{10... | collective-permute-start | bytes 294920 | tf_op jit(solution)/shard_map/ppermute | solution.py:350
  5.7 5.7 %collective-permute-start.6 = (f32[192,128]{1,0:T(8,128)S(1)}, f32[192,128]{1,0:T(8,128)S(1)}, u32[]{:S(2)}, u32[]{:S(2)}) collective-permute-start(f32[192,128]{1,0:T(8,128)S(1)} %get-tuple-element.43), channel_id=1, source_target_pairs={{0,24},{8,16},{16,8},{24,0},{1,25},{9,17},{17,9},{25,1},{2,26},{10... | collective-permute-start | bytes 294920 | tf_op jit(solution)/shard_map/ppermute | solution.py:350
  9.1 5.5 %collective-permute-start.3 = (f32[64,384]{1,0:T(8,128)S(1)}, f32[64,384]{1,0:T(8,128)S(1)}, u32[]{:S(2)}, u32[]{:S(2)}) collective-permute-start(f32[64,384]{1,0:T(8,128)S(1)} %near_part.8.near_ref.near_before_ref), channel_id=1, source_target_pairs={{0,8},{8,0},{16,24},{24,16},{1,9},{9,1},{17,25},{25,17},{2,10},{10... | collective-permute-start | bytes 294920 | tf_op jit(solution)/shard_map/ppermute | solution.py:358
  9.6 5.5 %collective-permute-start.2 = (f32[64,384]{1,0:T(8,128)S(1)}, f32[64,384]{1,0:T(8,128)S(1)}, u32[]{:S(2)}, u32[]{:S(2)}) collective-permute-start(f32[64,384]{1,0:T(8,128)S(1)} %far_part.1.far_ref.before_ref.far_before_ref), channel_id=1, source_target_pairs={{0,24},{8,16},{16,8},{24,0},{1,25},{9,17},{17,9},{25,1},{2,26},{10... | collective-permute-start | bytes 294920 | tf_op jit(solution)/shard_map/ppermute | solution.py:350
  11.3 6.0 %collective-permute-start.7 = (f32[192,128]{1,0:T(8,128)S(1)}, f32[192,128]{1,0:T(8,128)S(1)}, u32[]{:S(2)}, u32[]{:S(2)}) collective-permute-start(f32[192,128]{1,0:T(8,128)S(1)} %collective-permute-done.6.mine_ref), channel_id=1, source_target_pairs={{0,1},{1,0},{2,3},{3,2},{4,5},{5,4},{6,7},{7,6},{8,9},{9,8},{10,11... | collective-permute-start | bytes 294920 | tf_op jit(solution)/shard_map/ppermute | solution.py:354
  14.9 5.6 %collective-permute-start.4 = (f32[64,384]{1,0:T(8,128)S(1)}, f32[64,384]{1,0:T(8,128)S(1)}, u32[]{:S(2)}, u32[]{:S(2)}) collective-permute-start(f32[64,384]{1,0:T(8,128)S(1)} %near_part.9.near_ref), channel_id=1, source_target_pairs={{0,8},{8,0},{16,24},{24,16},{1,9},{9,1},{17,25},{25,17},{2,10},{10... | collective-permute-start | bytes 294920 | tf_op jit(solution)/shard_map/ppermute | solution.py:358
  15.9 8.5 %collective-permute-start.5 = (f32[2,64,384]{2,1,0:T(8,128)S(1)}, f32[2,64,384]{2,1,0:T(8,128)S(1)}, u32[]{:S(2)}, u32[]{:S(2)}) collective-permute-start(f32[2,64,384]{2,1,0:T(8,128)S(1)} %get-tuple-element.42.sent_ref), channel_id=1, source_target_pairs={{0,24},{8,16},{16,8},{24,0},{1,25},{9,17},{17,9},{25,1},{2,26},{10... | collective-permute-start | bytes 589832 | tf_op jit(solution)/shard_map/ppermute | solution.py:350
  17.3 7.0 %collective-permute-start.8 = (f32[384,128]{1,0:T(8,128)S(1)}, f32[384,128]{1,0:T(8,128)S(1)}, u32[]{:S(2)}, u32[]{:S(2)}) collective-permute-start(f32[384,128]{1,0:T(8,128)S(1)} %pad_maximum_fusion.1), channel_id=1, source_target_pairs={{0,2},{1,3},{2,0},{3,1},{4,6},{5,7},{6,4},{7,5},{8,10},{9,11},{10,... | collective-permute-start | bytes 589832 | tf_op jit(solution)/shard_map/ppermute | solution.py:354
  20.8 1.5 %collective-permute-start.9 = (f32[64,384]{1,0:T(8,128)S(1)}, f32[64,384]{1,0:T(8,128)S(1)}, u32[]{:S(2)}, u32[]{:S(2)}) collective-permute-start(f32[64,384]{1,0:T(8,128)S(1)} %near_part.10.near_ref.near_before_ref), channel_id=1, source_target_pairs={{0,8},{8,0},{16,24},{24,16},{1,9},{9,1},{17,25},{25,17},{2,10},{10... | collective-permute-start | bytes 294920 | tf_op jit(solution)/shard_map/ppermute | solution.py:358
  22.6 4.8 %collective-permute-start.10 = (f32[64,384]{1,0:T(8,128)S(1)}, f32[64,384]{1,0:T(8,128)S(1)}, u32[]{:S(2)}, u32[]{:S(2)}) collective-permute-start(f32[64,384]{1,0:T(8,128)S(1)} %near_part.11.near_ref), channel_id=1, source_target_pairs={{0,8},{8,0},{16,24},{24,16},{1,9},{9,1},{17,25},{25,17},{2,10},{10... | collective-permute-start | bytes 294920 | tf_op jit(solution)/shard_map/ppermute | solution.py:358
  25.8 6.8 %collective-permute-start.11 = (f32[2,64,384]{2,1,0:T(8,128)S(1)}, f32[2,64,384]{2,1,0:T(8,128)S(1)}, u32[]{:S(2)}, u32[]{:S(2)}) collective-permute-start(f32[2,64,384]{2,1,0:T(8,128)S(1)} %get-tuple-element.50.sent_ref), channel_id=1, source_target_pairs={{0,24},{8,16},{16,8},{24,0},{1,25},{9,17},{17,9},{25,1},{2,26},{10... | collective-permute-start | bytes 589832 | tf_op jit(solution)/shard_map/ppermute | solution.py:350
  27.7 2.2 %collective-permute-start.12 = (f32[64,384]{1,0:T(8,128)S(1)}, f32[64,384]{1,0:T(8,128)S(1)}, u32[]{:S(2)}, u32[]{:S(2)}) collective-permute-start(f32[64,384]{1,0:T(8,128)S(1)} %near_part.12.near_ref.near_before_ref), channel_id=1, source_target_pairs={{0,8},{8,0},{16,24},{24,16},{1,9},{9,1},{17,25},{25,17},{2,10},{10... | collective-permute-start | bytes 294920 | tf_op jit(solution)/shard_map/ppermute | solution.py:358
  30.2 5.9 %collective-permute-start.13 = (f32[64,384]{1,0:T(8,128)S(1)}, f32[64,384]{1,0:T(8,128)S(1)}, u32[]{:S(2)}, u32[]{:S(2)}) collective-permute-start(f32[64,384]{1,0:T(8,128)S(1)} %near_part.13.near_ref), channel_id=1, source_target_pairs={{0,8},{8,0},{16,24},{24,16},{1,9},{9,1},{17,25},{25,17},{2,10},{10... | collective-permute-start | bytes 294920 | tf_op jit(solution)/shard_map/ppermute | solution.py:358
  33.8 7.1 %collective-permute-start.14 = (f32[2,64,384]{2,1,0:T(8,128)S(1)}, f32[2,64,384]{2,1,0:T(8,128)S(1)}, u32[]{:S(2)}, u32[]{:S(2)}) collective-permute-start(f32[2,64,384]{2,1,0:T(8,128)S(1)} %get-tuple-element.55.sent_ref), channel_id=1, source_target_pairs={{0,24},{8,16},{16,8},{24,0},{1,25},{9,17},{17,9},{25,1},{2,26},{10... | collective-permute-start | bytes 589832 | tf_op jit(solution)/shard_map/ppermute | solution.py:350
  36.4 2.2 %collective-permute-start.15 = (f32[64,384]{1,0:T(8,128)S(1)}, f32[64,384]{1,0:T(8,128)S(1)}, u32[]{:S(2)}, u32[]{:S(2)}) collective-permute-start(f32[64,384]{1,0:T(8,128)S(1)} %near_part.14.near_ref), channel_id=1, source_target_pairs={{0,8},{8,0},{16,24},{24,16},{1,9},{9,1},{17,25},{25,17},{2,10},{10... | collective-permute-start | bytes 294920 | tf_op jit(solution)/shard_map/ppermute | solution.py:358
  60.0 1.6 %collective-permute-start.16 = (f32[576,128]{1,0:T(8,128)S(1)}, f32[576,128]{1,0:T(8,128)S(1)}, u32[]{:S(2)}, u32[]{:S(2)}) collective-permute-start(f32[576,128]{1,0:T(8,128)S(1)} %get-tuple-element.57), channel_id=1, source_target_pairs={{0,8},{1,9},{2,10},{3,11},{4,12},{5,13},{6,14},{7,15},{8,0},{9,1},... | collective-permute-start | bytes 884744 | tf_op jit(solution)/shard_map/ppermute | solution.py:418
  61.7 4.4 %collective-permute-start.17 = (f32[144,128]{1,0:T(8,128)S(1)}, f32[144,128]{1,0:T(8,128)S(1)}, u32[]{:S(2)}, u32[]{:S(2)}) collective-permute-start(f32[144,128]{1,0:T(8,128)S(1)} %get-tuple-element.59), channel_id=1, source_target_pairs={{0,16},{1,17},{2,18},{3,19},{4,20},{5,21},{6,22},{7,23},{8,24},{9,... | collective-permute-start | bytes 221192 | tf_op jit(solution)/shard_map/ppermute | solution.py:418
  63.0 5.1 %collective-permute-start.18 = (f32[144,128]{1,0:T(8,128)S(1)}, f32[144,128]{1,0:T(8,128)S(1)}, u32[]{:S(2)}, u32[]{:S(2)}) collective-permute-start(f32[144,128]{1,0:T(8,128)S(1)} %get-tuple-element.60), channel_id=1, source_target_pairs={{0,1},{1,0},{2,3},{3,2},{4,5},{5,4},{6,7},{7,6},{8,9},{9,8},{10,11... | collective-permute-start | bytes 221192 | tf_op jit(solution)/shard_map/ppermute | solution.py:418
  64.1 5.3 %collective-permute-start.19 = (f32[144,128]{1,0:T(8,128)S(1)}, f32[144,128]{1,0:T(8,128)S(1)}, u32[]{:S(2)}, u32[]{:S(2)}) collective-permute-start(f32[144,128]{1,0:T(8,128)S(1)} %get-tuple-element.61), channel_id=1, source_target_pairs={{0,17},{1,16},{2,19},{3,18},{4,21},{5,20},{6,23},{7,22},{8,25},{9,... | collective-permute-start | bytes 221192 | tf_op jit(solution)/shard_map/ppermute | solution.py:418
  69.4 4.5 %collective-permute-start.20 = (f32[144,128]{1,0:T(8,128)S(1)}, f32[144,128]{1,0:T(8,128)S(1)}, u32[]{:S(2)}, u32[]{:S(2)}) collective-permute-start(f32[144,128]{1,0:T(8,128)S(1)} %add_add_fusion.1), channel_id=1, source_target_pairs={{0,2},{1,3},{2,0},{3,1},{4,6},{5,7},{6,4},{7,5},{8,10},{9,11},{10,... | collective-permute-start | bytes 221192 | tf_op jit(solution)/shard_map/ppermute | solution.py:418
  69.8 6.7 %collective-permute-start.21 = (f32[144,128]{1,0:T(8,128)S(1)}, f32[144,128]{1,0:T(8,128)S(1)}, u32[]{:S(2)}, u32[]{:S(2)}) collective-permute-start(f32[144,128]{1,0:T(8,128)S(1)} %add_add_fusion.1), channel_id=1, source_target_pairs={{0,4},{1,5},{2,6},{3,7},{4,0},{5,1},{6,2},{7,3},{8,12},{9,13},{10,... | collective-permute-start | bytes 221192 | tf_op jit(solution)/shard_map/ppermute | solution.py:418
  71.5 6.3 %collective-permute-start.22 = (f32[144,128]{1,0:T(8,128)S(1)}, f32[144,128]{1,0:T(8,128)S(1)}, u32[]{:S(2)}, u32[]{:S(2)}) collective-permute-start(f32[144,128]{1,0:T(8,128)S(1)} %add_add_fusion.1), channel_id=1, source_target_pairs={{0,6},{1,7},{2,4},{3,5},{4,2},{5,3},{6,0},{7,1},{8,14},{9,15},{10,... | collective-permute-start | bytes 221192 | tf_op jit(solution)/shard_map/ppermute | solution.py:418
  77.7 4.4 %collective-permute-start.23 = (f32[144,128]{1,0:T(8,128)S(1)}, f32[144,128]{1,0:T(8,128)S(1)}, u32[]{:S(2)}, u32[]{:S(2)}) collective-permute-start(f32[144,128]{1,0:T(8,128)S(1)} %add_add_fusion), channel_id=1, source_target_pairs={{0,16},{1,17},{2,18},{3,19},{4,20},{5,21},{6,22},{7,23},{8,24},{9,... | collective-permute-start | bytes 221192 | tf_op jit(solution)/shard_map/ppermute | solution.py:418
  78.6 4.4 %collective-permute-start.24 = (f32[144,128]{1,0:T(8,128)S(1)}, f32[144,128]{1,0:T(8,128)S(1)}, u32[]{:S(2)}, u32[]{:S(2)}) collective-permute-start(f32[144,128]{1,0:T(8,128)S(1)} %add_add_fusion), channel_id=1, source_target_pairs={{0,1},{1,0},{2,3},{3,2},{4,5},{5,4},{6,7},{7,6},{8,9},{9,8},{10,11... | collective-permute-start | bytes 221192 | tf_op jit(solution)/shard_map/ppermute | solution.py:418
  79.4 5.3 %collective-permute-start.25 = (f32[144,128]{1,0:T(8,128)S(1)}, f32[144,128]{1,0:T(8,128)S(1)}, u32[]{:S(2)}, u32[]{:S(2)}) collective-permute-start(f32[144,128]{1,0:T(8,128)S(1)} %add_add_fusion), channel_id=1, source_target_pairs={{0,17},{1,16},{2,19},{3,18},{4,21},{5,20},{6,23},{7,22},{8,25},{9,... | collective-permute-start | bytes 221192 | tf_op jit(solution)/shard_map/ppermute | solution.py:418
  84.7 1.6 %collective-permute-start.26 = (f32[576,128]{1,0:T(8,128)S(1)}, f32[576,128]{1,0:T(8,128)S(1)}, u32[]{:S(2)}, u32[]{:S(2)}) collective-permute-start(f32[576,128]{1,0:T(8,128)S(1)} %pad_maximum_fusion.own_ref), channel_id=1, source_target_pairs={{0,8},{1,9},{2,10},{3,11},{4,12},{5,13},{6,14},{7,15},{8,0},{9,1},... | collective-permute-start | bytes 884744 | tf_op jit(solution)/shard_map/ppermute | solution.py:418

commit v5 on v4

--- a/solution.py
+++ b/solution.py
@@ -89,8 +89,8 @@
             block = held[place, slot]
             hi, lo = split(block)
             there = pl.ds(pl.multiple_of((half + offset + REACH) * size, size), size)
-            hi_ref[pair, here, there] = hi
-            lo_ref[pair, here, there] = lo
+            hi_ref[pair, there, here] = hi.T
+            lo_ref[pair, there, here] = lo.T
             if row < REACH:
 
                 @pl.when(row + offset < 0)
@@ -109,7 +109,7 @@
 
 def spread_part(columns, vectors, blocks, total_blocks):
     rows, slots, size, _ = blocks.shape
-    spread = jax.ShapeDtypeStruct((rows // 2, 2 * size, (2 * REACH + 2) * size), BF16)
+    spread = jax.ShapeDtypeStruct((rows // 2, (2 * REACH + 2) * size, 2 * size), BF16)
     edge = jax.ShapeDtypeStruct((vectors.shape[0], REACH * size), F32)
     crossing = REACH * (REACH + 1) // 2 * size
     cross = jax.ShapeDtypeStruct((crossing // CROSS_PARTS, size), F32)
@@ -143,8 +143,8 @@
         there = slice((begin - self.at) * size, (end - self.at) * size)
         inside = slice((begin - start) * size, (end - start) * size)
         rows = slice(None) if half is None else slice(half * size, (half + 1) * size)
-        hi, lo = hi_ref[pair, rows, inside], lo_ref[pair, rows, inside]
-        return dot_split(self.hi[:, there], self.both[:, there], hi, lo, NT)
+        hi, lo = hi_ref[pair, inside, rows], lo_ref[pair, inside, rows]
+        return dot_split(self.hi[:, there], self.both[:, there], hi, lo, NN)
 
 
 def reversed_blocks(edge, size):
@@ -172,7 +172,7 @@
 
 
 def first_kernel(terms_ref, vectors_ref, hi_ref, lo_ref, out_ref):
-    pairs, width, _ = hi_ref.shape
+    pairs, _, width = hi_ref.shape
     scale, diag = terms_ref[0:1, :], terms_ref[1:2, :]
     strip = Strip(vectors_ref[...], 0, width // 2)
     for pair in range(pairs):
@@ -182,7 +182,7 @@
 
 
 def local_kernel(first_pair, terms_ref, far_ref, mid_ref, near_ref, far_before_ref, mid_before_ref, near_before_ref, hi_ref, lo_ref, out_ref, *full_ref):
-    pairs, width, _ = hi_ref.shape
+    pairs, _, width = hi_ref.shape
     edge, start = near_ref.shape[1], far_ref.shape[1]
     scale, diag = terms_ref[0:1, :], terms_ref[1:2, :]
     current = jnp.concatenate([far_ref[...], mid_ref[:, start:-edge], near_ref[...]], axis=1)
@@ -197,7 +197,7 @@
 
 
 def second_kernel(terms_ref, mid_ref, near_ref, before_ref, hi_ref, lo_ref, out_ref):
-    pairs, width, _ = hi_ref.shape
+    pairs, _, width = hi_ref.shape
     edge = near_ref.shape[1]
     scale, diag = terms_ref[0:1, :], terms_ref[1:2, :]
     current = jnp.concatenate([mid_ref[:, edge:-edge], near_ref[...]], axis=1)
@@ -211,7 +211,7 @@
 
 def step_call(kernel, name, operands, operator, outs):
     size = operands[1].size
-    width = operator[0].shape[1]
+    width = operator[0].shape[-1]
     return pl.pallas_call(
         kernel,
         in_specs=[VM] * (len(operands) + 2),
@@ -224,7 +224,7 @@
 
 
 def near_kernel(factor, terms_ref, mid_ref, halo_ref, hi_ref, lo_ref, out_ref):
-    size, edge = hi_ref.shape[1] // 2, halo_ref.shape[1]
+    size, edge = hi_ref.shape[2] // 2, halo_ref.shape[1]
     scale = factor * terms_ref[0:1, 0:1]
     out_ref[...] = mid_ref[:, -edge:] + scale * near_sum((hi_ref, lo_ref), halo_ref[...], size)
 
@@ -238,13 +238,13 @@
 
 
 def far_kernel(terms_ref, mid_ref, halo_ref, hi_ref, lo_ref, far_ref):
-    size, edge = hi_ref.shape[1] // 2, halo_ref.shape[1]
+    size, edge = hi_ref.shape[2] // 2, halo_ref.shape[1]
     far_ref[...] = mid_ref[:, :edge] + 0.5 * terms_ref[0:1, 0:1] * far_sum((hi_ref, lo_ref), halo_ref[...], size)
 
 
 def turn_one_kernel(terms_ref, mid_ref, halo_ref, before_ref, hi_ref, lo_ref, far_ref, send_ref):
     operator = (hi_ref, lo_ref)
-    size, edge = hi_ref.shape[1] // 2, halo_ref.shape[1]
+    size, edge = hi_ref.shape[2] // 2, halo_ref.shape[1]
     scale, diag = terms_ref[0:1, 0:1], terms_ref[1:2, 0:1]
     edge_rows = mid_ref[:, :edge] + scale * far_sum(operator, halo_ref[...], size)
     far = jnp.concatenate([edge_rows, mid_ref[:, edge : 2 * edge]], axis=1)
@@ -274,7 +274,7 @@
 
 
 def turn(terms_ref, mid_ref, sent_ref, got_ref, beyond_refs, operator):
-    size, edge = operator[0].shape[1] // 2, sent_ref.shape[2]
+    size, edge = operator[0].shape[2] // 2, sent_ref.shape[2]
     scale, diag = terms_ref[0:1, 0:1], terms_ref[1:2, 0:1]
     between = sent_ref[1] + scale * far_sum(operator, got_ref[0], size)
     beyond = beyond_refs[0][...] if len(beyond_refs) == 1 else beyond_sum(terms_ref, sent_ref, *beyond_refs)
@@ -312,7 +312,7 @@
 def turn_two_kernel(terms_ref, mid_ref, sent_ref, got_ref, *refs):
     *beyond_refs, hi_ref, lo_ref, between_ref, far_ref, send_ref = refs
     operator = (hi_ref, lo_ref)
-    size, edge = hi_ref.shape[1] // 2, between_ref.shape[1]
+    size, edge = hi_ref.shape[2] // 2, between_ref.shape[1]
     between, far = turn(terms_ref, mid_ref, sent_ref, got_ref, beyond_refs, operator)
     between_ref[...] = between
     far_ref[...] = far
@@ -325,7 +325,7 @@
 
 
 def last_kernel(parts, terms_ref, mid_ref, sent_ref, got_ref, beyond_ref, near_ref, hi_ref, lo_ref, out_ref):
-    size = hi_ref.shape[1] // 2
+    size = hi_ref.shape[2] // 2
     _, far = turn(terms_ref, mid_ref, sent_ref, got_ref, (beyond_ref,), (hi_ref, lo_ref))
     whole = jnp.concatenate([far, mid_ref[:, far.shape[1] : -near_ref.shape[1]], near_ref[...]], axis=1)
     mirrored = jnp.concatenate(reversed_blocks(whole, size), axis=1)

time: 88.4 us -> 87.2 us (0.986)
  Pallas kernels: 24.6 us -> 18.7 us
  waiting for transfers between devices: 19.4 us -> 23.7 us
    pallas_call x23, Pallas kernels: 19.4 us -> 12.6 us  [step_call(): pl.pallas_call(kernel, in_specs=[VM] * (len(operands) + 2), out_specs=[VM...]
    ppermute x6, waiting for transfers between devices: 3.83 us -> 6.88 us  [far_swap(): lax.ppermute(x, 'narrow', [(i, (i + 1) % size if i % 2 else (i - 1) % siz...]
    pallas_call x1, Pallas kernels: 2.52 us -> 3.51 us  [spread_part(): pl.pallas_call(functools.partial(spread_kernel, total_blocks), in_specs=[...]
    ppermute x8, starting transfers between devices: 2.96 us -> 3.86 us  [near_swap(): lax.ppermute(x, 'narrow', [(i, i ^ 1) for i in range(lax.axis_size('narro...]
  transfers between devices with their start and end apart: 27 -> 27, of which waited for: 13 -> 17; matrix products, arithmetic and copies ran while one was open for 0% -> 0% of each run, Pallas kernels for 21% -> 14%
where the time goes in v5:
time: 87.2 us; the launch traced here: 87 us
  starting transfers between devices  25.1 us (29%)
  waiting for transfers between devices  23.7 us (27%)
  Pallas kernels  18.7 us (21%)
  blocking collectives  17.6 us (20%)
  between operations  1.65 us (2%)
    all_to_all x1, blocking collectives, regroup(): lax.all_to_all(parts, 'wide', split_axis=0, concat_axis=0, tiled=True)  17.6 us
    ppermute x11, waiting for transfers between devices, swap(): return lax.ppermute(x, ('narrow', 'wide'), pair_perm(mask))  14.2 us
    pallas_call x23, Pallas kernels, step_call(): pl.pallas_call(kernel, in_specs=[VM] * (len(operands) + 2), out_specs=[VM...  12.6 us
    ppermute x11, starting transfers between devices, swap(): return lax.ppermute(x, ('narrow', 'wide'), pair_perm(mask))  11.7 us
    ppermute x6, waiting for transfers between devices, far_swap(): lax.ppermute(x, 'narrow', [(i, (i + 1) % size if i % 2 else (i - 1) % siz...  6.88 us
    ppermute x6, starting transfers between devices, far_swap(): lax.ppermute(x, 'narrow', [(i, (i + 1) % size if i % 2 else (i - 1) % siz...  6.39 us
    ppermute x8, starting transfers between devices, near_swap(): lax.ppermute(x, 'narrow', [(i, i ^ 1) for i in range(lax.axis_size('narro...  3.86 us
    pallas_call x1, Pallas kernels, spread_part(): pl.pallas_call(functools.partial(spread_kernel, total_blocks), in_specs=[...  3.51 us
  transfers between devices with their start and end apart: 27, of which 17 were waited for; matrix products, arithmetic and copies ran while one was open for 0% of the time, Pallas kernels for 14%

profile of v5, /device:TPU:0, one launch (start us, length us, event | category | flops | bytes accessed | tf_op | source)
XLA Modules:
  0.0 87.0 jit_solution(9786887252493253407)
XLA Ops:
  0.0 3.5 %spread_part.1 = (f32[64,384]{1,0:T(8,128)S(1)}, f32[64,384]{1,0:T(8,128)S(1)}, f32[64,1536]{1,0:T(8,128)S(1)}, f32[192,128]{1,0:T(8,128)S(1)}, bf16[6,1024,256]...) custom-call(s32[5,12]{1,0:T(8,128)} %bitcast.3, f32[64,1536]{1,0:T(8,128)} %vectors_hbm.1, f32[12,5,128,128]{3,2,1,0:T(8,128)} %blocks_hbm.1), custom_call_target="tpu_custom_call" | custom-call | tf_op jit(solution)/shard_map/spread_part/pallas_call | solution.py:116
  3.5 0.5 collective-permute-start.1
  4.0 2.6 %collective-permute-start = (f32[64,384]{1,0:T(8,128)S(1)}, f32[64,384]{1,0:T(8,128)S(1)}, u32[]{:S(2)}, u32[]{:S(2)}) collective-permute-start(f32[64,384]{1,0:T(8,128)S(1)} %get-tuple-element.37.far_before_ref), channel_id=1, source_target_pairs={{0,24},{8,16},{16,8},{24,0},{1,25},{9,17},{17,9},{25,1},{2,26},{10... | collective-permute-start | bytes 294920 | tf_op jit(solution)/shard_map/ppermute | solution.py:350
  8.1 0.9 %first_part.1.mid_ref.mid_before_ref = f32[64,1536]{1,0:T(8,128)S(1)} custom-call(f32[2,256]{1,0:T(2,128)S(1)} %concatenate.12.terms_ref, f32[64,1536]{1,0:T(8,128)S(1)} %get-tuple-element.34.vectors_ref.mid_before_ref, bf16[6,1024,256]{2,1,0:T(8,128)(2,1)S(1)} %get-tuple-element.35.hi_ref.refs_2_.refs_1_, ...), custom_call_target="tpu_custom_call" | custom-call | flops 603979776 | bytes 786432 | tf_op jit(solution)/shard_map/first_part/pallas_call | solution.py:215
  10.0 2.3 %collective-permute-start.2 = (f32[64,384]{1,0:T(8,128)S(1)}, f32[64,384]{1,0:T(8,128)S(1)}, u32[]{:S(2)}, u32[]{:S(2)}) collective-permute-start(f32[64,384]{1,0:T(8,128)S(1)} %far_part.1.far_ref.before_ref.far_before_ref), channel_id=1, source_target_pairs={{0,24},{8,16},{16,8},{24,0},{1,25},{9,17},{17,9},{25,1},{2,26},{10... | collective-permute-start | bytes 294920 | tf_op jit(solution)/shard_map/ppermute | solution.py:350
  12.3 1.5 %collective-permute-start.7 = (f32[192,128]{1,0:T(8,128)S(1)}, f32[192,128]{1,0:T(8,128)S(1)}, u32[]{:S(2)}, u32[]{:S(2)}) collective-permute-start(f32[192,128]{1,0:T(8,128)S(1)} %collective-permute-done.6.mine_ref), channel_id=1, source_target_pairs={{0,1},{1,0},{2,3},{3,2},{4,5},{5,4},{6,7},{7,6},{8,9},{9,8},{10,11... | collective-permute-start | bytes 294920 | tf_op jit(solution)/shard_map/ppermute | solution.py:354
  13.8 1.0 %local_part.4.mid_ref = f32[64,1536]{1,0:T(8,128)S(1)} custom-call(f32[2,256]{1,0:T(2,128)S(1)} %concatenate.12.terms_ref, f32[64,384]{1,0:T(8,128)S(1)} %far_part.1.far_ref.before_ref.far_before_ref, f32[64,1536]{1,0:T(8,128)S(1)} %first_part.1.mid_ref.mid_before_ref, f32[64,384]{1,0:T(8,128)S(1)} %near_part.8.near_ref.near_before_ref, ...), custom_call_target="tpu_custom_call" | custom-call | flops 150994944 | bytes 196608 | tf_op jit(solution)/shard_map/local_part/pallas_call | solution.py:215
  15.3 0.6 turn_one.1
  15.9 1.3 %collective-permute-start.5 = (f32[2,64,384]{2,1,0:T(8,128)S(1)}, f32[2,64,384]{2,1,0:T(8,128)S(1)}, u32[]{:S(2)}, u32[]{:S(2)}) collective-permute-start(f32[2,64,384]{2,1,0:T(8,128)S(1)} %get-tuple-element.42.sent_ref), channel_id=1, source_target_pairs={{0,24},{8,16},{16,8},{24,0},{1,25},{9,17},{17,9},{25,1},{2,26},{10... | collective-permute-start | bytes 589832 | tf_op jit(solution)/shard_map/ppermute | solution.py:350
  17.3 1.6 %collective-permute-start.8 = (f32[384,128]{1,0:T(8,128)S(1)}, f32[384,128]{1,0:T(8,128)S(1)}, u32[]{:S(2)}, u32[]{:S(2)}) collective-permute-start(f32[384,128]{1,0:T(8,128)S(1)} %pad_maximum_fusion.1), channel_id=1, source_target_pairs={{0,2},{1,3},{2,0},{3,1},{4,6},{5,7},{6,4},{7,5},{8,10},{9,11},{10,... | collective-permute-start | bytes 589832 | tf_op jit(solution)/shard_map/ppermute | solution.py:354
  18.9 0.8 local_part.5
  20.1 0.8 second_part.3.mid_ref
  20.9 0.5 collective-permute-done.9.halo_ref
  21.8 2.0 %collective-permute-done.8.two_ref = f32[384,128]{1,0:T(8,128)S(1)} collective-permute-done((f32[384,128]{1,0:T(8,128)S(1)}, f32[384,128]{1,0:T(8,128)S(1)}, u32[]{:S(2)}, u32[]{:S(2)}) %collective-permute-start.8) | collective-permute-done | bytes 196640 | tf_op jit(solution)/shard_map/ppermute | solution.py:354
  23.9 1.0 %turn_two.2 = (f32[64,384]{1,0:T(8,128)S(1)}, f32[64,768]{1,0:T(8,128)S(1)}, f32[2,64,384]{2,1,0:T(8,128)S(1)}) custom-call(f32[2,256]{1,0:T(2,128)S(1)} %concatenate.12.terms_ref, f32[64,1536]{1,0:T(8,128)S(1)} %second_part.3.mid_ref, f32[2,64,384]{2,1,0:T(8,128)S(1)} %get-tuple-element.42.sent_ref, f32[2,64,384]{2,1,0:T(8,128)S(1)} %collective-permute-done.5.got_ref, ...), custom_call_target="tpu_custom_call" | custom-call | flops 603979776 | bytes 786432 | tf_op jit(solution)/shard_map/turn_two/pallas_call | solution.py:215
  25.0 0.8 local_part.6
  26.0 1.4 %collective-permute-start.12 = (f32[64,384]{1,0:T(8,128)S(1)}, f32[64,384]{1,0:T(8,128)S(1)}, u32[]{:S(2)}, u32[]{:S(2)}) collective-permute-start(f32[64,384]{1,0:T(8,128)S(1)} %near_part.12.near_ref.near_before_ref), channel_id=1, source_target_pairs={{0,8},{8,0},{16,24},{24,16},{1,9},{9,1},{17,25},{25,17},{2,10},{10... | collective-permute-start | bytes 294920 | tf_op jit(solution)/shard_map/ppermute | solution.py:358
  27.4 0.8 second_part.4.mid_ref
  28.6 0.4 collective-permute-start.13
  29.3 2.6 %collective-permute-done.11.got_ref = f32[2,64,384]{2,1,0:T(8,128)S(1)} collective-permute-done((f32[2,64,384]{2,1,0:T(8,128)S(1)}, f32[2,64,384]{2,1,0:T(8,128)S(1)}, u32[]{:S(2)}, u32[]{:S(2)}) %collective-permute-start.11) | collective-permute-done | bytes 196640 | tf_op jit(solution)/shard_map/ppermute | solution.py:350
  31.9 0.9 %turn_two.3 = (f32[64,384]{1,0:T(8,128)S(1)}, f32[64,768]{1,0:T(8,128)S(1)}, f32[2,64,384]{2,1,0:T(8,128)S(1)}) custom-call(f32[2,256]{1,0:T(2,128)S(1)} %concatenate.12.terms_ref, f32[64,1536]{1,0:T(8,128)S(1)} %second_part.4.mid_ref, f32[2,64,384]{2,1,0:T(8,128)S(1)} %get-tuple-element.50.sent_ref, f32[2,64,384]{2,1,0:T(8,128)S(1)} %collective-permute-done.11.got_ref, ...), custom_call_target="tpu_custom_call" | custom-call | flops 603979776 | bytes 786432 | tf_op jit(solution)/shard_map/turn_two/pallas_call | solution.py:215
  32.9 0.8 local_part.7
  33.9 1.0 %collective-permute-start.15 = (f32[64,384]{1,0:T(8,128)S(1)}, f32[64,384]{1,0:T(8,128)S(1)}, u32[]{:S(2)}, u32[]{:S(2)}) collective-permute-start(f32[64,384]{1,0:T(8,128)S(1)} %near_part.14.near_ref), channel_id=1, source_target_pairs={{0,8},{8,0},{16,24},{24,16},{1,9},{9,1},{17,25},{25,17},{2,10},{10... | collective-permute-start | bytes 294920 | tf_op jit(solution)/shard_map/ppermute | solution.py:358
  35.2 0.8 second_part.5.mid_ref
  36.3 3.7 %collective-permute-done.14.got_ref = f32[2,64,384]{2,1,0:T(8,128)S(1)} collective-permute-done((f32[2,64,384]{2,1,0:T(8,128)S(1)}, f32[2,64,384]{2,1,0:T(8,128)S(1)}, u32[]{:S(2)}, u32[]{:S(2)}) %collective-permute-start.14) | collective-permute-done | bytes 196640 | tf_op jit(solution)/shard_map/ppermute | solution.py:350
  40.0 0.7 last_part.1
  40.7 17.6 %all_to_all.5.parts_ref = f32[8,96,128]{2,1,0:T(8,128)S(1)} all-to-all(f32[8,96,128]{2,1,0:T(8,128)S(1)} %last_part.1), channel_id=1, replica_groups=mesh['narrow'=4,'wide'=8] {'wide'}, dimensions={0} | all-to-all | bytes 786432 | tf_op jit(solution)/shard_map/all_to_all | solution.py:676
  58.3 0.7 gram.1
  59.1 1.6 %collective-permute-done.16.refs_1_ = f32[576,128]{1,0:T(8,128)S(1)} collective-permute-done((f32[576,128]{1,0:T(8,128)S(1)}, f32[576,128]{1,0:T(8,128)S(1)}, u32[]{:S(2)}, u32[]{:S(2)}) %collective-permute-start.16) | collective-permute-done | bytes 294944 | tf_op jit(solution)/shard_map/ppermute | solution.py:418
  60.7 0.6 collective-permute-start.17
  61.4 1.1 %collective-permute-start.18 = (f32[144,128]{1,0:T(8,128)S(1)}, f32[144,128]{1,0:T(8,128)S(1)}, u32[]{:S(2)}, u32[]{:S(2)}) collective-permute-start(f32[144,128]{1,0:T(8,128)S(1)} %get-tuple-element.60), channel_id=1, source_target_pairs={{0,1},{1,0},{2,3},{3,2},{4,5},{5,4},{6,7},{7,6},{8,9},{9,8},{10,11... | collective-permute-start | bytes 221192 | tf_op jit(solution)/shard_map/ppermute | solution.py:418
  62.5 1.8 %collective-permute-start.19 = (f32[144,128]{1,0:T(8,128)S(1)}, f32[144,128]{1,0:T(8,128)S(1)}, u32[]{:S(2)}, u32[]{:S(2)}) collective-permute-start(f32[144,128]{1,0:T(8,128)S(1)} %get-tuple-element.61), channel_id=1, source_target_pairs={{0,17},{1,16},{2,19},{3,18},{4,21},{5,20},{6,23},{7,22},{8,25},{9,... | collective-permute-start | bytes 221192 | tf_op jit(solution)/shard_map/ppermute | solution.py:418
  64.3 1.1 %collective-permute-done.17 = f32[144,128]{1,0:T(8,128)S(1)} collective-permute-done((f32[144,128]{1,0:T(8,128)S(1)}, f32[144,128]{1,0:T(8,128)S(1)}, u32[]{:S(2)}, u32[]{:S(2)}) %collective-permute-start.17) | collective-permute-done | bytes 73760 | tf_op jit(solution)/shard_map/ppermute | solution.py:418
  65.4 1.0 %collective-permute-done.18 = f32[144,128]{1,0:T(8,128)S(1)} collective-permute-done((f32[144,128]{1,0:T(8,128)S(1)}, f32[144,128]{1,0:T(8,128)S(1)}, u32[]{:S(2)}, u32[]{:S(2)}) %collective-permute-start.18) | collective-permute-done | bytes 73760 | tf_op jit(solution)/shard_map/ppermute | solution.py:418
  66.3 1.4 %collective-permute-done.19 = f32[144,128]{1,0:T(8,128)S(1)} collective-permute-done((f32[144,128]{1,0:T(8,128)S(1)}, f32[144,128]{1,0:T(8,128)S(1)}, u32[]{:S(2)}, u32[]{:S(2)}) %collective-permute-start.19) | collective-permute-done | bytes 73760 | tf_op jit(solution)/shard_map/ppermute | solution.py:418
  67.7 0.5 collective-permute-start.20
  68.2 1.6 %collective-permute-start.21 = (f32[144,128]{1,0:T(8,128)S(1)}, f32[144,128]{1,0:T(8,128)S(1)}, u32[]{:S(2)}, u32[]{:S(2)}) collective-permute-start(f32[144,128]{1,0:T(8,128)S(1)} %add_add_fusion.1), channel_id=1, source_target_pairs={{0,4},{1,5},{2,6},{3,7},{4,0},{5,1},{6,2},{7,3},{8,12},{9,13},{10,... | collective-permute-start | bytes 221192 | tf_op jit(solution)/shard_map/ppermute | solution.py:418
  69.8 2.4 %collective-permute-start.22 = (f32[144,128]{1,0:T(8,128)S(1)}, f32[144,128]{1,0:T(8,128)S(1)}, u32[]{:S(2)}, u32[]{:S(2)}) collective-permute-start(f32[144,128]{1,0:T(8,128)S(1)} %add_add_fusion.1), channel_id=1, source_target_pairs={{0,6},{1,7},{2,4},{3,5},{4,2},{5,3},{6,0},{7,1},{8,14},{9,15},{10,... | collective-permute-start | bytes 221192 | tf_op jit(solution)/shard_map/ppermute | solution.py:418
  72.2 2.8 %collective-permute-done.21 = f32[144,128]{1,0:T(8,128)S(1)} collective-permute-done((f32[144,128]{1,0:T(8,128)S(1)}, f32[144,128]{1,0:T(8,128)S(1)}, u32[]{:S(2)}, u32[]{:S(2)}) %collective-permute-start.21) | collective-permute-done | bytes 73760 | tf_op jit(solution)/shard_map/ppermute | solution.py:418
  75.0 1.1 %collective-permute-done.22 = f32[144,128]{1,0:T(8,128)S(1)} collective-permute-done((f32[144,128]{1,0:T(8,128)S(1)}, f32[144,128]{1,0:T(8,128)S(1)}, u32[]{:S(2)}, u32[]{:S(2)}) %collective-permute-start.22) | collective-permute-done | bytes 73760 | tf_op jit(solution)/shard_map/ppermute | solution.py:418
  76.1 1.5 %collective-permute-start.23 = (f32[144,128]{1,0:T(8,128)S(1)}, f32[144,128]{1,0:T(8,128)S(1)}, u32[]{:S(2)}, u32[]{:S(2)}) collective-permute-start(f32[144,128]{1,0:T(8,128)S(1)} %add_add_fusion), channel_id=1, source_target_pairs={{0,16},{1,17},{2,18},{3,19},{4,20},{5,21},{6,22},{7,23},{8,24},{9,... | collective-permute-start | bytes 221192 | tf_op jit(solution)/shard_map/ppermute | solution.py:418
  77.6 0.8 collective-permute-start.24
  78.4 1.3 %collective-permute-start.25 = (f32[144,128]{1,0:T(8,128)S(1)}, f32[144,128]{1,0:T(8,128)S(1)}, u32[]{:S(2)}, u32[]{:S(2)}) collective-permute-start(f32[144,128]{1,0:T(8,128)S(1)} %add_add_fusion), channel_id=1, source_target_pairs={{0,17},{1,16},{2,19},{3,18},{4,21},{5,20},{6,23},{7,22},{8,25},{9,... | collective-permute-start | bytes 221192 | tf_op jit(solution)/shard_map/ppermute | solution.py:418
  79.7 0.9 collective-permute-done.23
  80.5 1.5 %collective-permute-done.24 = f32[144,128]{1,0:T(8,128)S(1)} collective-permute-done((f32[144,128]{1,0:T(8,128)S(1)}, f32[144,128]{1,0:T(8,128)S(1)}, u32[]{:S(2)}, u32[]{:S(2)}) %collective-permute-start.24) | collective-permute-done | bytes 73760 | tf_op jit(solution)/shard_map/ppermute | solution.py:418
  82.0 1.7 %collective-permute-done.25 = f32[144,128]{1,0:T(8,128)S(1)} collective-permute-done((f32[144,128]{1,0:T(8,128)S(1)}, f32[144,128]{1,0:T(8,128)S(1)}, u32[]{:S(2)}, u32[]{:S(2)}) %collective-permute-start.25) | collective-permute-done | bytes 73760 | tf_op jit(solution)/shard_map/ppermute | solution.py:418
  84.0 1.4 %collective-permute-done.26.other_ref = f32[576,128]{1,0:T(8,128)S(1)} collective-permute-done((f32[576,128]{1,0:T(8,128)S(1)}, f32[576,128]{1,0:T(8,128)S(1)}, u32[]{:S(2)}, u32[]{:S(2)}) %collective-permute-start.26) | collective-permute-done | bytes 294944 | tf_op jit(solution)/shard_map/ppermute | solution.py:418
  85.3 1.6 %rotate.1 = f32[192,512]{1,0:T(8,128)} custom-call(f32[576,128]{1,0:T(8,128)S(1)} %pad_maximum_fusion.own_ref, f32[576,128]{1,0:T(8,128)S(1)} %collective-permute-done.26.other_ref, f32[192,512]{1,0:T(8,128)S(1)} %turned.1.rows_ref), custom_call_target="tpu_custom_call" | custom-call | tf_op jit(solution)/shard_map/rotate/pallas_call | solution.py:656
  (42 shorter events, 4.5 us)
Async XLA Ops:
  3.5 5.5 %collective-permute-start.1 = (f32[64,384]{1,0:T(8,128)S(1)}, f32[64,384]{1,0:T(8,128)S(1)}, u32[]{:S(2)}, u32[]{:S(2)}) collective-permute-start(f32[64,384]{1,0:T(8,128)S(1)} %get-tuple-element.38.near_before_ref), channel_id=1, source_target_pairs={{0,8},{8,0},{16,24},{24,16},{1,9},{9,1},{17,25},{25,17},{2,10},{10... | collective-permute-start | bytes 294920 | tf_op jit(solution)/shard_map/ppermute | solution.py:358
  4.0 5.7 %collective-permute-start = (f32[64,384]{1,0:T(8,128)S(1)}, f32[64,384]{1,0:T(8,128)S(1)}, u32[]{:S(2)}, u32[]{:S(2)}) collective-permute-start(f32[64,384]{1,0:T(8,128)S(1)} %get-tuple-element.37.far_before_ref), channel_id=1, source_target_pairs={{0,24},{8,16},{16,8},{24,0},{1,25},{9,17},{17,9},{25,1},{2,26},{10... | collective-permute-start | bytes 294920 | tf_op jit(solution)/shard_map/ppermute | solution.py:350
  6.7 5.6 %collective-permute-start.6 = (f32[192,128]{1,0:T(8,128)S(1)}, f32[192,128]{1,0:T(8,128)S(1)}, u32[]{:S(2)}, u32[]{:S(2)}) collective-permute-start(f32[192,128]{1,0:T(8,128)S(1)} %get-tuple-element.43), channel_id=1, source_target_pairs={{0,24},{8,16},{16,8},{24,0},{1,25},{9,17},{17,9},{25,1},{2,26},{10... | collective-permute-start | bytes 294920 | tf_op jit(solution)/shard_map/ppermute | solution.py:350
  9.3 5.5 %collective-permute-start.3 = (f32[64,384]{1,0:T(8,128)S(1)}, f32[64,384]{1,0:T(8,128)S(1)}, u32[]{:S(2)}, u32[]{:S(2)}) collective-permute-start(f32[64,384]{1,0:T(8,128)S(1)} %near_part.8.near_ref.near_before_ref), channel_id=1, source_target_pairs={{0,8},{8,0},{16,24},{24,16},{1,9},{9,1},{17,25},{25,17},{2,10},{10... | collective-permute-start | bytes 294920 | tf_op jit(solution)/shard_map/ppermute | solution.py:358
  10.0 5.3 %collective-permute-start.2 = (f32[64,384]{1,0:T(8,128)S(1)}, f32[64,384]{1,0:T(8,128)S(1)}, u32[]{:S(2)}, u32[]{:S(2)}) collective-permute-start(f32[64,384]{1,0:T(8,128)S(1)} %far_part.1.far_ref.before_ref.far_before_ref), channel_id=1, source_target_pairs={{0,24},{8,16},{16,8},{24,0},{1,25},{9,17},{17,9},{25,1},{2,26},{10... | collective-permute-start | bytes 294920 | tf_op jit(solution)/shard_map/ppermute | solution.py:350
  12.3 5.0 %collective-permute-start.7 = (f32[192,128]{1,0:T(8,128)S(1)}, f32[192,128]{1,0:T(8,128)S(1)}, u32[]{:S(2)}, u32[]{:S(2)}) collective-permute-start(f32[192,128]{1,0:T(8,128)S(1)} %collective-permute-done.6.mine_ref), channel_id=1, source_target_pairs={{0,1},{1,0},{2,3},{3,2},{4,5},{5,4},{6,7},{7,6},{8,9},{9,8},{10,11... | collective-permute-start | bytes 294920 | tf_op jit(solution)/shard_map/ppermute | solution.py:354
  15.0 4.8 %collective-permute-start.4 = (f32[64,384]{1,0:T(8,128)S(1)}, f32[64,384]{1,0:T(8,128)S(1)}, u32[]{:S(2)}, u32[]{:S(2)}) collective-permute-start(f32[64,384]{1,0:T(8,128)S(1)} %near_part.9.near_ref), channel_id=1, source_target_pairs={{0,8},{8,0},{16,24},{24,16},{1,9},{9,1},{17,25},{25,17},{2,10},{10... | collective-permute-start | bytes 294920 | tf_op jit(solution)/shard_map/ppermute | solution.py:358
  15.9 7.9 %collective-permute-start.5 = (f32[2,64,384]{2,1,0:T(8,128)S(1)}, f32[2,64,384]{2,1,0:T(8,128)S(1)}, u32[]{:S(2)}, u32[]{:S(2)}) collective-permute-start(f32[2,64,384]{2,1,0:T(8,128)S(1)} %get-tuple-element.42.sent_ref), channel_id=1, source_target_pairs={{0,24},{8,16},{16,8},{24,0},{1,25},{9,17},{17,9},{25,1},{2,26},{10... | collective-permute-start | bytes 589832 | tf_op jit(solution)/shard_map/ppermute | solution.py:350
  17.3 6.5 %collective-permute-start.8 = (f32[384,128]{1,0:T(8,128)S(1)}, f32[384,128]{1,0:T(8,128)S(1)}, u32[]{:S(2)}, u32[]{:S(2)}) collective-permute-start(f32[384,128]{1,0:T(8,128)S(1)} %pad_maximum_fusion.1), channel_id=1, source_target_pairs={{0,2},{1,3},{2,0},{3,1},{4,6},{5,7},{6,4},{7,5},{8,10},{9,11},{10,... | collective-permute-start | bytes 589832 | tf_op jit(solution)/shard_map/ppermute | solution.py:354
  20.0 1.4 %collective-permute-start.9 = (f32[64,384]{1,0:T(8,128)S(1)}, f32[64,384]{1,0:T(8,128)S(1)}, u32[]{:S(2)}, u32[]{:S(2)}) collective-permute-start(f32[64,384]{1,0:T(8,128)S(1)} %near_part.10.near_ref.near_before_ref), channel_id=1, source_target_pairs={{0,8},{8,0},{16,24},{24,16},{1,9},{9,1},{17,25},{25,17},{2,10},{10... | collective-permute-start | bytes 294920 | tf_op jit(solution)/shard_map/ppermute | solution.py:358
  21.6 4.2 %collective-permute-start.10 = (f32[64,384]{1,0:T(8,128)S(1)}, f32[64,384]{1,0:T(8,128)S(1)}, u32[]{:S(2)}, u32[]{:S(2)}) collective-permute-start(f32[64,384]{1,0:T(8,128)S(1)} %near_part.11.near_ref), channel_id=1, source_target_pairs={{0,8},{8,0},{16,24},{24,16},{1,9},{9,1},{17,25},{25,17},{2,10},{10... | collective-permute-start | bytes 294920 | tf_op jit(solution)/shard_map/ppermute | solution.py:358
  24.9 7.0 %collective-permute-start.11 = (f32[2,64,384]{2,1,0:T(8,128)S(1)}, f32[2,64,384]{2,1,0:T(8,128)S(1)}, u32[]{:S(2)}, u32[]{:S(2)}) collective-permute-start(f32[2,64,384]{2,1,0:T(8,128)S(1)} %get-tuple-element.50.sent_ref), channel_id=1, source_target_pairs={{0,24},{8,16},{16,8},{24,0},{1,25},{9,17},{17,9},{25,1},{2,26},{10... | collective-permute-start | bytes 589832 | tf_op jit(solution)/shard_map/ppermute | solution.py:350
  26.0 2.3 %collective-permute-start.12 = (f32[64,384]{1,0:T(8,128)S(1)}, f32[64,384]{1,0:T(8,128)S(1)}, u32[]{:S(2)}, u32[]{:S(2)}) collective-permute-start(f32[64,384]{1,0:T(8,128)S(1)} %near_part.12.near_ref.near_before_ref), channel_id=1, source_target_pairs={{0,8},{8,0},{16,24},{24,16},{1,9},{9,1},{17,25},{25,17},{2,10},{10... | collective-permute-start | bytes 294920 | tf_op jit(solution)/shard_map/ppermute | solution.py:358
  28.6 5.1 %collective-permute-start.13 = (f32[64,384]{1,0:T(8,128)S(1)}, f32[64,384]{1,0:T(8,128)S(1)}, u32[]{:S(2)}, u32[]{:S(2)}) collective-permute-start(f32[64,384]{1,0:T(8,128)S(1)} %near_part.13.near_ref), channel_id=1, source_target_pairs={{0,8},{8,0},{16,24},{24,16},{1,9},{9,1},{17,25},{25,17},{2,10},{10... | collective-permute-start | bytes 294920 | tf_op jit(solution)/shard_map/ppermute | solution.py:358
  32.8 7.2 %collective-permute-start.14 = (f32[2,64,384]{2,1,0:T(8,128)S(1)}, f32[2,64,384]{2,1,0:T(8,128)S(1)}, u32[]{:S(2)}, u32[]{:S(2)}) collective-permute-start(f32[2,64,384]{2,1,0:T(8,128)S(1)} %get-tuple-element.55.sent_ref), channel_id=1, source_target_pairs={{0,24},{8,16},{16,8},{24,0},{1,25},{9,17},{17,9},{25,1},{2,26},{10... | collective-permute-start | bytes 589832 | tf_op jit(solution)/shard_map/ppermute | solution.py:350
  33.9 2.1 %collective-permute-start.15 = (f32[64,384]{1,0:T(8,128)S(1)}, f32[64,384]{1,0:T(8,128)S(1)}, u32[]{:S(2)}, u32[]{:S(2)}) collective-permute-start(f32[64,384]{1,0:T(8,128)S(1)} %near_part.14.near_ref), channel_id=1, source_target_pairs={{0,8},{8,0},{16,24},{24,16},{1,9},{9,1},{17,25},{25,17},{2,10},{10... | collective-permute-start | bytes 294920 | tf_op jit(solution)/shard_map/ppermute | solution.py:358
  59.1 1.6 %collective-permute-start.16 = (f32[576,128]{1,0:T(8,128)S(1)}, f32[576,128]{1,0:T(8,128)S(1)}, u32[]{:S(2)}, u32[]{:S(2)}) collective-permute-start(f32[576,128]{1,0:T(8,128)S(1)} %get-tuple-element.57), channel_id=1, source_target_pairs={{0,8},{1,9},{2,10},{3,11},{4,12},{5,13},{6,14},{7,15},{8,0},{9,1},... | collective-permute-start | bytes 884744 | tf_op jit(solution)/shard_map/ppermute | solution.py:418
  60.7 4.6 %collective-permute-start.17 = (f32[144,128]{1,0:T(8,128)S(1)}, f32[144,128]{1,0:T(8,128)S(1)}, u32[]{:S(2)}, u32[]{:S(2)}) collective-permute-start(f32[144,128]{1,0:T(8,128)S(1)} %get-tuple-element.59), channel_id=1, source_target_pairs={{0,16},{1,17},{2,18},{3,19},{4,20},{5,21},{6,22},{7,23},{8,24},{9,... | collective-permute-start | bytes 221192 | tf_op jit(solution)/shard_map/ppermute | solution.py:418
  61.4 5.0 %collective-permute-start.18 = (f32[144,128]{1,0:T(8,128)S(1)}, f32[144,128]{1,0:T(8,128)S(1)}, u32[]{:S(2)}, u32[]{:S(2)}) collective-permute-start(f32[144,128]{1,0:T(8,128)S(1)} %get-tuple-element.60), channel_id=1, source_target_pairs={{0,1},{1,0},{2,3},{3,2},{4,5},{5,4},{6,7},{7,6},{8,9},{9,8},{10,11... | collective-permute-start | bytes 221192 | tf_op jit(solution)/shard_map/ppermute | solution.py:418
  62.5 5.3 %collective-permute-start.19 = (f32[144,128]{1,0:T(8,128)S(1)}, f32[144,128]{1,0:T(8,128)S(1)}, u32[]{:S(2)}, u32[]{:S(2)}) collective-permute-start(f32[144,128]{1,0:T(8,128)S(1)} %get-tuple-element.61), channel_id=1, source_target_pairs={{0,17},{1,16},{2,19},{3,18},{4,21},{5,20},{6,23},{7,22},{8,25},{9,... | collective-permute-start | bytes 221192 | tf_op jit(solution)/shard_map/ppermute | solution.py:418
  67.7 4.5 %collective-permute-start.20 = (f32[144,128]{1,0:T(8,128)S(1)}, f32[144,128]{1,0:T(8,128)S(1)}, u32[]{:S(2)}, u32[]{:S(2)}) collective-permute-start(f32[144,128]{1,0:T(8,128)S(1)} %add_add_fusion.1), channel_id=1, source_target_pairs={{0,2},{1,3},{2,0},{3,1},{4,6},{5,7},{6,4},{7,5},{8,10},{9,11},{10,... | collective-permute-start | bytes 221192 | tf_op jit(solution)/shard_map/ppermute | solution.py:418
  68.2 6.8 %collective-permute-start.21 = (f32[144,128]{1,0:T(8,128)S(1)}, f32[144,128]{1,0:T(8,128)S(1)}, u32[]{:S(2)}, u32[]{:S(2)}) collective-permute-start(f32[144,128]{1,0:T(8,128)S(1)} %add_add_fusion.1), channel_id=1, source_target_pairs={{0,4},{1,5},{2,6},{3,7},{4,0},{5,1},{6,2},{7,3},{8,12},{9,13},{10,... | collective-permute-start | bytes 221192 | tf_op jit(solution)/shard_map/ppermute | solution.py:418
  69.8 6.3 %collective-permute-start.22 = (f32[144,128]{1,0:T(8,128)S(1)}, f32[144,128]{1,0:T(8,128)S(1)}, u32[]{:S(2)}, u32[]{:S(2)}) collective-permute-start(f32[144,128]{1,0:T(8,128)S(1)} %add_add_fusion.1), channel_id=1, source_target_pairs={{0,6},{1,7},{2,4},{3,5},{4,2},{5,3},{6,0},{7,1},{8,14},{9,15},{10,... | collective-permute-start | bytes 221192 | tf_op jit(solution)/shard_map/ppermute | solution.py:418
  76.1 4.4 %collective-permute-start.23 = (f32[144,128]{1,0:T(8,128)S(1)}, f32[144,128]{1,0:T(8,128)S(1)}, u32[]{:S(2)}, u32[]{:S(2)}) collective-permute-start(f32[144,128]{1,0:T(8,128)S(1)} %add_add_fusion), channel_id=1, source_target_pairs={{0,16},{1,17},{2,18},{3,19},{4,20},{5,21},{6,22},{7,23},{8,24},{9,... | collective-permute-start | bytes 221192 | tf_op jit(solution)/shard_map/ppermute | solution.py:418
  77.6 4.4 %collective-permute-start.24 = (f32[144,128]{1,0:T(8,128)S(1)}, f32[144,128]{1,0:T(8,128)S(1)}, u32[]{:S(2)}, u32[]{:S(2)}) collective-permute-start(f32[144,128]{1,0:T(8,128)S(1)} %add_add_fusion), channel_id=1, source_target_pairs={{0,1},{1,0},{2,3},{3,2},{4,5},{5,4},{6,7},{7,6},{8,9},{9,8},{10,11... | collective-permute-start | bytes 221192 | tf_op jit(solution)/shard_map/ppermute | solution.py:418
  78.4 5.3 %collective-permute-start.25 = (f32[144,128]{1,0:T(8,128)S(1)}, f32[144,128]{1,0:T(8,128)S(1)}, u32[]{:S(2)}, u32[]{:S(2)}) collective-permute-start(f32[144,128]{1,0:T(8,128)S(1)} %add_add_fusion), channel_id=1, source_target_pairs={{0,17},{1,16},{2,19},{3,18},{4,21},{5,20},{6,23},{7,22},{8,25},{9,... | collective-permute-start | bytes 221192 | tf_op jit(solution)/shard_map/ppermute | solution.py:418
  83.7 1.6 %collective-permute-start.26 = (f32[576,128]{1,0:T(8,128)S(1)}, f32[576,128]{1,0:T(8,128)S(1)}, u32[]{:S(2)}, u32[]{:S(2)}) collective-permute-start(f32[576,128]{1,0:T(8,128)S(1)} %pad_maximum_fusion.own_ref), channel_id=1, source_target_pairs={{0,8},{1,9},{2,10},{3,11},{4,12},{5,13},{6,14},{7,15},{8,0},{9,1},... | collective-permute-start | bytes 884744 | tf_op jit(solution)/shard_map/ppermute | solution.py:418

commit v6 on v5

--- a/solution.py
+++ b/solution.py
@@ -534,12 +534,13 @@
     rows_ref[...] = rows
     tiles, half = rows.shape[0] // TILE, TILE // 2
     hi, lo = split(rows)
+    hi_turned, lo_turned = hi.T, lo.T
     at, tops = 0, len(tile_pairs(tiles)) * TILE
     lasts = tops + tiles * half
     for i in range(tiles):
         here, there = slice(i * TILE, (i + 1) * TILE), slice(i * TILE, None)
         both = jnp.concatenate([hi[here], lo[here]], axis=0)
-        strip = dot_split(hi[here], both, hi[there], lo[there], NT)
+        strip = dot_split(hi[here], both, hi_turned[:, there], lo_turned[:, there], NN)
         packed[tops + i * half : tops + (i + 1) * half, :] = strip[:half, :TILE]
         last = strip[half:, half:TILE]
         if i % 2 == 0:

time: 87.2 us -> 87.2 us (level)
  no operation moved by 1% of the time
where the time goes in v6:
time: 87.2 us; the launch traced here: 87 us
  starting transfers between devices  25.1 us (29%)
  waiting for transfers between devices  23.7 us (27%)
  Pallas kernels  18.7 us (21%)
  blocking collectives  17.6 us (20%)
  between operations  1.65 us (2%)
    all_to_all x1, blocking collectives, regroup(): lax.all_to_all(parts, 'wide', split_axis=0, concat_axis=0, tiled=True)  17.6 us
    ppermute x11, waiting for transfers between devices, swap(): return lax.ppermute(x, ('narrow', 'wide'), pair_perm(mask))  14.2 us
    pallas_call x23, Pallas kernels, step_call(): pl.pallas_call(kernel, in_specs=[VM] * (len(operands) + 2), out_specs=[VM...  12.6 us
    ppermute x11, starting transfers between devices, swap(): return lax.ppermute(x, ('narrow', 'wide'), pair_perm(mask))  11.7 us
    ppermute x6, waiting for transfers between devices, far_swap(): lax.ppermute(x, 'narrow', [(i, (i + 1) % size if i % 2 else (i - 1) % siz...  6.88 us
    ppermute x6, starting transfers between devices, far_swap(): lax.ppermute(x, 'narrow', [(i, (i + 1) % size if i % 2 else (i - 1) % siz...  6.39 us
    ppermute x8, starting transfers between devices, near_swap(): lax.ppermute(x, 'narrow', [(i, i ^ 1) for i in range(lax.axis_size('narro...  3.86 us
    pallas_call x1, Pallas kernels, spread_part(): pl.pallas_call(functools.partial(spread_kernel, total_blocks), in_specs=[...  3.51 us
  transfers between devices with their start and end apart: 27, of which 17 were waited for; matrix products, arithmetic and copies ran while one was open for 0% of the time, Pallas kernels for 14%

profile of v6, /device:TPU:0, one launch (start us, length us, event | category | flops | bytes accessed | tf_op | source)
XLA Modules:
  0.0 87.0 jit_solution(9786887252493253407)
XLA Ops:
  0.0 3.5 %spread_part.1 = (f32[64,384]{1,0:T(8,128)S(1)}, f32[64,384]{1,0:T(8,128)S(1)}, f32[64,1536]{1,0:T(8,128)S(1)}, f32[192,128]{1,0:T(8,128)S(1)}, bf16[6,1024,256]...) custom-call(s32[5,12]{1,0:T(8,128)} %bitcast.3, f32[64,1536]{1,0:T(8,128)} %vectors_hbm.1, f32[12,5,128,128]{3,2,1,0:T(8,128)} %blocks_hbm.1), custom_call_target="tpu_custom_call" | custom-call | tf_op jit(solution)/shard_map/spread_part/pallas_call | solution.py:116
  3.5 0.5 collective-permute-start.1
  4.0 2.6 %collective-permute-start = (f32[64,384]{1,0:T(8,128)S(1)}, f32[64,384]{1,0:T(8,128)S(1)}, u32[]{:S(2)}, u32[]{:S(2)}) collective-permute-start(f32[64,384]{1,0:T(8,128)S(1)} %get-tuple-element.37.far_before_ref), channel_id=1, source_target_pairs={{0,24},{8,16},{16,8},{24,0},{1,25},{9,17},{17,9},{25,1},{2,26},{10... | collective-permute-start | bytes 294920 | tf_op jit(solution)/shard_map/ppermute | solution.py:350
  8.1 0.9 %first_part.1.mid_ref.mid_before_ref = f32[64,1536]{1,0:T(8,128)S(1)} custom-call(f32[2,256]{1,0:T(2,128)S(1)} %concatenate.12.terms_ref, f32[64,1536]{1,0:T(8,128)S(1)} %get-tuple-element.34.vectors_ref.mid_before_ref, bf16[6,1024,256]{2,1,0:T(8,128)(2,1)S(1)} %get-tuple-element.35.hi_ref.refs_2_.refs_1_, ...), custom_call_target="tpu_custom_call" | custom-call | flops 603979776 | bytes 786432 | tf_op jit(solution)/shard_map/first_part/pallas_call | solution.py:215
  10.0 2.3 %collective-permute-start.2 = (f32[64,384]{1,0:T(8,128)S(1)}, f32[64,384]{1,0:T(8,128)S(1)}, u32[]{:S(2)}, u32[]{:S(2)}) collective-permute-start(f32[64,384]{1,0:T(8,128)S(1)} %far_part.1.far_ref.before_ref.far_before_ref), channel_id=1, source_target_pairs={{0,24},{8,16},{16,8},{24,0},{1,25},{9,17},{17,9},{25,1},{2,26},{10... | collective-permute-start | bytes 294920 | tf_op jit(solution)/shard_map/ppermute | solution.py:350
  12.3 1.5 %collective-permute-start.7 = (f32[192,128]{1,0:T(8,128)S(1)}, f32[192,128]{1,0:T(8,128)S(1)}, u32[]{:S(2)}, u32[]{:S(2)}) collective-permute-start(f32[192,128]{1,0:T(8,128)S(1)} %collective-permute-done.6.mine_ref), channel_id=1, source_target_pairs={{0,1},{1,0},{2,3},{3,2},{4,5},{5,4},{6,7},{7,6},{8,9},{9,8},{10,11... | collective-permute-start | bytes 294920 | tf_op jit(solution)/shard_map/ppermute | solution.py:354
  13.8 1.0 %local_part.4.mid_ref = f32[64,1536]{1,0:T(8,128)S(1)} custom-call(f32[2,256]{1,0:T(2,128)S(1)} %concatenate.12.terms_ref, f32[64,384]{1,0:T(8,128)S(1)} %far_part.1.far_ref.before_ref.far_before_ref, f32[64,1536]{1,0:T(8,128)S(1)} %first_part.1.mid_ref.mid_before_ref, f32[64,384]{1,0:T(8,128)S(1)} %near_part.8.near_ref.near_before_ref, ...), custom_call_target="tpu_custom_call" | custom-call | flops 150994944 | bytes 196608 | tf_op jit(solution)/shard_map/local_part/pallas_call | solution.py:215
  15.3 0.6 turn_one.1
  15.9 1.3 %collective-permute-start.5 = (f32[2,64,384]{2,1,0:T(8,128)S(1)}, f32[2,64,384]{2,1,0:T(8,128)S(1)}, u32[]{:S(2)}, u32[]{:S(2)}) collective-permute-start(f32[2,64,384]{2,1,0:T(8,128)S(1)} %get-tuple-element.42.sent_ref), channel_id=1, source_target_pairs={{0,24},{8,16},{16,8},{24,0},{1,25},{9,17},{17,9},{25,1},{2,26},{10... | collective-permute-start | bytes 589832 | tf_op jit(solution)/shard_map/ppermute | solution.py:350
  17.3 1.6 %collective-permute-start.8 = (f32[384,128]{1,0:T(8,128)S(1)}, f32[384,128]{1,0:T(8,128)S(1)}, u32[]{:S(2)}, u32[]{:S(2)}) collective-permute-start(f32[384,128]{1,0:T(8,128)S(1)} %pad_maximum_fusion.1), channel_id=1, source_target_pairs={{0,2},{1,3},{2,0},{3,1},{4,6},{5,7},{6,4},{7,5},{8,10},{9,11},{10,... | collective-permute-start | bytes 589832 | tf_op jit(solution)/shard_map/ppermute | solution.py:354
  18.9 0.8 local_part.5
  20.1 0.8 second_part.3.mid_ref
  20.9 0.5 collective-permute-done.9.halo_ref
  21.8 2.0 %collective-permute-done.8.two_ref = f32[384,128]{1,0:T(8,128)S(1)} collective-permute-done((f32[384,128]{1,0:T(8,128)S(1)}, f32[384,128]{1,0:T(8,128)S(1)}, u32[]{:S(2)}, u32[]{:S(2)}) %collective-permute-start.8) | collective-permute-done | bytes 196640 | tf_op jit(solution)/shard_map/ppermute | solution.py:354
  23.9 1.0 %turn_two.2 = (f32[64,384]{1,0:T(8,128)S(1)}, f32[64,768]{1,0:T(8,128)S(1)}, f32[2,64,384]{2,1,0:T(8,128)S(1)}) custom-call(f32[2,256]{1,0:T(2,128)S(1)} %concatenate.12.terms_ref, f32[64,1536]{1,0:T(8,128)S(1)} %second_part.3.mid_ref, f32[2,64,384]{2,1,0:T(8,128)S(1)} %get-tuple-element.42.sent_ref, f32[2,64,384]{2,1,0:T(8,128)S(1)} %collective-permute-done.5.got_ref, ...), custom_call_target="tpu_custom_call" | custom-call | flops 603979776 | bytes 786432 | tf_op jit(solution)/shard_map/turn_two/pallas_call | solution.py:215
  25.0 0.8 local_part.6
  26.0 1.4 %collective-permute-start.12 = (f32[64,384]{1,0:T(8,128)S(1)}, f32[64,384]{1,0:T(8,128)S(1)}, u32[]{:S(2)}, u32[]{:S(2)}) collective-permute-start(f32[64,384]{1,0:T(8,128)S(1)} %near_part.12.near_ref.near_before_ref), channel_id=1, source_target_pairs={{0,8},{8,0},{16,24},{24,16},{1,9},{9,1},{17,25},{25,17},{2,10},{10... | collective-permute-start | bytes 294920 | tf_op jit(solution)/shard_map/ppermute | solution.py:358
  27.4 0.8 second_part.4.mid_ref
  28.6 0.4 collective-permute-start.13
  29.3 2.6 %collective-permute-done.11.got_ref = f32[2,64,384]{2,1,0:T(8,128)S(1)} collective-permute-done((f32[2,64,384]{2,1,0:T(8,128)S(1)}, f32[2,64,384]{2,1,0:T(8,128)S(1)}, u32[]{:S(2)}, u32[]{:S(2)}) %collective-permute-start.11) | collective-permute-done | bytes 196640 | tf_op jit(solution)/shard_map/ppermute | solution.py:350
  31.9 0.9 %turn_two.3 = (f32[64,384]{1,0:T(8,128)S(1)}, f32[64,768]{1,0:T(8,128)S(1)}, f32[2,64,384]{2,1,0:T(8,128)S(1)}) custom-call(f32[2,256]{1,0:T(2,128)S(1)} %concatenate.12.terms_ref, f32[64,1536]{1,0:T(8,128)S(1)} %second_part.4.mid_ref, f32[2,64,384]{2,1,0:T(8,128)S(1)} %get-tuple-element.50.sent_ref, f32[2,64,384]{2,1,0:T(8,128)S(1)} %collective-permute-done.11.got_ref, ...), custom_call_target="tpu_custom_call" | custom-call | flops 603979776 | bytes 786432 | tf_op jit(solution)/shard_map/turn_two/pallas_call | solution.py:215
  32.9 0.8 local_part.7
  33.9 1.0 %collective-permute-start.15 = (f32[64,384]{1,0:T(8,128)S(1)}, f32[64,384]{1,0:T(8,128)S(1)}, u32[]{:S(2)}, u32[]{:S(2)}) collective-permute-start(f32[64,384]{1,0:T(8,128)S(1)} %near_part.14.near_ref), channel_id=1, source_target_pairs={{0,8},{8,0},{16,24},{24,16},{1,9},{9,1},{17,25},{25,17},{2,10},{10... | collective-permute-start | bytes 294920 | tf_op jit(solution)/shard_map/ppermute | solution.py:358
  35.2 0.8 second_part.5.mid_ref
  36.3 3.7 %collective-permute-done.14.got_ref = f32[2,64,384]{2,1,0:T(8,128)S(1)} collective-permute-done((f32[2,64,384]{2,1,0:T(8,128)S(1)}, f32[2,64,384]{2,1,0:T(8,128)S(1)}, u32[]{:S(2)}, u32[]{:S(2)}) %collective-permute-start.14) | collective-permute-done | bytes 196640 | tf_op jit(solution)/shard_map/ppermute | solution.py:350
  40.0 0.7 last_part.1
  40.7 17.6 %all_to_all.5.parts_ref = f32[8,96,128]{2,1,0:T(8,128)S(1)} all-to-all(f32[8,96,128]{2,1,0:T(8,128)S(1)} %last_part.1), channel_id=1, replica_groups=mesh['narrow'=4,'wide'=8] {'wide'}, dimensions={0} | all-to-all | bytes 786432 | tf_op jit(solution)/shard_map/all_to_all | solution.py:677
  58.3 0.7 gram.1
  59.1 1.6 %collective-permute-done.16.refs_1_ = f32[576,128]{1,0:T(8,128)S(1)} collective-permute-done((f32[576,128]{1,0:T(8,128)S(1)}, f32[576,128]{1,0:T(8,128)S(1)}, u32[]{:S(2)}, u32[]{:S(2)}) %collective-permute-start.16) | collective-permute-done | bytes 294944 | tf_op jit(solution)/shard_map/ppermute | solution.py:418
  60.7 0.6 collective-permute-start.17
  61.4 1.1 %collective-permute-start.18 = (f32[144,128]{1,0:T(8,128)S(1)}, f32[144,128]{1,0:T(8,128)S(1)}, u32[]{:S(2)}, u32[]{:S(2)}) collective-permute-start(f32[144,128]{1,0:T(8,128)S(1)} %get-tuple-element.60), channel_id=1, source_target_pairs={{0,1},{1,0},{2,3},{3,2},{4,5},{5,4},{6,7},{7,6},{8,9},{9,8},{10,11... | collective-permute-start | bytes 221192 | tf_op jit(solution)/shard_map/ppermute | solution.py:418
  62.5 1.8 %collective-permute-start.19 = (f32[144,128]{1,0:T(8,128)S(1)}, f32[144,128]{1,0:T(8,128)S(1)}, u32[]{:S(2)}, u32[]{:S(2)}) collective-permute-start(f32[144,128]{1,0:T(8,128)S(1)} %get-tuple-element.61), channel_id=1, source_target_pairs={{0,17},{1,16},{2,19},{3,18},{4,21},{5,20},{6,23},{7,22},{8,25},{9,... | collective-permute-start | bytes 221192 | tf_op jit(solution)/shard_map/ppermute | solution.py:418
  64.3 1.1 %collective-permute-done.17 = f32[144,128]{1,0:T(8,128)S(1)} collective-permute-done((f32[144,128]{1,0:T(8,128)S(1)}, f32[144,128]{1,0:T(8,128)S(1)}, u32[]{:S(2)}, u32[]{:S(2)}) %collective-permute-start.17) | collective-permute-done | bytes 73760 | tf_op jit(solution)/shard_map/ppermute | solution.py:418
  65.4 1.0 %collective-permute-done.18 = f32[144,128]{1,0:T(8,128)S(1)} collective-permute-done((f32[144,128]{1,0:T(8,128)S(1)}, f32[144,128]{1,0:T(8,128)S(1)}, u32[]{:S(2)}, u32[]{:S(2)}) %collective-permute-start.18) | collective-permute-done | bytes 73760 | tf_op jit(solution)/shard_map/ppermute | solution.py:418
  66.3 1.4 %collective-permute-done.19 = f32[144,128]{1,0:T(8,128)S(1)} collective-permute-done((f32[144,128]{1,0:T(8,128)S(1)}, f32[144,128]{1,0:T(8,128)S(1)}, u32[]{:S(2)}, u32[]{:S(2)}) %collective-permute-start.19) | collective-permute-done | bytes 73760 | tf_op jit(solution)/shard_map/ppermute | solution.py:418
  67.7 0.5 collective-permute-start.20
  68.2 1.6 %collective-permute-start.21 = (f32[144,128]{1,0:T(8,128)S(1)}, f32[144,128]{1,0:T(8,128)S(1)}, u32[]{:S(2)}, u32[]{:S(2)}) collective-permute-start(f32[144,128]{1,0:T(8,128)S(1)} %add_add_fusion.1), channel_id=1, source_target_pairs={{0,4},{1,5},{2,6},{3,7},{4,0},{5,1},{6,2},{7,3},{8,12},{9,13},{10,... | collective-permute-start | bytes 221192 | tf_op jit(solution)/shard_map/ppermute | solution.py:418
  69.8 2.4 %collective-permute-start.22 = (f32[144,128]{1,0:T(8,128)S(1)}, f32[144,128]{1,0:T(8,128)S(1)}, u32[]{:S(2)}, u32[]{:S(2)}) collective-permute-start(f32[144,128]{1,0:T(8,128)S(1)} %add_add_fusion.1), channel_id=1, source_target_pairs={{0,6},{1,7},{2,4},{3,5},{4,2},{5,3},{6,0},{7,1},{8,14},{9,15},{10,... | collective-permute-start | bytes 221192 | tf_op jit(solution)/shard_map/ppermute | solution.py:418
  72.2 2.8 %collective-permute-done.21 = f32[144,128]{1,0:T(8,128)S(1)} collective-permute-done((f32[144,128]{1,0:T(8,128)S(1)}, f32[144,128]{1,0:T(8,128)S(1)}, u32[]{:S(2)}, u32[]{:S(2)}) %collective-permute-start.21) | collective-permute-done | bytes 73760 | tf_op jit(solution)/shard_map/ppermute | solution.py:418
  75.0 1.1 %collective-permute-done.22 = f32[144,128]{1,0:T(8,128)S(1)} collective-permute-done((f32[144,128]{1,0:T(8,128)S(1)}, f32[144,128]{1,0:T(8,128)S(1)}, u32[]{:S(2)}, u32[]{:S(2)}) %collective-permute-start.22) | collective-permute-done | bytes 73760 | tf_op jit(solution)/shard_map/ppermute | solution.py:418
  76.1 1.5 %collective-permute-start.23 = (f32[144,128]{1,0:T(8,128)S(1)}, f32[144,128]{1,0:T(8,128)S(1)}, u32[]{:S(2)}, u32[]{:S(2)}) collective-permute-start(f32[144,128]{1,0:T(8,128)S(1)} %add_add_fusion), channel_id=1, source_target_pairs={{0,16},{1,17},{2,18},{3,19},{4,20},{5,21},{6,22},{7,23},{8,24},{9,... | collective-permute-start | bytes 221192 | tf_op jit(solution)/shard_map/ppermute | solution.py:418
  77.6 0.8 collective-permute-start.24
  78.4 1.3 %collective-permute-start.25 = (f32[144,128]{1,0:T(8,128)S(1)}, f32[144,128]{1,0:T(8,128)S(1)}, u32[]{:S(2)}, u32[]{:S(2)}) collective-permute-start(f32[144,128]{1,0:T(8,128)S(1)} %add_add_fusion), channel_id=1, source_target_pairs={{0,17},{1,16},{2,19},{3,18},{4,21},{5,20},{6,23},{7,22},{8,25},{9,... | collective-permute-start | bytes 221192 | tf_op jit(solution)/shard_map/ppermute | solution.py:418
  79.7 0.9 collective-permute-done.23
  80.5 1.5 %collective-permute-done.24 = f32[144,128]{1,0:T(8,128)S(1)} collective-permute-done((f32[144,128]{1,0:T(8,128)S(1)}, f32[144,128]{1,0:T(8,128)S(1)}, u32[]{:S(2)}, u32[]{:S(2)}) %collective-permute-start.24) | collective-permute-done | bytes 73760 | tf_op jit(solution)/shard_map/ppermute | solution.py:418
  82.0 1.7 %collective-permute-done.25 = f32[144,128]{1,0:T(8,128)S(1)} collective-permute-done((f32[144,128]{1,0:T(8,128)S(1)}, f32[144,128]{1,0:T(8,128)S(1)}, u32[]{:S(2)}, u32[]{:S(2)}) %collective-permute-start.25) | collective-permute-done | bytes 73760 | tf_op jit(solution)/shard_map/ppermute | solution.py:418
  84.0 1.4 %collective-permute-done.26.other_ref = f32[576,128]{1,0:T(8,128)S(1)} collective-permute-done((f32[576,128]{1,0:T(8,128)S(1)}, f32[576,128]{1,0:T(8,128)S(1)}, u32[]{:S(2)}, u32[]{:S(2)}) %collective-permute-start.26) | collective-permute-done | bytes 294944 | tf_op jit(solution)/shard_map/ppermute | solution.py:418
  85.3 1.6 %rotate.1 = f32[192,512]{1,0:T(8,128)} custom-call(f32[576,128]{1,0:T(8,128)S(1)} %pad_maximum_fusion.own_ref, f32[576,128]{1,0:T(8,128)S(1)} %collective-permute-done.26.other_ref, f32[192,512]{1,0:T(8,128)S(1)} %turned.1.rows_ref), custom_call_target="tpu_custom_call" | custom-call | tf_op jit(solution)/shard_map/rotate/pallas_call | solution.py:657
  (42 shorter events, 4.5 us)
Async XLA Ops:
  3.5 5.5 %collective-permute-start.1 = (f32[64,384]{1,0:T(8,128)S(1)}, f32[64,384]{1,0:T(8,128)S(1)}, u32[]{:S(2)}, u32[]{:S(2)}) collective-permute-start(f32[64,384]{1,0:T(8,128)S(1)} %get-tuple-element.38.near_before_ref), channel_id=1, source_target_pairs={{0,8},{8,0},{16,24},{24,16},{1,9},{9,1},{17,25},{25,17},{2,10},{10... | collective-permute-start | bytes 294920 | tf_op jit(solution)/shard_map/ppermute | solution.py:358
  4.0 5.7 %collective-permute-start = (f32[64,384]{1,0:T(8,128)S(1)}, f32[64,384]{1,0:T(8,128)S(1)}, u32[]{:S(2)}, u32[]{:S(2)}) collective-permute-start(f32[64,384]{1,0:T(8,128)S(1)} %get-tuple-element.37.far_before_ref), channel_id=1, source_target_pairs={{0,24},{8,16},{16,8},{24,0},{1,25},{9,17},{17,9},{25,1},{2,26},{10... | collective-permute-start | bytes 294920 | tf_op jit(solution)/shard_map/ppermute | solution.py:350
  6.7 5.6 %collective-permute-start.6 = (f32[192,128]{1,0:T(8,128)S(1)}, f32[192,128]{1,0:T(8,128)S(1)}, u32[]{:S(2)}, u32[]{:S(2)}) collective-permute-start(f32[192,128]{1,0:T(8,128)S(1)} %get-tuple-element.43), channel_id=1, source_target_pairs={{0,24},{8,16},{16,8},{24,0},{1,25},{9,17},{17,9},{25,1},{2,26},{10... | collective-permute-start | bytes 294920 | tf_op jit(solution)/shard_map/ppermute | solution.py:350
  9.3 5.5 %collective-permute-start.3 = (f32[64,384]{1,0:T(8,128)S(1)}, f32[64,384]{1,0:T(8,128)S(1)}, u32[]{:S(2)}, u32[]{:S(2)}) collective-permute-start(f32[64,384]{1,0:T(8,128)S(1)} %near_part.8.near_ref.near_before_ref), channel_id=1, source_target_pairs={{0,8},{8,0},{16,24},{24,16},{1,9},{9,1},{17,25},{25,17},{2,10},{10... | collective-permute-start | bytes 294920 | tf_op jit(solution)/shard_map/ppermute | solution.py:358
  10.0 5.3 %collective-permute-start.2 = (f32[64,384]{1,0:T(8,128)S(1)}, f32[64,384]{1,0:T(8,128)S(1)}, u32[]{:S(2)}, u32[]{:S(2)}) collective-permute-start(f32[64,384]{1,0:T(8,128)S(1)} %far_part.1.far_ref.before_ref.far_before_ref), channel_id=1, source_target_pairs={{0,24},{8,16},{16,8},{24,0},{1,25},{9,17},{17,9},{25,1},{2,26},{10... | collective-permute-start | bytes 294920 | tf_op jit(solution)/shard_map/ppermute | solution.py:350
  12.3 5.0 %collective-permute-start.7 = (f32[192,128]{1,0:T(8,128)S(1)}, f32[192,128]{1,0:T(8,128)S(1)}, u32[]{:S(2)}, u32[]{:S(2)}) collective-permute-start(f32[192,128]{1,0:T(8,128)S(1)} %collective-permute-done.6.mine_ref), channel_id=1, source_target_pairs={{0,1},{1,0},{2,3},{3,2},{4,5},{5,4},{6,7},{7,6},{8,9},{9,8},{10,11... | collective-permute-start | bytes 294920 | tf_op jit(solution)/shard_map/ppermute | solution.py:354
  15.0 4.8 %collective-permute-start.4 = (f32[64,384]{1,0:T(8,128)S(1)}, f32[64,384]{1,0:T(8,128)S(1)}, u32[]{:S(2)}, u32[]{:S(2)}) collective-permute-start(f32[64,384]{1,0:T(8,128)S(1)} %near_part.9.near_ref), channel_id=1, source_target_pairs={{0,8},{8,0},{16,24},{24,16},{1,9},{9,1},{17,25},{25,17},{2,10},{10... | collective-permute-start | bytes 294920 | tf_op jit(solution)/shard_map/ppermute | solution.py:358
  15.9 7.9 %collective-permute-start.5 = (f32[2,64,384]{2,1,0:T(8,128)S(1)}, f32[2,64,384]{2,1,0:T(8,128)S(1)}, u32[]{:S(2)}, u32[]{:S(2)}) collective-permute-start(f32[2,64,384]{2,1,0:T(8,128)S(1)} %get-tuple-element.42.sent_ref), channel_id=1, source_target_pairs={{0,24},{8,16},{16,8},{24,0},{1,25},{9,17},{17,9},{25,1},{2,26},{10... | collective-permute-start | bytes 589832 | tf_op jit(solution)/shard_map/ppermute | solution.py:350
  17.3 6.5 %collective-permute-start.8 = (f32[384,128]{1,0:T(8,128)S(1)}, f32[384,128]{1,0:T(8,128)S(1)}, u32[]{:S(2)}, u32[]{:S(2)}) collective-permute-start(f32[384,128]{1,0:T(8,128)S(1)} %pad_maximum_fusion.1), channel_id=1, source_target_pairs={{0,2},{1,3},{2,0},{3,1},{4,6},{5,7},{6,4},{7,5},{8,10},{9,11},{10,... | collective-permute-start | bytes 589832 | tf_op jit(solution)/shard_map/ppermute | solution.py:354
  20.0 1.4 %collective-permute-start.9 = (f32[64,384]{1,0:T(8,128)S(1)}, f32[64,384]{1,0:T(8,128)S(1)}, u32[]{:S(2)}, u32[]{:S(2)}) collective-permute-start(f32[64,384]{1,0:T(8,128)S(1)} %near_part.10.near_ref.near_before_ref), channel_id=1, source_target_pairs={{0,8},{8,0},{16,24},{24,16},{1,9},{9,1},{17,25},{25,17},{2,10},{10... | collective-permute-start | bytes 294920 | tf_op jit(solution)/shard_map/ppermute | solution.py:358
  21.6 4.2 %collective-permute-start.10 = (f32[64,384]{1,0:T(8,128)S(1)}, f32[64,384]{1,0:T(8,128)S(1)}, u32[]{:S(2)}, u32[]{:S(2)}) collective-permute-start(f32[64,384]{1,0:T(8,128)S(1)} %near_part.11.near_ref), channel_id=1, source_target_pairs={{0,8},{8,0},{16,24},{24,16},{1,9},{9,1},{17,25},{25,17},{2,10},{10... | collective-permute-start | bytes 294920 | tf_op jit(solution)/shard_map/ppermute | solution.py:358
  24.9 7.0 %collective-permute-start.11 = (f32[2,64,384]{2,1,0:T(8,128)S(1)}, f32[2,64,384]{2,1,0:T(8,128)S(1)}, u32[]{:S(2)}, u32[]{:S(2)}) collective-permute-start(f32[2,64,384]{2,1,0:T(8,128)S(1)} %get-tuple-element.50.sent_ref), channel_id=1, source_target_pairs={{0,24},{8,16},{16,8},{24,0},{1,25},{9,17},{17,9},{25,1},{2,26},{10... | collective-permute-start | bytes 589832 | tf_op jit(solution)/shard_map/ppermute | solution.py:350
  26.0 2.3 %collective-permute-start.12 = (f32[64,384]{1,0:T(8,128)S(1)}, f32[64,384]{1,0:T(8,128)S(1)}, u32[]{:S(2)}, u32[]{:S(2)}) collective-permute-start(f32[64,384]{1,0:T(8,128)S(1)} %near_part.12.near_ref.near_before_ref), channel_id=1, source_target_pairs={{0,8},{8,0},{16,24},{24,16},{1,9},{9,1},{17,25},{25,17},{2,10},{10... | collective-permute-start | bytes 294920 | tf_op jit(solution)/shard_map/ppermute | solution.py:358
  28.6 5.1 %collective-permute-start.13 = (f32[64,384]{1,0:T(8,128)S(1)}, f32[64,384]{1,0:T(8,128)S(1)}, u32[]{:S(2)}, u32[]{:S(2)}) collective-permute-start(f32[64,384]{1,0:T(8,128)S(1)} %near_part.13.near_ref), channel_id=1, source_target_pairs={{0,8},{8,0},{16,24},{24,16},{1,9},{9,1},{17,25},{25,17},{2,10},{10... | collective-permute-start | bytes 294920 | tf_op jit(solution)/shard_map/ppermute | solution.py:358
  32.8 7.2 %collective-permute-start.14 = (f32[2,64,384]{2,1,0:T(8,128)S(1)}, f32[2,64,384]{2,1,0:T(8,128)S(1)}, u32[]{:S(2)}, u32[]{:S(2)}) collective-permute-start(f32[2,64,384]{2,1,0:T(8,128)S(1)} %get-tuple-element.55.sent_ref), channel_id=1, source_target_pairs={{0,24},{8,16},{16,8},{24,0},{1,25},{9,17},{17,9},{25,1},{2,26},{10... | collective-permute-start | bytes 589832 | tf_op jit(solution)/shard_map/ppermute | solution.py:350
  33.9 2.1 %collective-permute-start.15 = (f32[64,384]{1,0:T(8,128)S(1)}, f32[64,384]{1,0:T(8,128)S(1)}, u32[]{:S(2)}, u32[]{:S(2)}) collective-permute-start(f32[64,384]{1,0:T(8,128)S(1)} %near_part.14.near_ref), channel_id=1, source_target_pairs={{0,8},{8,0},{16,24},{24,16},{1,9},{9,1},{17,25},{25,17},{2,10},{10... | collective-permute-start | bytes 294920 | tf_op jit(solution)/shard_map/ppermute | solution.py:358
  59.1 1.6 %collective-permute-start.16 = (f32[576,128]{1,0:T(8,128)S(1)}, f32[576,128]{1,0:T(8,128)S(1)}, u32[]{:S(2)}, u32[]{:S(2)}) collective-permute-start(f32[576,128]{1,0:T(8,128)S(1)} %get-tuple-element.57), channel_id=1, source_target_pairs={{0,8},{1,9},{2,10},{3,11},{4,12},{5,13},{6,14},{7,15},{8,0},{9,1},... | collective-permute-start | bytes 884744 | tf_op jit(solution)/shard_map/ppermute | solution.py:418
  60.7 4.6 %collective-permute-start.17 = (f32[144,128]{1,0:T(8,128)S(1)}, f32[144,128]{1,0:T(8,128)S(1)}, u32[]{:S(2)}, u32[]{:S(2)}) collective-permute-start(f32[144,128]{1,0:T(8,128)S(1)} %get-tuple-element.59), channel_id=1, source_target_pairs={{0,16},{1,17},{2,18},{3,19},{4,20},{5,21},{6,22},{7,23},{8,24},{9,... | collective-permute-start | bytes 221192 | tf_op jit(solution)/shard_map/ppermute | solution.py:418
  61.4 5.0 %collective-permute-start.18 = (f32[144,128]{1,0:T(8,128)S(1)}, f32[144,128]{1,0:T(8,128)S(1)}, u32[]{:S(2)}, u32[]{:S(2)}) collective-permute-start(f32[144,128]{1,0:T(8,128)S(1)} %get-tuple-element.60), channel_id=1, source_target_pairs={{0,1},{1,0},{2,3},{3,2},{4,5},{5,4},{6,7},{7,6},{8,9},{9,8},{10,11... | collective-permute-start | bytes 221192 | tf_op jit(solution)/shard_map/ppermute | solution.py:418
  62.5 5.3 %collective-permute-start.19 = (f32[144,128]{1,0:T(8,128)S(1)}, f32[144,128]{1,0:T(8,128)S(1)}, u32[]{:S(2)}, u32[]{:S(2)}) collective-permute-start(f32[144,128]{1,0:T(8,128)S(1)} %get-tuple-element.61), channel_id=1, source_target_pairs={{0,17},{1,16},{2,19},{3,18},{4,21},{5,20},{6,23},{7,22},{8,25},{9,... | collective-permute-start | bytes 221192 | tf_op jit(solution)/shard_map/ppermute | solution.py:418
  67.7 4.5 %collective-permute-start.20 = (f32[144,128]{1,0:T(8,128)S(1)}, f32[144,128]{1,0:T(8,128)S(1)}, u32[]{:S(2)}, u32[]{:S(2)}) collective-permute-start(f32[144,128]{1,0:T(8,128)S(1)} %add_add_fusion.1), channel_id=1, source_target_pairs={{0,2},{1,3},{2,0},{3,1},{4,6},{5,7},{6,4},{7,5},{8,10},{9,11},{10,... | collective-permute-start | bytes 221192 | tf_op jit(solution)/shard_map/ppermute | solution.py:418
  68.2 6.8 %collective-permute-start.21 = (f32[144,128]{1,0:T(8,128)S(1)}, f32[144,128]{1,0:T(8,128)S(1)}, u32[]{:S(2)}, u32[]{:S(2)}) collective-permute-start(f32[144,128]{1,0:T(8,128)S(1)} %add_add_fusion.1), channel_id=1, source_target_pairs={{0,4},{1,5},{2,6},{3,7},{4,0},{5,1},{6,2},{7,3},{8,12},{9,13},{10,... | collective-permute-start | bytes 221192 | tf_op jit(solution)/shard_map/ppermute | solution.py:418
  69.8 6.3 %collective-permute-start.22 = (f32[144,128]{1,0:T(8,128)S(1)}, f32[144,128]{1,0:T(8,128)S(1)}, u32[]{:S(2)}, u32[]{:S(2)}) collective-permute-start(f32[144,128]{1,0:T(8,128)S(1)} %add_add_fusion.1), channel_id=1, source_target_pairs={{0,6},{1,7},{2,4},{3,5},{4,2},{5,3},{6,0},{7,1},{8,14},{9,15},{10,... | collective-permute-start | bytes 221192 | tf_op jit(solution)/shard_map/ppermute | solution.py:418
  76.1 4.4 %collective-permute-start.23 = (f32[144,128]{1,0:T(8,128)S(1)}, f32[144,128]{1,0:T(8,128)S(1)}, u32[]{:S(2)}, u32[]{:S(2)}) collective-permute-start(f32[144,128]{1,0:T(8,128)S(1)} %add_add_fusion), channel_id=1, source_target_pairs={{0,16},{1,17},{2,18},{3,19},{4,20},{5,21},{6,22},{7,23},{8,24},{9,... | collective-permute-start | bytes 221192 | tf_op jit(solution)/shard_map/ppermute | solution.py:418
  77.6 4.4 %collective-permute-start.24 = (f32[144,128]{1,0:T(8,128)S(1)}, f32[144,128]{1,0:T(8,128)S(1)}, u32[]{:S(2)}, u32[]{:S(2)}) collective-permute-start(f32[144,128]{1,0:T(8,128)S(1)} %add_add_fusion), channel_id=1, source_target_pairs={{0,1},{1,0},{2,3},{3,2},{4,5},{5,4},{6,7},{7,6},{8,9},{9,8},{10,11... | collective-permute-start | bytes 221192 | tf_op jit(solution)/shard_map/ppermute | solution.py:418
  78.4 5.3 %collective-permute-start.25 = (f32[144,128]{1,0:T(8,128)S(1)}, f32[144,128]{1,0:T(8,128)S(1)}, u32[]{:S(2)}, u32[]{:S(2)}) collective-permute-start(f32[144,128]{1,0:T(8,128)S(1)} %add_add_fusion), channel_id=1, source_target_pairs={{0,17},{1,16},{2,19},{3,18},{4,21},{5,20},{6,23},{7,22},{8,25},{9,... | collective-permute-start | bytes 221192 | tf_op jit(solution)/shard_map/ppermute | solution.py:418
  83.7 1.6 %collective-permute-start.26 = (f32[576,128]{1,0:T(8,128)S(1)}, f32[576,128]{1,0:T(8,128)S(1)}, u32[]{:S(2)}, u32[]{:S(2)}) collective-permute-start(f32[576,128]{1,0:T(8,128)S(1)} %pad_maximum_fusion.own_ref), channel_id=1, source_target_pairs={{0,8},{1,9},{2,10},{3,11},{4,12},{5,13},{6,14},{7,15},{8,0},{9,1},... | collective-permute-start | bytes 884744 | tf_op jit(solution)/shard_map/ppermute | solution.py:418

commit v7 on v5

--- a/solution.py
+++ b/solution.py
@@ -70,8 +70,12 @@
         large.append(pltpu.make_async_copy(blocks_hbm.at[pl.ds(begin, 2)], held.at[pl.ds(2 * pair, 2)], pair_sems.at[pair]))
     for copy in copies + large:
         copy.start()
-    hi_ref[...] = jnp.zeros_like(hi_ref)
-    lo_ref[...] = jnp.zeros_like(lo_ref)
+    for half in range(2):
+        always = {half + offset + REACH for offset in (-1, 1, REACH if half else -REACH)}
+        for slot in set(range(2 * REACH + 2)) - always:
+            empty = jnp.zeros((rows // 2, size, size), BF16)
+            hi_ref[:, slot * size : (slot + 1) * size, half * size : (half + 1) * size] = empty
+            lo_ref[:, slot * size : (slot + 1) * size, half * size : (half + 1) * size] = empty
     cross_ref[...] = jnp.zeros_like(cross_ref)
     first = lax.axis_index("narrow") * rows
     copies[0].wait()

time: 87.2 us -> 87.2 us (level)
  no operation moved by 1% of the time
where the time goes in v7:
time: 87.2 us; the launch traced here: 86.9 us
  starting transfers between devices  25.1 us (29%)
  waiting for transfers between devices  23.7 us (27%)
  Pallas kernels  18.7 us (21%)
  blocking collectives  17.6 us (20%)
  between operations  1.65 us (2%)
    all_to_all x1, blocking collectives, regroup(): lax.all_to_all(parts, 'wide', split_axis=0, concat_axis=0, tiled=True)  17.6 us
    ppermute x11, waiting for transfers between devices, swap(): return lax.ppermute(x, ('narrow', 'wide'), pair_perm(mask))  14.2 us
    pallas_call x23, Pallas kernels, step_call(): pl.pallas_call(kernel, in_specs=[VM] * (len(operands) + 2), out_specs=[VM...  12.6 us
    ppermute x11, starting transfers between devices, swap(): return lax.ppermute(x, ('narrow', 'wide'), pair_perm(mask))  11.7 us
    ppermute x6, waiting for transfers between devices, far_swap(): lax.ppermute(x, 'narrow', [(i, (i + 1) % size if i % 2 else (i - 1) % siz...  6.89 us
    ppermute x6, starting transfers between devices, far_swap(): lax.ppermute(x, 'narrow', [(i, (i + 1) % size if i % 2 else (i - 1) % siz...  6.39 us
    ppermute x8, starting transfers between devices, near_swap(): lax.ppermute(x, 'narrow', [(i, i ^ 1) for i in range(lax.axis_size('narro...  3.85 us
    pallas_call x1, Pallas kernels, spread_part(): pl.pallas_call(functools.partial(spread_kernel, total_blocks), in_specs=[...  3.51 us
  transfers between devices with their start and end apart: 27, of which 17 were waited for; matrix products, arithmetic and copies ran while one was open for 0% of the time, Pallas kernels for 14%

profile of v7, /device:TPU:0, one launch (start us, length us, event | category | flops | bytes accessed | tf_op | source)
XLA Modules:
  0.0 86.9 jit_solution(2557751878021332229)
XLA Ops:
  0.0 3.5 %spread_part.1 = (f32[64,384]{1,0:T(8,128)S(1)}, f32[64,384]{1,0:T(8,128)S(1)}, f32[64,1536]{1,0:T(8,128)S(1)}, f32[192,128]{1,0:T(8,128)S(1)}, bf16[6,1024,256]...) custom-call(s32[5,12]{1,0:T(8,128)} %bitcast.3, f32[64,1536]{1,0:T(8,128)} %vectors_hbm.1, f32[12,5,128,128]{3,2,1,0:T(8,128)} %blocks_hbm.1), custom_call_target="tpu_custom_call" | custom-call | tf_op jit(solution)/shard_map/spread_part/pallas_call | solution.py:120
  3.5 0.5 collective-permute-start.1
  4.0 2.6 %collective-permute-start = (f32[64,384]{1,0:T(8,128)S(1)}, f32[64,384]{1,0:T(8,128)S(1)}, u32[]{:S(2)}, u32[]{:S(2)}) collective-permute-start(f32[64,384]{1,0:T(8,128)S(1)} %get-tuple-element.37.far_before_ref), channel_id=1, source_target_pairs={{0,24},{8,16},{16,8},{24,0},{1,25},{9,17},{17,9},{25,1},{2,26},{10... | collective-permute-start | bytes 294920 | tf_op jit(solution)/shard_map/ppermute | solution.py:354
  8.1 0.9 %first_part.1.mid_ref.mid_before_ref = f32[64,1536]{1,0:T(8,128)S(1)} custom-call(f32[2,256]{1,0:T(2,128)S(1)} %concatenate.12.terms_ref, f32[64,1536]{1,0:T(8,128)S(1)} %get-tuple-element.34.vectors_ref.mid_before_ref, bf16[6,1024,256]{2,1,0:T(8,128)(2,1)S(1)} %get-tuple-element.35.hi_ref.refs_2_.refs_1_, ...), custom_call_target="tpu_custom_call" | custom-call | flops 603979776 | bytes 786432 | tf_op jit(solution)/shard_map/first_part/pallas_call | solution.py:219
  10.0 2.3 %collective-permute-start.2 = (f32[64,384]{1,0:T(8,128)S(1)}, f32[64,384]{1,0:T(8,128)S(1)}, u32[]{:S(2)}, u32[]{:S(2)}) collective-permute-start(f32[64,384]{1,0:T(8,128)S(1)} %far_part.1.far_ref.before_ref.far_before_ref), channel_id=1, source_target_pairs={{0,24},{8,16},{16,8},{24,0},{1,25},{9,17},{17,9},{25,1},{2,26},{10... | collective-permute-start | bytes 294920 | tf_op jit(solution)/shard_map/ppermute | solution.py:354
  12.3 1.5 %collective-permute-start.7 = (f32[192,128]{1,0:T(8,128)S(1)}, f32[192,128]{1,0:T(8,128)S(1)}, u32[]{:S(2)}, u32[]{:S(2)}) collective-permute-start(f32[192,128]{1,0:T(8,128)S(1)} %collective-permute-done.6.mine_ref), channel_id=1, source_target_pairs={{0,1},{1,0},{2,3},{3,2},{4,5},{5,4},{6,7},{7,6},{8,9},{9,8},{10,11... | collective-permute-start | bytes 294920 | tf_op jit(solution)/shard_map/ppermute | solution.py:358
  13.8 1.0 %local_part.4.mid_ref = f32[64,1536]{1,0:T(8,128)S(1)} custom-call(f32[2,256]{1,0:T(2,128)S(1)} %concatenate.12.terms_ref, f32[64,384]{1,0:T(8,128)S(1)} %far_part.1.far_ref.before_ref.far_before_ref, f32[64,1536]{1,0:T(8,128)S(1)} %first_part.1.mid_ref.mid_before_ref, f32[64,384]{1,0:T(8,128)S(1)} %near_part.8.near_ref.near_before_ref, ...), custom_call_target="tpu_custom_call" | custom-call | flops 150994944 | bytes 196608 | tf_op jit(solution)/shard_map/local_part/pallas_call | solution.py:219
  15.3 0.6 turn_one.1
  15.9 1.3 %collective-permute-start.5 = (f32[2,64,384]{2,1,0:T(8,128)S(1)}, f32[2,64,384]{2,1,0:T(8,128)S(1)}, u32[]{:S(2)}, u32[]{:S(2)}) collective-permute-start(f32[2,64,384]{2,1,0:T(8,128)S(1)} %get-tuple-element.42.sent_ref), channel_id=1, source_target_pairs={{0,24},{8,16},{16,8},{24,0},{1,25},{9,17},{17,9},{25,1},{2,26},{10... | collective-permute-start | bytes 589832 | tf_op jit(solution)/shard_map/ppermute | solution.py:354
  17.3 1.6 %collective-permute-start.8 = (f32[384,128]{1,0:T(8,128)S(1)}, f32[384,128]{1,0:T(8,128)S(1)}, u32[]{:S(2)}, u32[]{:S(2)}) collective-permute-start(f32[384,128]{1,0:T(8,128)S(1)} %pad_maximum_fusion.1), channel_id=1, source_target_pairs={{0,2},{1,3},{2,0},{3,1},{4,6},{5,7},{6,4},{7,5},{8,10},{9,11},{10,... | collective-permute-start | bytes 589832 | tf_op jit(solution)/shard_map/ppermute | solution.py:358
  18.9 0.8 local_part.5
  20.1 0.8 second_part.3.mid_ref
  20.9 0.5 collective-permute-done.9.halo_ref
  21.8 2.0 %collective-permute-done.8.two_ref = f32[384,128]{1,0:T(8,128)S(1)} collective-permute-done((f32[384,128]{1,0:T(8,128)S(1)}, f32[384,128]{1,0:T(8,128)S(1)}, u32[]{:S(2)}, u32[]{:S(2)}) %collective-permute-start.8) | collective-permute-done | bytes 196640 | tf_op jit(solution)/shard_map/ppermute | solution.py:358
  23.9 1.0 %turn_two.2 = (f32[64,384]{1,0:T(8,128)S(1)}, f32[64,768]{1,0:T(8,128)S(1)}, f32[2,64,384]{2,1,0:T(8,128)S(1)}) custom-call(f32[2,256]{1,0:T(2,128)S(1)} %concatenate.12.terms_ref, f32[64,1536]{1,0:T(8,128)S(1)} %second_part.3.mid_ref, f32[2,64,384]{2,1,0:T(8,128)S(1)} %get-tuple-element.42.sent_ref, f32[2,64,384]{2,1,0:T(8,128)S(1)} %collective-permute-done.5.got_ref, ...), custom_call_target="tpu_custom_call" | custom-call | flops 603979776 | bytes 786432 | tf_op jit(solution)/shard_map/turn_two/pallas_call | solution.py:219
  25.0 0.8 local_part.6
  26.0 1.4 %collective-permute-start.12 = (f32[64,384]{1,0:T(8,128)S(1)}, f32[64,384]{1,0:T(8,128)S(1)}, u32[]{:S(2)}, u32[]{:S(2)}) collective-permute-start(f32[64,384]{1,0:T(8,128)S(1)} %near_part.12.near_ref.near_before_ref), channel_id=1, source_target_pairs={{0,8},{8,0},{16,24},{24,16},{1,9},{9,1},{17,25},{25,17},{2,10},{10... | collective-permute-start | bytes 294920 | tf_op jit(solution)/shard_map/ppermute | solution.py:362
  27.4 0.8 second_part.4.mid_ref
  28.6 0.4 collective-permute-start.13
  29.3 2.6 %collective-permute-done.11.got_ref = f32[2,64,384]{2,1,0:T(8,128)S(1)} collective-permute-done((f32[2,64,384]{2,1,0:T(8,128)S(1)}, f32[2,64,384]{2,1,0:T(8,128)S(1)}, u32[]{:S(2)}, u32[]{:S(2)}) %collective-permute-start.11) | collective-permute-done | bytes 196640 | tf_op jit(solution)/shard_map/ppermute | solution.py:354
  31.9 0.9 %turn_two.3 = (f32[64,384]{1,0:T(8,128)S(1)}, f32[64,768]{1,0:T(8,128)S(1)}, f32[2,64,384]{2,1,0:T(8,128)S(1)}) custom-call(f32[2,256]{1,0:T(2,128)S(1)} %concatenate.12.terms_ref, f32[64,1536]{1,0:T(8,128)S(1)} %second_part.4.mid_ref, f32[2,64,384]{2,1,0:T(8,128)S(1)} %get-tuple-element.50.sent_ref, f32[2,64,384]{2,1,0:T(8,128)S(1)} %collective-permute-done.11.got_ref, ...), custom_call_target="tpu_custom_call" | custom-call | flops 603979776 | bytes 786432 | tf_op jit(solution)/shard_map/turn_two/pallas_call | solution.py:219
  32.9 0.8 local_part.7
  34.0 1.0 %collective-permute-start.15 = (f32[64,384]{1,0:T(8,128)S(1)}, f32[64,384]{1,0:T(8,128)S(1)}, u32[]{:S(2)}, u32[]{:S(2)}) collective-permute-start(f32[64,384]{1,0:T(8,128)S(1)} %near_part.14.near_ref), channel_id=1, source_target_pairs={{0,8},{8,0},{16,24},{24,16},{1,9},{9,1},{17,25},{25,17},{2,10},{10... | collective-permute-start | bytes 294920 | tf_op jit(solution)/shard_map/ppermute | solution.py:362
  35.2 0.8 second_part.5.mid_ref
  36.3 3.7 %collective-permute-done.14.got_ref = f32[2,64,384]{2,1,0:T(8,128)S(1)} collective-permute-done((f32[2,64,384]{2,1,0:T(8,128)S(1)}, f32[2,64,384]{2,1,0:T(8,128)S(1)}, u32[]{:S(2)}, u32[]{:S(2)}) %collective-permute-start.14) | collective-permute-done | bytes 196640 | tf_op jit(solution)/shard_map/ppermute | solution.py:354
  40.0 0.7 last_part.1
  40.7 17.6 %all_to_all.5.parts_ref = f32[8,96,128]{2,1,0:T(8,128)S(1)} all-to-all(f32[8,96,128]{2,1,0:T(8,128)S(1)} %last_part.1), channel_id=1, replica_groups=mesh['narrow'=4,'wide'=8] {'wide'}, dimensions={0} | all-to-all | bytes 786432 | tf_op jit(solution)/shard_map/all_to_all | solution.py:680
  58.3 0.7 gram.1
  59.1 1.6 %collective-permute-done.16.refs_1_ = f32[576,128]{1,0:T(8,128)S(1)} collective-permute-done((f32[576,128]{1,0:T(8,128)S(1)}, f32[576,128]{1,0:T(8,128)S(1)}, u32[]{:S(2)}, u32[]{:S(2)}) %collective-permute-start.16) | collective-permute-done | bytes 294944 | tf_op jit(solution)/shard_map/ppermute | solution.py:422
  60.7 0.7 collective-permute-start.17
  61.4 1.1 %collective-permute-start.18 = (f32[144,128]{1,0:T(8,128)S(1)}, f32[144,128]{1,0:T(8,128)S(1)}, u32[]{:S(2)}, u32[]{:S(2)}) collective-permute-start(f32[144,128]{1,0:T(8,128)S(1)} %get-tuple-element.60), channel_id=1, source_target_pairs={{0,1},{1,0},{2,3},{3,2},{4,5},{5,4},{6,7},{7,6},{8,9},{9,8},{10,11... | collective-permute-start | bytes 221192 | tf_op jit(solution)/shard_map/ppermute | solution.py:422
  62.5 1.8 %collective-permute-start.19 = (f32[144,128]{1,0:T(8,128)S(1)}, f32[144,128]{1,0:T(8,128)S(1)}, u32[]{:S(2)}, u32[]{:S(2)}) collective-permute-start(f32[144,128]{1,0:T(8,128)S(1)} %get-tuple-element.61), channel_id=1, source_target_pairs={{0,17},{1,16},{2,19},{3,18},{4,21},{5,20},{6,23},{7,22},{8,25},{9,... | collective-permute-start | bytes 221192 | tf_op jit(solution)/shard_map/ppermute | solution.py:422
  64.3 1.0 %collective-permute-done.17 = f32[144,128]{1,0:T(8,128)S(1)} collective-permute-done((f32[144,128]{1,0:T(8,128)S(1)}, f32[144,128]{1,0:T(8,128)S(1)}, u32[]{:S(2)}, u32[]{:S(2)}) %collective-permute-start.17) | collective-permute-done | bytes 73760 | tf_op jit(solution)/shard_map/ppermute | solution.py:422
  65.3 1.2 %collective-permute-done.18 = f32[144,128]{1,0:T(8,128)S(1)} collective-permute-done((f32[144,128]{1,0:T(8,128)S(1)}, f32[144,128]{1,0:T(8,128)S(1)}, u32[]{:S(2)}, u32[]{:S(2)}) %collective-permute-start.18) | collective-permute-done | bytes 73760 | tf_op jit(solution)/shard_map/ppermute | solution.py:422
  66.5 1.2 %collective-permute-done.19 = f32[144,128]{1,0:T(8,128)S(1)} collective-permute-done((f32[144,128]{1,0:T(8,128)S(1)}, f32[144,128]{1,0:T(8,128)S(1)}, u32[]{:S(2)}, u32[]{:S(2)}) %collective-permute-start.19) | collective-permute-done | bytes 73760 | tf_op jit(solution)/shard_map/ppermute | solution.py:422
  67.7 0.5 collective-permute-start.20
  68.2 1.6 %collective-permute-start.21 = (f32[144,128]{1,0:T(8,128)S(1)}, f32[144,128]{1,0:T(8,128)S(1)}, u32[]{:S(2)}, u32[]{:S(2)}) collective-permute-start(f32[144,128]{1,0:T(8,128)S(1)} %add_add_fusion.1), channel_id=1, source_target_pairs={{0,4},{1,5},{2,6},{3,7},{4,0},{5,1},{6,2},{7,3},{8,12},{9,13},{10,... | collective-permute-start | bytes 221192 | tf_op jit(solution)/shard_map/ppermute | solution.py:422
  69.8 2.4 %collective-permute-start.22 = (f32[144,128]{1,0:T(8,128)S(1)}, f32[144,128]{1,0:T(8,128)S(1)}, u32[]{:S(2)}, u32[]{:S(2)}) collective-permute-start(f32[144,128]{1,0:T(8,128)S(1)} %add_add_fusion.1), channel_id=1, source_target_pairs={{0,6},{1,7},{2,4},{3,5},{4,2},{5,3},{6,0},{7,1},{8,14},{9,15},{10,... | collective-permute-start | bytes 221192 | tf_op jit(solution)/shard_map/ppermute | solution.py:422
  72.2 2.8 %collective-permute-done.21 = f32[144,128]{1,0:T(8,128)S(1)} collective-permute-done((f32[144,128]{1,0:T(8,128)S(1)}, f32[144,128]{1,0:T(8,128)S(1)}, u32[]{:S(2)}, u32[]{:S(2)}) %collective-permute-start.21) | collective-permute-done | bytes 73760 | tf_op jit(solution)/shard_map/ppermute | solution.py:422
  75.0 1.1 %collective-permute-done.22 = f32[144,128]{1,0:T(8,128)S(1)} collective-permute-done((f32[144,128]{1,0:T(8,128)S(1)}, f32[144,128]{1,0:T(8,128)S(1)}, u32[]{:S(2)}, u32[]{:S(2)}) %collective-permute-start.22) | collective-permute-done | bytes 73760 | tf_op jit(solution)/shard_map/ppermute | solution.py:422
  76.1 1.5 %collective-permute-start.23 = (f32[144,128]{1,0:T(8,128)S(1)}, f32[144,128]{1,0:T(8,128)S(1)}, u32[]{:S(2)}, u32[]{:S(2)}) collective-permute-start(f32[144,128]{1,0:T(8,128)S(1)} %add_add_fusion), channel_id=1, source_target_pairs={{0,16},{1,17},{2,18},{3,19},{4,20},{5,21},{6,22},{7,23},{8,24},{9,... | collective-permute-start | bytes 221192 | tf_op jit(solution)/shard_map/ppermute | solution.py:422
  77.6 0.8 collective-permute-start.24
  78.4 1.3 %collective-permute-start.25 = (f32[144,128]{1,0:T(8,128)S(1)}, f32[144,128]{1,0:T(8,128)S(1)}, u32[]{:S(2)}, u32[]{:S(2)}) collective-permute-start(f32[144,128]{1,0:T(8,128)S(1)} %add_add_fusion), channel_id=1, source_target_pairs={{0,17},{1,16},{2,19},{3,18},{4,21},{5,20},{6,23},{7,22},{8,25},{9,... | collective-permute-start | bytes 221192 | tf_op jit(solution)/shard_map/ppermute | solution.py:422
  79.7 0.9 collective-permute-done.23
  80.5 1.4 %collective-permute-done.24 = f32[144,128]{1,0:T(8,128)S(1)} collective-permute-done((f32[144,128]{1,0:T(8,128)S(1)}, f32[144,128]{1,0:T(8,128)S(1)}, u32[]{:S(2)}, u32[]{:S(2)}) %collective-permute-start.24) | collective-permute-done | bytes 73760 | tf_op jit(solution)/shard_map/ppermute | solution.py:422
  82.0 1.7 %collective-permute-done.25 = f32[144,128]{1,0:T(8,128)S(1)} collective-permute-done((f32[144,128]{1,0:T(8,128)S(1)}, f32[144,128]{1,0:T(8,128)S(1)}, u32[]{:S(2)}, u32[]{:S(2)}) %collective-permute-start.25) | collective-permute-done | bytes 73760 | tf_op jit(solution)/shard_map/ppermute | solution.py:422
  83.9 1.4 %collective-permute-done.26.other_ref = f32[576,128]{1,0:T(8,128)S(1)} collective-permute-done((f32[576,128]{1,0:T(8,128)S(1)}, f32[576,128]{1,0:T(8,128)S(1)}, u32[]{:S(2)}, u32[]{:S(2)}) %collective-permute-start.26) | collective-permute-done | bytes 294944 | tf_op jit(solution)/shard_map/ppermute | solution.py:422
  85.3 1.6 %rotate.1 = f32[192,512]{1,0:T(8,128)} custom-call(f32[576,128]{1,0:T(8,128)S(1)} %pad_maximum_fusion.own_ref, f32[576,128]{1,0:T(8,128)S(1)} %collective-permute-done.26.other_ref, f32[192,512]{1,0:T(8,128)S(1)} %turned.1.rows_ref), custom_call_target="tpu_custom_call" | custom-call | tf_op jit(solution)/shard_map/rotate/pallas_call | solution.py:660
  (42 shorter events, 4.5 us)
Async XLA Ops:
  3.5 5.5 %collective-permute-start.1 = (f32[64,384]{1,0:T(8,128)S(1)}, f32[64,384]{1,0:T(8,128)S(1)}, u32[]{:S(2)}, u32[]{:S(2)}) collective-permute-start(f32[64,384]{1,0:T(8,128)S(1)} %get-tuple-element.38.near_before_ref), channel_id=1, source_target_pairs={{0,8},{8,0},{16,24},{24,16},{1,9},{9,1},{17,25},{25,17},{2,10},{10... | collective-permute-start | bytes 294920 | tf_op jit(solution)/shard_map/ppermute | solution.py:362
  4.0 5.7 %collective-permute-start = (f32[64,384]{1,0:T(8,128)S(1)}, f32[64,384]{1,0:T(8,128)S(1)}, u32[]{:S(2)}, u32[]{:S(2)}) collective-permute-start(f32[64,384]{1,0:T(8,128)S(1)} %get-tuple-element.37.far_before_ref), channel_id=1, source_target_pairs={{0,24},{8,16},{16,8},{24,0},{1,25},{9,17},{17,9},{25,1},{2,26},{10... | collective-permute-start | bytes 294920 | tf_op jit(solution)/shard_map/ppermute | solution.py:354
  6.7 5.6 %collective-permute-start.6 = (f32[192,128]{1,0:T(8,128)S(1)}, f32[192,128]{1,0:T(8,128)S(1)}, u32[]{:S(2)}, u32[]{:S(2)}) collective-permute-start(f32[192,128]{1,0:T(8,128)S(1)} %get-tuple-element.43), channel_id=1, source_target_pairs={{0,24},{8,16},{16,8},{24,0},{1,25},{9,17},{17,9},{25,1},{2,26},{10... | collective-permute-start | bytes 294920 | tf_op jit(solution)/shard_map/ppermute | solution.py:354
  9.3 5.5 %collective-permute-start.3 = (f32[64,384]{1,0:T(8,128)S(1)}, f32[64,384]{1,0:T(8,128)S(1)}, u32[]{:S(2)}, u32[]{:S(2)}) collective-permute-start(f32[64,384]{1,0:T(8,128)S(1)} %near_part.8.near_ref.near_before_ref), channel_id=1, source_target_pairs={{0,8},{8,0},{16,24},{24,16},{1,9},{9,1},{17,25},{25,17},{2,10},{10... | collective-permute-start | bytes 294920 | tf_op jit(solution)/shard_map/ppermute | solution.py:362
  10.0 5.3 %collective-permute-start.2 = (f32[64,384]{1,0:T(8,128)S(1)}, f32[64,384]{1,0:T(8,128)S(1)}, u32[]{:S(2)}, u32[]{:S(2)}) collective-permute-start(f32[64,384]{1,0:T(8,128)S(1)} %far_part.1.far_ref.before_ref.far_before_ref), channel_id=1, source_target_pairs={{0,24},{8,16},{16,8},{24,0},{1,25},{9,17},{17,9},{25,1},{2,26},{10... | collective-permute-start | bytes 294920 | tf_op jit(solution)/shard_map/ppermute | solution.py:354
  12.3 5.0 %collective-permute-start.7 = (f32[192,128]{1,0:T(8,128)S(1)}, f32[192,128]{1,0:T(8,128)S(1)}, u32[]{:S(2)}, u32[]{:S(2)}) collective-permute-start(f32[192,128]{1,0:T(8,128)S(1)} %collective-permute-done.6.mine_ref), channel_id=1, source_target_pairs={{0,1},{1,0},{2,3},{3,2},{4,5},{5,4},{6,7},{7,6},{8,9},{9,8},{10,11... | collective-permute-start | bytes 294920 | tf_op jit(solution)/shard_map/ppermute | solution.py:358
  15.0 4.8 %collective-permute-start.4 = (f32[64,384]{1,0:T(8,128)S(1)}, f32[64,384]{1,0:T(8,128)S(1)}, u32[]{:S(2)}, u32[]{:S(2)}) collective-permute-start(f32[64,384]{1,0:T(8,128)S(1)} %near_part.9.near_ref), channel_id=1, source_target_pairs={{0,8},{8,0},{16,24},{24,16},{1,9},{9,1},{17,25},{25,17},{2,10},{10... | collective-permute-start | bytes 294920 | tf_op jit(solution)/shard_map/ppermute | solution.py:362
  15.9 7.9 %collective-permute-start.5 = (f32[2,64,384]{2,1,0:T(8,128)S(1)}, f32[2,64,384]{2,1,0:T(8,128)S(1)}, u32[]{:S(2)}, u32[]{:S(2)}) collective-permute-start(f32[2,64,384]{2,1,0:T(8,128)S(1)} %get-tuple-element.42.sent_ref), channel_id=1, source_target_pairs={{0,24},{8,16},{16,8},{24,0},{1,25},{9,17},{17,9},{25,1},{2,26},{10... | collective-permute-start | bytes 589832 | tf_op jit(solution)/shard_map/ppermute | solution.py:354
  17.3 6.5 %collective-permute-start.8 = (f32[384,128]{1,0:T(8,128)S(1)}, f32[384,128]{1,0:T(8,128)S(1)}, u32[]{:S(2)}, u32[]{:S(2)}) collective-permute-start(f32[384,128]{1,0:T(8,128)S(1)} %pad_maximum_fusion.1), channel_id=1, source_target_pairs={{0,2},{1,3},{2,0},{3,1},{4,6},{5,7},{6,4},{7,5},{8,10},{9,11},{10,... | collective-permute-start | bytes 589832 | tf_op jit(solution)/shard_map/ppermute | solution.py:358
  20.0 1.4 %collective-permute-start.9 = (f32[64,384]{1,0:T(8,128)S(1)}, f32[64,384]{1,0:T(8,128)S(1)}, u32[]{:S(2)}, u32[]{:S(2)}) collective-permute-start(f32[64,384]{1,0:T(8,128)S(1)} %near_part.10.near_ref.near_before_ref), channel_id=1, source_target_pairs={{0,8},{8,0},{16,24},{24,16},{1,9},{9,1},{17,25},{25,17},{2,10},{10... | collective-permute-start | bytes 294920 | tf_op jit(solution)/shard_map/ppermute | solution.py:362
  21.6 4.2 %collective-permute-start.10 = (f32[64,384]{1,0:T(8,128)S(1)}, f32[64,384]{1,0:T(8,128)S(1)}, u32[]{:S(2)}, u32[]{:S(2)}) collective-permute-start(f32[64,384]{1,0:T(8,128)S(1)} %near_part.11.near_ref), channel_id=1, source_target_pairs={{0,8},{8,0},{16,24},{24,16},{1,9},{9,1},{17,25},{25,17},{2,10},{10... | collective-permute-start | bytes 294920 | tf_op jit(solution)/shard_map/ppermute | solution.py:362
  24.9 7.0 %collective-permute-start.11 = (f32[2,64,384]{2,1,0:T(8,128)S(1)}, f32[2,64,384]{2,1,0:T(8,128)S(1)}, u32[]{:S(2)}, u32[]{:S(2)}) collective-permute-start(f32[2,64,384]{2,1,0:T(8,128)S(1)} %get-tuple-element.50.sent_ref), channel_id=1, source_target_pairs={{0,24},{8,16},{16,8},{24,0},{1,25},{9,17},{17,9},{25,1},{2,26},{10... | collective-permute-start | bytes 589832 | tf_op jit(solution)/shard_map/ppermute | solution.py:354
  26.0 2.3 %collective-permute-start.12 = (f32[64,384]{1,0:T(8,128)S(1)}, f32[64,384]{1,0:T(8,128)S(1)}, u32[]{:S(2)}, u32[]{:S(2)}) collective-permute-start(f32[64,384]{1,0:T(8,128)S(1)} %near_part.12.near_ref.near_before_ref), channel_id=1, source_target_pairs={{0,8},{8,0},{16,24},{24,16},{1,9},{9,1},{17,25},{25,17},{2,10},{10... | collective-permute-start | bytes 294920 | tf_op jit(solution)/shard_map/ppermute | solution.py:362
  28.6 5.1 %collective-permute-start.13 = (f32[64,384]{1,0:T(8,128)S(1)}, f32[64,384]{1,0:T(8,128)S(1)}, u32[]{:S(2)}, u32[]{:S(2)}) collective-permute-start(f32[64,384]{1,0:T(8,128)S(1)} %near_part.13.near_ref), channel_id=1, source_target_pairs={{0,8},{8,0},{16,24},{24,16},{1,9},{9,1},{17,25},{25,17},{2,10},{10... | collective-permute-start | bytes 294920 | tf_op jit(solution)/shard_map/ppermute | solution.py:362
  32.8 7.2 %collective-permute-start.14 = (f32[2,64,384]{2,1,0:T(8,128)S(1)}, f32[2,64,384]{2,1,0:T(8,128)S(1)}, u32[]{:S(2)}, u32[]{:S(2)}) collective-permute-start(f32[2,64,384]{2,1,0:T(8,128)S(1)} %get-tuple-element.55.sent_ref), channel_id=1, source_target_pairs={{0,24},{8,16},{16,8},{24,0},{1,25},{9,17},{17,9},{25,1},{2,26},{10... | collective-permute-start | bytes 589832 | tf_op jit(solution)/shard_map/ppermute | solution.py:354
  34.0 2.1 %collective-permute-start.15 = (f32[64,384]{1,0:T(8,128)S(1)}, f32[64,384]{1,0:T(8,128)S(1)}, u32[]{:S(2)}, u32[]{:S(2)}) collective-permute-start(f32[64,384]{1,0:T(8,128)S(1)} %near_part.14.near_ref), channel_id=1, source_target_pairs={{0,8},{8,0},{16,24},{24,16},{1,9},{9,1},{17,25},{25,17},{2,10},{10... | collective-permute-start | bytes 294920 | tf_op jit(solution)/shard_map/ppermute | solution.py:362
  59.0 1.6 %collective-permute-start.16 = (f32[576,128]{1,0:T(8,128)S(1)}, f32[576,128]{1,0:T(8,128)S(1)}, u32[]{:S(2)}, u32[]{:S(2)}) collective-permute-start(f32[576,128]{1,0:T(8,128)S(1)} %get-tuple-element.57), channel_id=1, source_target_pairs={{0,8},{1,9},{2,10},{3,11},{4,12},{5,13},{6,14},{7,15},{8,0},{9,1},... | collective-permute-start | bytes 884744 | tf_op jit(solution)/shard_map/ppermute | solution.py:422
  60.7 4.6 %collective-permute-start.17 = (f32[144,128]{1,0:T(8,128)S(1)}, f32[144,128]{1,0:T(8,128)S(1)}, u32[]{:S(2)}, u32[]{:S(2)}) collective-permute-start(f32[144,128]{1,0:T(8,128)S(1)} %get-tuple-element.59), channel_id=1, source_target_pairs={{0,16},{1,17},{2,18},{3,19},{4,20},{5,21},{6,22},{7,23},{8,24},{9,... | collective-permute-start | bytes 221192 | tf_op jit(solution)/shard_map/ppermute | solution.py:422
  61.4 5.1 %collective-permute-start.18 = (f32[144,128]{1,0:T(8,128)S(1)}, f32[144,128]{1,0:T(8,128)S(1)}, u32[]{:S(2)}, u32[]{:S(2)}) collective-permute-start(f32[144,128]{1,0:T(8,128)S(1)} %get-tuple-element.60), channel_id=1, source_target_pairs={{0,1},{1,0},{2,3},{3,2},{4,5},{5,4},{6,7},{7,6},{8,9},{9,8},{10,11... | collective-permute-start | bytes 221192 | tf_op jit(solution)/shard_map/ppermute | solution.py:422
  62.5 5.3 %collective-permute-start.19 = (f32[144,128]{1,0:T(8,128)S(1)}, f32[144,128]{1,0:T(8,128)S(1)}, u32[]{:S(2)}, u32[]{:S(2)}) collective-permute-start(f32[144,128]{1,0:T(8,128)S(1)} %get-tuple-element.61), channel_id=1, source_target_pairs={{0,17},{1,16},{2,19},{3,18},{4,21},{5,20},{6,23},{7,22},{8,25},{9,... | collective-permute-start | bytes 221192 | tf_op jit(solution)/shard_map/ppermute | solution.py:422
  67.7 4.5 %collective-permute-start.20 = (f32[144,128]{1,0:T(8,128)S(1)}, f32[144,128]{1,0:T(8,128)S(1)}, u32[]{:S(2)}, u32[]{:S(2)}) collective-permute-start(f32[144,128]{1,0:T(8,128)S(1)} %add_add_fusion.1), channel_id=1, source_target_pairs={{0,2},{1,3},{2,0},{3,1},{4,6},{5,7},{6,4},{7,5},{8,10},{9,11},{10,... | collective-permute-start | bytes 221192 | tf_op jit(solution)/shard_map/ppermute | solution.py:422
  68.2 6.7 %collective-permute-start.21 = (f32[144,128]{1,0:T(8,128)S(1)}, f32[144,128]{1,0:T(8,128)S(1)}, u32[]{:S(2)}, u32[]{:S(2)}) collective-permute-start(f32[144,128]{1,0:T(8,128)S(1)} %add_add_fusion.1), channel_id=1, source_target_pairs={{0,4},{1,5},{2,6},{3,7},{4,0},{5,1},{6,2},{7,3},{8,12},{9,13},{10,... | collective-permute-start | bytes 221192 | tf_op jit(solution)/shard_map/ppermute | solution.py:422
  69.8 6.3 %collective-permute-start.22 = (f32[144,128]{1,0:T(8,128)S(1)}, f32[144,128]{1,0:T(8,128)S(1)}, u32[]{:S(2)}, u32[]{:S(2)}) collective-permute-start(f32[144,128]{1,0:T(8,128)S(1)} %add_add_fusion.1), channel_id=1, source_target_pairs={{0,6},{1,7},{2,4},{3,5},{4,2},{5,3},{6,0},{7,1},{8,14},{9,15},{10,... | collective-permute-start | bytes 221192 | tf_op jit(solution)/shard_map/ppermute | solution.py:422
  76.1 4.4 %collective-permute-start.23 = (f32[144,128]{1,0:T(8,128)S(1)}, f32[144,128]{1,0:T(8,128)S(1)}, u32[]{:S(2)}, u32[]{:S(2)}) collective-permute-start(f32[144,128]{1,0:T(8,128)S(1)} %add_add_fusion), channel_id=1, source_target_pairs={{0,16},{1,17},{2,18},{3,19},{4,20},{5,21},{6,22},{7,23},{8,24},{9,... | collective-permute-start | bytes 221192 | tf_op jit(solution)/shard_map/ppermute | solution.py:422
  77.6 4.4 %collective-permute-start.24 = (f32[144,128]{1,0:T(8,128)S(1)}, f32[144,128]{1,0:T(8,128)S(1)}, u32[]{:S(2)}, u32[]{:S(2)}) collective-permute-start(f32[144,128]{1,0:T(8,128)S(1)} %add_add_fusion), channel_id=1, source_target_pairs={{0,1},{1,0},{2,3},{3,2},{4,5},{5,4},{6,7},{7,6},{8,9},{9,8},{10,11... | collective-permute-start | bytes 221192 | tf_op jit(solution)/shard_map/ppermute | solution.py:422
  78.4 5.3 %collective-permute-start.25 = (f32[144,128]{1,0:T(8,128)S(1)}, f32[144,128]{1,0:T(8,128)S(1)}, u32[]{:S(2)}, u32[]{:S(2)}) collective-permute-start(f32[144,128]{1,0:T(8,128)S(1)} %add_add_fusion), channel_id=1, source_target_pairs={{0,17},{1,16},{2,19},{3,18},{4,21},{5,20},{6,23},{7,22},{8,25},{9,... | collective-permute-start | bytes 221192 | tf_op jit(solution)/shard_map/ppermute | solution.py:422
  83.7 1.6 %collective-permute-start.26 = (f32[576,128]{1,0:T(8,128)S(1)}, f32[576,128]{1,0:T(8,128)S(1)}, u32[]{:S(2)}, u32[]{:S(2)}) collective-permute-start(f32[576,128]{1,0:T(8,128)S(1)} %pad_maximum_fusion.own_ref), channel_id=1, source_target_pairs={{0,8},{1,9},{2,10},{3,11},{4,12},{5,13},{6,14},{7,15},{8,0},{9,1},... | collective-permute-start | bytes 884744 | tf_op jit(solution)/shard_map/ppermute | solution.py:422
